TPU v7x, 32 devices: a whole 2x2x4 slice. The times are simulated.
32 devices in a mesh: tiles: 8 (over y, x, core), slab: 4 (over z).
Axes of the slice: x: 2, y: 2, z: 4, core: 2. Of those that a mesh axis runs over, the one named last changes fastest.
Arguments:
- adjoint: float32 [4, 3, 32, 8100], P('slab', None, 'tiles'), may hold values from -6 to 6
- state: float32 [4, 3, 32, 8100], P('slab', None, 'tiles'), may hold values from 0.1 to 10
- weights: float32 [4, 32, 8100], P('slab', 'tiles'), may hold values from 0.02 to 0.24
- vertical: float32 [4, 32, 8100], P('slab', 'tiles'), may hold values from 0.02 to 0.3
- mask: int32 [4, 32, 8100], P('slab', 'tiles'), may hold values 0 or 1
- rate: float32 [3, 32, 8100], P(None, 'tiles'), may hold values from 0.005 to 0.1
- neighbours: int32 [32, 4], P('tiles'), may hold values from -1 to 31, as said below
- links: int32 [32, 4], P('tiles'), may hold values from 0 to 7, as said below
- owners: int32 [32], replicated, may hold values from 0 to 7
Outputs:
- adjoint_out: float32 [4, 3, 32, 8100], P('slab', None, 'tiles')
- control_gradient: float32 [4, 8, 675], P('slab', 'tiles')
Inputs may be any that keep to these rules, and one draw needn't show every extreme that they name: Tiles are placed row by row in a layout of 8 columns, tile t at position t + 2: neighbours[t, s] is t - 8, t + 8, t - 1, t + 1 or -1, and links are mutual: if neighbours[t, s] = u >= 0 then neighbours[u, links[t, s] // 2] = t and links[u, links[t, s] // 2] = 2 s + links[t, s] % 2. `links`: 0 where the side is closed; odd only across the seam between the faces and the cap.
All inputs are finite; a program needn't handle non-finite values. No bound on the sum of `mask` on one device may be relied on, other than what follows from the above.
Results may differ from a plain program's by a relative error of at most 0.000071.
Values sent between devices are 32-bit elements; how exact they have to be, the bound alone decides.
No kernel may reach another device: no remote copies, remote signals or barrier semaphores. Data moves between devices by JAX's collectives and lax.ppermute only.
A program may use at most 64 MiB of HBM per device.

v0:
```python
import jax
import jax.numpy as jnp
from jax import lax
from jax.sharding import PartitionSpec as P

TILE = 90
SUBSTEPS = 2
BLOCK = 6
ROW_TILES = 8
COARSE = 15


def padded_2(cells, sides, width):
    for axis, dim in sides:
        count = lax.axis_size(axis)
        ends = count - 1
        head = lax.slice_in_dim(cells, 0, width, axis=dim)
        tail = lax.slice_in_dim(cells, cells.shape[dim] - width, cells.shape[dim], axis=dim)
        cells = jnp.concatenate(
            [
                lax.ppermute(tail, axis, [(i, (i + 1) % count) for i in range(ends)]),
                cells,
                lax.ppermute(head, axis, [((i + 1) % count, i) for i in range(ends)]),
            ],
            axis=dim,
        )
    return cells


def from_behind(block, axis, distance):
    devices = range(lax.axis_size(axis))
    route = [(i - distance, i) for i in devices if i - distance in devices]
    return lax.ppermute(block, axis, route)


def edge_rows(field):
    return jnp.concatenate(
        (field[..., 0, :], field[..., -1, :], field[..., :, 0], field[..., :, -1]), axis=-1
    )


def pick_halo(edge_all, source, neighbours, links):
    width = edge_all.shape[-1] // 4
    grid = edge_all.reshape(edge_all.shape[:-1] + (4, width))
    picked = grid[..., source, links // 2, :]
    picked = jnp.where((links % 2)[..., None] == 1, picked[..., ::-1], picked)
    return jnp.where(neighbours[..., None] >= 0, picked, jnp.float32(0.0))


def neighbour_sum(field, halo):
    upper = jnp.concatenate((halo[..., 0, :][..., None, :], field[..., :-1, :]), axis=-2)
    lower = jnp.concatenate((field[..., 1:, :], halo[..., 1, :][..., None, :]), axis=-2)
    left_side = jnp.concatenate((halo[..., 2, :][..., :, None], field[..., :, :-1]), axis=-1)
    right_side = jnp.concatenate((field[..., :, 1:], halo[..., 3, :][..., :, None]), axis=-1)
    return upper + lower + left_side + right_side


def reach_offsets(tiles_dev, number):
    found = set()
    for within in range(tiles_dev):
        for stride in (1, -1, ROW_TILES, -ROW_TILES):
            offset = (within + stride) // tiles_dev
            if offset != 0 and abs(offset) < number:
                found.add(offset)
    return sorted(found)


def window_slots(neighbours, offsets, tiles_dev, here):
    target = jnp.maximum(neighbours, 0)
    moved = target // tiles_dev - here
    slot = jnp.zeros_like(target)
    for number, offset in enumerate(offsets):
        slot = slot + (moved == offset).astype(jnp.int32) * (number + 1)
    return slot * tiles_dev + target % tiles_dev


def shards(adjoint, state, weights, vertical, mask, rate, neighbours, links, owners):
    levels_here, tracers, count_here, cells = adjoint.shape
    shape_four = (levels_here, count_here, TILE, TILE)
    lam = adjoint.reshape(levels_here, tracers, count_here, TILE, TILE)
    wet = mask.astype(jnp.float32).reshape(shape_four)
    mixing = wet * weights.reshape(shape_four)
    stacked = jnp.stack((vertical.reshape(shape_four), wet))
    padded = padded_2(stacked, (("slab", 1),), 1)
    above = stacked[0] * wet * padded[1, :-2]
    below = padded[0, 2:] * padded[1, 2:] * wet
    uptake = 1.0 - rate.reshape(1, tracers, count_here, TILE, TILE)
    wet_edges = edge_rows(wet)
    here = lax.axis_index("tiles")
    offsets = reach_offsets(count_here, lax.axis_size("tiles"))
    source = window_slots(neighbours, offsets, count_here, here)
    for step in range(SUBSTEPS):
        spread = mixing[:, None] * lam
        spread_edges = edge_rows(spread)
        wet_column = wet_edges[:, None]
        spread_parts = [spread_edges]
        wet_parts = [wet_column]
        for offset in offsets:
            moved_spread, moved_wet = from_behind((spread_edges, wet_column), "tiles", -offset)
            spread_parts.append(moved_spread)
            wet_parts.append(moved_wet)
        spread_all = jnp.concatenate(spread_parts, axis=2)
        wet_all = jnp.concatenate(wet_parts, axis=2)
        count = neighbour_sum(wet, pick_halo(wet_all[:, 0], source, neighbours, links))
        halo = pick_halo(spread_all, source, neighbours, links)
        horizontal = lam * (1.0 - (mixing * count)[:, None]) + wet[:, None] * neighbour_sum(
            spread, halo
        )
        taken = horizontal * uptake
        outer = padded_2(taken, (("slab", 0),), 1)
        lam = taken + above[:, None] * (outer[:-2] - taken) + below[:, None] * (outer[2:] - taken)
    term = wet[:, None] * lam * state.reshape(levels_here, tracers, count_here, TILE, TILE)
    term = term.reshape(levels_here, tracers, count_here, COARSE, BLOCK, COARSE, BLOCK).sum(
        axis=(4, 6)
    )
    term = term.reshape(levels_here, tracers, count_here, COARSE * COARSE)
    owner_count = lax.axis_size("tiles")
    start = here * count_here
    mine = lax.dynamic_slice_in_dim(owners, start, count_here)
    onehot = (mine[:, None] == jnp.arange(owner_count, dtype=jnp.int32)[None, :]).astype(
        jnp.float32
    )
    partial_terms = jnp.einsum("lctq,tk->lkcq", term, onehot, precision=lax.Precision.HIGHEST)
    partial_terms = partial_terms.reshape(levels_here, owner_count, tracers * COARSE * COARSE)
    gradient = lax.psum_scatter(partial_terms, "tiles", scatter_dimension=1, tiled=True)
    return (lam.reshape(levels_here, tracers, count_here, TILE * TILE), gradient)


def solution(mesh):
    placed = (
        P("slab", None, "tiles", None),
        P("slab", None, "tiles", None),
        P("slab", "tiles", None),
        P("slab", "tiles", None),
        P("slab", "tiles", None),
        P(None, "tiles", None),
        P("tiles", None),
        P("tiles", None),
        P(),
    )
    return jax.shard_map(
        shards,
        mesh=mesh,
        in_specs=placed,
        out_specs=(P("slab", None, "tiles", None), P("slab", "tiles", None)),
        check_vma=False,
    )
```

profile of v0, /device:TPU:0, one launch (start us, length us, event | category | flops | bytes accessed | tf_op | source)
XLA Modules:
  0.0 148.6 jit_solution(15857602420671330725)
XLA Ops:
  0.6 0.9 convert_element_type.4
  2.3 4.8 %collective-permute-start = (f32[1,1,4,360]{3,2,1,0:T(4,128)S(1)}, f32[1,1,4,360]{3,2,1,0:T(4,128)S(1)}, u32[]{:S(2)}, u32[]{:S(2)}) collective-permute-start(f32[1,1,4,360]{3,2,1,0:T(4,128)S(1)} %maximum_bitcast_fusion), channel_id=1, source_target_pairs={{0,8},{4,12},{8,16},{12,20},{16,24},{20,28},{1,9},{5,13},{9,17},{1... | collective-permute-start | bytes 17288 | tf_op jit(solution)/shard_map/ppermute | solution.py:33
  7.1 1.5 collective-permute-start.1
  8.6 1.3 collective-permute-start.2
  9.9 1.3 collective-permute-start.3
  11.5 1.2 squeeze_stack_reshape.3
  12.8 0.7 constant_dynamic-update-slice_fusion.6
  13.5 0.7 constant_dynamic-update-slice_fusion.5
  14.2 4.2 %collective-permute-start.8 = (f32[2,1,4,90,90]{4,3,2,1,0:T(8,128)}, f32[2,1,4,90,90]{4,3,2,1,0:T(8,128)}, u32[]{:S(2)}, u32[]{:S(2)}) collective-permute-start(f32[2,1,4,90,90]{4,3,2,1,0:T(8,128)} %constant_dynamic-update-slice_fusion.5), channel_id=1, source_target_pairs={{0,1},{1,2},{2,3},{4,5},{5,6},{6,7},{8,9},{9,10},{10,11},{12,13},{... | collective-permute-start | bytes 777608 | tf_op jit(solution)/shard_map/ppermute | solution.py:21
  18.5 1.1 broadcast_subtract_fusion
  19.6 0.7 fusion.27
  20.4 0.7 fusion.32
  21.4 0.9 sub.65
  22.7 1.2 reshape.556
  23.8 1.9 %reshape.554 = f32[1,3,4,90,90]{4,3,2,1,0:T(8,128)S(1)} reshape(f32[1,3,4,8100]{3,2,1,0:T(4,128)} %param.9) | data formatting | bytes 777600 | tf_op jit(solution)/shard_map/reshape | solution.py:80
  26.2 0.6 gather_fusion
  27.5 0.7 copy-done.3
  28.3 0.9 fusion.44
  29.2 0.7 slice_reduce_fusion.3
  30.0 6.8 %collective-permute-start.4 = (f32[1,3,4,360]{3,2,1,0:T(4,128)S(1)}, f32[1,3,4,360]{3,2,1,0:T(4,128)S(1)}, u32[]{:S(2)}, u32[]{:S(2)}) collective-permute-start(f32[1,3,4,360]{3,2,1,0:T(4,128)S(1)} %pad_maximum_fusion), channel_id=1, source_target_pairs={{0,8},{4,12},{8,16},{12,20},{16,24},{20,28},{1,9},{5,13},{9,17},{1... | collective-permute-start | bytes 51848 | tf_op jit(solution)/shard_map/ppermute | solution.py:33
  36.8 1.5 collective-permute-start.5
  38.3 1.3 collective-permute-start.6
  39.6 1.3 collective-permute-start.7
  40.9 1.2 fusion.43
  42.1 1.3 collective-permute-start.10
  43.4 0.9 collective-permute-done.6
  44.3 4.6 %collective-permute-done.7 = f32[1,3,4,360]{3,2,1,0:T(4,128)S(1)} collective-permute-done((f32[1,3,4,360]{3,2,1,0:T(4,128)S(1)}, f32[1,3,4,360]{3,2,1,0:T(4,128)S(1)}, u32[]{:S(2)}, u32[]{:S(2)}) %collective-permute-start.7) | collective-permute-done | bytes 17312 | tf_op jit(solution)/shard_map/ppermute | solution.py:33
  49.2 0.6 gather_fusion.1
  50.3 0.3 copy.122
  50.6 1.9 %fusion.4 = f32[1,3,4,90,90]{4,3,2,1,0:T(8,128)S(1)} fusion(f32[1,3,4,90,90]{4,3,2,1,0:T(8,128)S(1)} %sub.65, f32[1,3,4,89,90]{4,3,2,1,0:T(8,128)} %get-tuple-element.21, f32[1,3,4,1,90]{4,3,2,1,0:T(1,128)S(1)} %get-tuple-element.41, f32[1,3,4,1,90]{4,3,2,1,0:T(1,128)S(1)} %get-tuple-element.40, f32[1,3,4,89,90]{4,3,2,1,0:T(8,128)S(1)} %get-tuple-element.20, ...), kind=kLoop, calls=%fused_computation.13 | loop fusion | flops 1069200 | bytes 2980800 | tf_op jit(solution)/shard_map/mul | solution.py:109
  52.5 0.4 copy.123
  52.9 1.3 collective-permute-start.11
  54.2 4.6 %collective-permute-start.9 = (f32[1,3,4,90,90]{4,2,3,1,0:T(4,128)S(1)}, f32[1,3,4,90,90]{4,2,3,1,0:T(4,128)S(1)}, u32[]{:S(2)}, u32[]{:S(2)}) collective-permute-start(f32[1,3,4,90,90]{4,2,3,1,0:T(4,128)S(1)} %copy.123), channel_id=1, source_target_pairs={{0,1},{1,2},{2,3},{4,5},{5,6},{6,7},{8,9},{9,10},{10,11},{12,13},{... | collective-permute-start | bytes 1166408 | tf_op jit(solution)/shard_map/ppermute | solution.py:21
  58.8 1.3 fusion.20
  60.2 8.7 %collective-permute-done.11 = f32[1,3,4,90,90]{4,2,3,1,0:T(4,128)S(1)} collective-permute-done((f32[1,3,4,90,90]{4,2,3,1,0:T(4,128)S(1)}, f32[1,3,4,90,90]{4,2,3,1,0:T(4,128)S(1)}, u32[]{:S(2)}, u32[]{:S(2)}) %collective-permute-start.11) | collective-permute-done | bytes 388832 | tf_op jit(solution)/shard_map/ppermute | solution.py:23
  68.9 1.2 collective-permute-done.9
  70.1 1.1 broadcast_multiply_fusion
  71.2 1.1 fusion.41
  72.3 0.7 slice_reduce_fusion.1
  73.1 5.4 %collective-permute-start.12 = (f32[1,3,4,360]{3,2,1,0:T(4,128)S(1)}, f32[1,3,4,360]{3,2,1,0:T(4,128)S(1)}, u32[]{:S(2)}, u32[]{:S(2)}) collective-permute-start(f32[1,3,4,360]{3,2,1,0:T(4,128)S(1)} %pad_maximum_fusion.1), channel_id=1, source_target_pairs={{0,8},{4,12},{8,16},{12,20},{16,24},{20,28},{1,9},{5,13},{9,17},{1... | collective-permute-start | bytes 51848 | tf_op jit(solution)/shard_map/ppermute | solution.py:33
  78.4 1.3 collective-permute-start.13
  79.7 1.3 collective-permute-start.14
  81.0 1.3 collective-permute-start.15
  82.3 1.2 fusion.40
  83.5 1.9 %collective-permute-done.14 = f32[1,3,4,360]{3,2,1,0:T(4,128)S(1)} collective-permute-done((f32[1,3,4,360]{3,2,1,0:T(4,128)S(1)}, f32[1,3,4,360]{3,2,1,0:T(4,128)S(1)}, u32[]{:S(2)}, u32[]{:S(2)}) %collective-permute-start.14) | collective-permute-done | bytes 17312 | tf_op jit(solution)/shard_map/ppermute | solution.py:33
  85.4 4.6 %collective-permute-done.15 = f32[1,3,4,360]{3,2,1,0:T(4,128)S(1)} collective-permute-done((f32[1,3,4,360]{3,2,1,0:T(4,128)S(1)}, f32[1,3,4,360]{3,2,1,0:T(4,128)S(1)}, u32[]{:S(2)}, u32[]{:S(2)}) %collective-permute-start.15) | collective-permute-done | bytes 17312 | tf_op jit(solution)/shard_map/ppermute | solution.py:33
  90.3 0.6 gather_fusion.2
  91.5 0.3 copy.131
  91.8 2.1 %fusion.9 = f32[1,3,4,90,90]{4,3,2,1,0:T(8,128)S(1)} fusion(f32[1,3,4,90,90]{4,3,2,1,0:T(8,128)S(1)} %sub.65, f32[1,3,4,89,90]{4,3,2,1,0:T(8,128)} %get-tuple-element.15, f32[1,3,4,1,90]{4,3,2,1,0:T(1,128)S(1)} %get-tuple-element.37, f32[1,3,4,1,90]{4,3,2,1,0:T(1,128)S(1)} %get-tuple-element.36, f32[1,3,4,89,90]{4,3,2,1,0:T(8,128)} %get-tuple-element.14, ...), kind=kLoop, calls=%fused_computation.19 | loop fusion | flops 1069200 | bytes 2980800 | tf_op jit(solution)/shard_map/mul | solution.py:109
  93.8 0.4 copy.132
  94.2 1.3 collective-permute-start.17
  95.5 5.4 %collective-permute-start.16 = (f32[1,3,4,90,90]{4,2,3,1,0:T(4,128)S(1)}, f32[1,3,4,90,90]{4,2,3,1,0:T(4,128)}, u32[]{:S(2)}, u32[]{:S(2)}) collective-permute-start(f32[1,3,4,90,90]{4,2,3,1,0:T(4,128)S(1)} %copy.132), channel_id=1, source_target_pairs={{0,1},{1,2},{2,3},{4,5},{5,6},{6,7},{8,9},{9,10},{10,11},{12,13},{... | collective-permute-start | bytes 1166408 | tf_op jit(solution)/shard_map/ppermute | solution.py:21
  100.9 1.9 %reshape.562 = f32[1,3,4,90,90]{4,3,2,1,0:T(8,128)S(1)} reshape(f32[1,3,4,8100]{3,2,1,0:T(4,128)} %param.10) | data formatting | bytes 777600 | tf_op jit(solution)/shard_map/reshape | solution.py:112
  102.8 0.7 dynamic_slice.3
  103.6 1.2 dynamic-slice
  104.8 5.0 %collective-permute-done.17 = f32[1,3,4,90,90]{4,2,3,1,0:T(4,128)S(1)} collective-permute-done((f32[1,3,4,90,90]{4,2,3,1,0:T(4,128)S(1)}, f32[1,3,4,90,90]{4,2,3,1,0:T(4,128)S(1)}, u32[]{:S(2)}, u32[]{:S(2)}) %collective-permute-start.17) | collective-permute-done | bytes 388832 | tf_op jit(solution)/shard_map/ppermute | solution.py:23
  109.8 1.2 collective-permute-done.16
  111.0 1.4 multiply_multiply_fusion
  112.3 1.2 reshape.561
  113.6 0.4 copy.136
  113.9 6.3 %reshape.563 = f32[3,4,15,6,15,6]{5,4,1,3,2,0:T(8,128)} reshape(f32[1,3,4,90,90]{4,2,3,1,0:T(4,128)S(1)} %copy.136) | data formatting | bytes 777600 | tf_op jit(solution)/shard_map/reshape | solution.py:113
  120.2 4.4 %reduce_sum.9 = f32[3,4,15,15]{3,1,2,0:T(4,128)S(1)} reduce(f32[3,4,15,6,15,6]{5,4,1,3,2,0:T(8,128)} %reshape.563, f32[]{:T(128)} %constant.90.clone.1), dimensions={3,5}, to_apply=%region_0.1 | reduce | flops 94500 | bytes 399604 | tf_op jit(solution)/shard_map/reduce_sum | solution.py:113
  125.1 22.4 %all-reduce = f32[1,8,675]{2,1,0:T(8,128)S(1)} all-reduce(f32[1,8,675]{2,1,0:T(8,128)S(1)} %convolution_bitcast_fusion), channel_id=2, replica_groups=mesh['tiles'=8,'slab'=4] {'tiles'}, use_global_device_ids=true, to_apply=%region_1.2.clone | all-reduce | flops 5400 | bytes 43200
  147.4 1.2 constant_dynamic-slice_fusion
  (72 shorter events, 5.0 us)
Async XLA Ops:
  2.3 23.5 %collective-permute-start = (f32[1,1,4,360]{3,2,1,0:T(4,128)S(1)}, f32[1,1,4,360]{3,2,1,0:T(4,128)S(1)}, u32[]{:S(2)}, u32[]{:S(2)}) collective-permute-start(f32[1,1,4,360]{3,2,1,0:T(4,128)S(1)} %maximum_bitcast_fusion), channel_id=1, source_target_pairs={{0,8},{4,12},{8,16},{12,20},{16,24},{20,28},{1,9},{5,13},{9,17},{1... | collective-permute-start | bytes 17288 | tf_op jit(solution)/shard_map/ppermute | solution.py:33
  7.1 18.8 %collective-permute-start.1 = (f32[1,1,4,360]{3,2,1,0:T(4,128)S(1)}, f32[1,1,4,360]{3,2,1,0:T(4,128)S(1)}, u32[]{:S(2)}, u32[]{:S(2)}) collective-permute-start(f32[1,1,4,360]{3,2,1,0:T(4,128)S(1)} %maximum_bitcast_fusion), channel_id=1, source_target_pairs={{0,4},{4,8},{8,12},{12,16},{16,20},{20,24},{24,28},{1,5},{5,9},{9,... | collective-permute-start | bytes 17288 | tf_op jit(solution)/shard_map/ppermute | solution.py:33
  8.6 17.4 %collective-permute-start.2 = (f32[1,1,4,360]{3,2,1,0:T(4,128)S(1)}, f32[1,1,4,360]{3,2,1,0:T(4,128)S(1)}, u32[]{:S(2)}, u32[]{:S(2)}) collective-permute-start(f32[1,1,4,360]{3,2,1,0:T(4,128)S(1)} %maximum_bitcast_fusion), channel_id=1, source_target_pairs={{4,0},{8,4},{12,8},{16,12},{20,16},{24,20},{28,24},{5,1},{9,5},{13... | collective-permute-start | bytes 17288 | tf_op jit(solution)/shard_map/ppermute | solution.py:33
  9.9 16.2 %collective-permute-start.3 = (f32[1,1,4,360]{3,2,1,0:T(4,128)S(1)}, f32[1,1,4,360]{3,2,1,0:T(4,128)S(1)}, u32[]{:S(2)}, u32[]{:S(2)}) collective-permute-start(f32[1,1,4,360]{3,2,1,0:T(4,128)S(1)} %maximum_bitcast_fusion), channel_id=1, source_target_pairs={{8,0},{12,4},{16,8},{20,12},{24,16},{28,20},{9,1},{13,5},{17,9},{2... | collective-permute-start | bytes 17288 | tf_op jit(solution)/shard_map/ppermute | solution.py:33
  11.5 9.6 %copy-start.1 = (f32[1,1,4,90,90]{4,3,2,1,0:T(8,128)}, f32[1,1,4,90,90]{4,3,2,1,0:T(8,128)S(1)}, u32[]{:S(2)}) copy-start(f32[1,1,4,90,90]{4,3,2,1,0:T(8,128)S(1)} %reshape.559) | copy-start | bytes 388804
  12.7 8.4 %copy-start.2 = (f32[1,1,4,90,90]{4,3,2,1,0:T(8,128)}, f32[1,1,4,90,90]{4,3,2,1,0:T(8,128)S(1)}, u32[]{:S(2)}) copy-start(f32[1,1,4,90,90]{4,3,2,1,0:T(8,128)S(1)} %squeeze_stack_reshape.3) | copy-start | bytes 388804
  14.2 44.6 %collective-permute-start.8 = (f32[2,1,4,90,90]{4,3,2,1,0:T(8,128)}, f32[2,1,4,90,90]{4,3,2,1,0:T(8,128)}, u32[]{:S(2)}, u32[]{:S(2)}) collective-permute-start(f32[2,1,4,90,90]{4,3,2,1,0:T(8,128)} %constant_dynamic-update-slice_fusion.5), channel_id=1, source_target_pairs={{0,1},{1,2},{2,3},{4,5},{5,6},{6,7},{8,9},{9,10},{10,11},{12,13},{... | collective-permute-start | bytes 777608 | tf_op jit(solution)/shard_map/ppermute | solution.py:21
  27.5 0.7 copy-start.3
  30.0 12.1 %collective-permute-start.4 = (f32[1,3,4,360]{3,2,1,0:T(4,128)S(1)}, f32[1,3,4,360]{3,2,1,0:T(4,128)S(1)}, u32[]{:S(2)}, u32[]{:S(2)}) collective-permute-start(f32[1,3,4,360]{3,2,1,0:T(4,128)S(1)} %pad_maximum_fusion), channel_id=1, source_target_pairs={{0,8},{4,12},{8,16},{12,20},{16,24},{20,28},{1,9},{5,13},{9,17},{1... | collective-permute-start | bytes 51848 | tf_op jit(solution)/shard_map/ppermute | solution.py:33
  36.8 6.6 %collective-permute-start.5 = (f32[1,3,4,360]{3,2,1,0:T(4,128)S(1)}, f32[1,3,4,360]{3,2,1,0:T(4,128)S(1)}, u32[]{:S(2)}, u32[]{:S(2)}) collective-permute-start(f32[1,3,4,360]{3,2,1,0:T(4,128)S(1)} %pad_maximum_fusion), channel_id=1, source_target_pairs={{0,4},{4,8},{8,12},{12,16},{16,20},{20,24},{24,28},{1,5},{5,9},{9,... | collective-permute-start | bytes 51848 | tf_op jit(solution)/shard_map/ppermute | solution.py:33
  38.3 6.1 %collective-permute-start.6 = (f32[1,3,4,360]{3,2,1,0:T(4,128)S(1)}, f32[1,3,4,360]{3,2,1,0:T(4,128)S(1)}, u32[]{:S(2)}, u32[]{:S(2)}) collective-permute-start(f32[1,3,4,360]{3,2,1,0:T(4,128)S(1)} %pad_maximum_fusion), channel_id=1, source_target_pairs={{4,0},{8,4},{12,8},{16,12},{20,16},{24,20},{28,24},{5,1},{9,5},{13... | collective-permute-start | bytes 51848 | tf_op jit(solution)/shard_map/ppermute | solution.py:33
  39.6 9.4 %collective-permute-start.7 = (f32[1,3,4,360]{3,2,1,0:T(4,128)S(1)}, f32[1,3,4,360]{3,2,1,0:T(4,128)S(1)}, u32[]{:S(2)}, u32[]{:S(2)}) collective-permute-start(f32[1,3,4,360]{3,2,1,0:T(4,128)S(1)} %pad_maximum_fusion), channel_id=1, source_target_pairs={{8,0},{12,4},{16,8},{20,12},{24,16},{28,20},{9,1},{13,5},{17,9},{2... | collective-permute-start | bytes 51848 | tf_op jit(solution)/shard_map/ppermute | solution.py:33
  42.1 16.7 %collective-permute-start.10 = (f32[2,1,4,90,90]{4,3,2,1,0:T(8,128)}, f32[2,1,4,90,90]{4,3,2,1,0:T(8,128)}, u32[]{:S(2)}, u32[]{:S(2)}) collective-permute-start(f32[2,1,4,90,90]{4,3,2,1,0:T(8,128)} %constant_dynamic-update-slice_fusion.5), channel_id=1, source_target_pairs={{1,0},{2,1},{3,2},{5,4},{6,5},{7,6},{9,8},{10,9},{11,10},{13,12},{... | collective-permute-start | bytes 777608 | tf_op jit(solution)/shard_map/ppermute | solution.py:23
  52.9 16.0 %collective-permute-start.11 = (f32[1,3,4,90,90]{4,2,3,1,0:T(4,128)S(1)}, f32[1,3,4,90,90]{4,2,3,1,0:T(4,128)S(1)}, u32[]{:S(2)}, u32[]{:S(2)}) collective-permute-start(f32[1,3,4,90,90]{4,2,3,1,0:T(4,128)S(1)} %copy.123), channel_id=1, source_target_pairs={{1,0},{2,1},{3,2},{5,4},{6,5},{7,6},{9,8},{10,9},{11,10},{13,12},{... | collective-permute-start | bytes 1166408 | tf_op jit(solution)/shard_map/ppermute | solution.py:23
  54.2 15.9 %collective-permute-start.9 = (f32[1,3,4,90,90]{4,2,3,1,0:T(4,128)S(1)}, f32[1,3,4,90,90]{4,2,3,1,0:T(4,128)S(1)}, u32[]{:S(2)}, u32[]{:S(2)}) collective-permute-start(f32[1,3,4,90,90]{4,2,3,1,0:T(4,128)S(1)} %copy.123), channel_id=1, source_target_pairs={{0,1},{1,2},{2,3},{4,5},{5,6},{6,7},{8,9},{9,10},{10,11},{12,13},{... | collective-permute-start | bytes 1166408 | tf_op jit(solution)/shard_map/ppermute | solution.py:21
  60.2 31.6 %copy-start = (f32[4,90,90]{2,1,0:T(8,128)}, f32[4,90,90]{2,1,0:T(8,128)S(1)}, u32[]{:S(2)}) copy-start(f32[4,90,90]{2,1,0:T(8,128)S(1)} %get-tuple-element.25) | copy-start | bytes 388804
  73.1 10.5 %collective-permute-start.12 = (f32[1,3,4,360]{3,2,1,0:T(4,128)S(1)}, f32[1,3,4,360]{3,2,1,0:T(4,128)S(1)}, u32[]{:S(2)}, u32[]{:S(2)}) collective-permute-start(f32[1,3,4,360]{3,2,1,0:T(4,128)S(1)} %pad_maximum_fusion.1), channel_id=1, source_target_pairs={{0,8},{4,12},{8,16},{12,20},{16,24},{20,28},{1,9},{5,13},{9,17},{1... | collective-permute-start | bytes 51848 | tf_op jit(solution)/shard_map/ppermute | solution.py:33
  78.4 5.1 %collective-permute-start.13 = (f32[1,3,4,360]{3,2,1,0:T(4,128)S(1)}, f32[1,3,4,360]{3,2,1,0:T(4,128)S(1)}, u32[]{:S(2)}, u32[]{:S(2)}) collective-permute-start(f32[1,3,4,360]{3,2,1,0:T(4,128)S(1)} %pad_maximum_fusion.1), channel_id=1, source_target_pairs={{0,4},{4,8},{8,12},{12,16},{16,20},{20,24},{24,28},{1,5},{5,9},{9,... | collective-permute-start | bytes 51848 | tf_op jit(solution)/shard_map/ppermute | solution.py:33
  79.7 5.7 %collective-permute-start.14 = (f32[1,3,4,360]{3,2,1,0:T(4,128)S(1)}, f32[1,3,4,360]{3,2,1,0:T(4,128)S(1)}, u32[]{:S(2)}, u32[]{:S(2)}) collective-permute-start(f32[1,3,4,360]{3,2,1,0:T(4,128)S(1)} %pad_maximum_fusion.1), channel_id=1, source_target_pairs={{4,0},{8,4},{12,8},{16,12},{20,16},{24,20},{28,24},{5,1},{9,5},{13... | collective-permute-start | bytes 51848 | tf_op jit(solution)/shard_map/ppermute | solution.py:33
  81.0 9.0 %collective-permute-start.15 = (f32[1,3,4,360]{3,2,1,0:T(4,128)S(1)}, f32[1,3,4,360]{3,2,1,0:T(4,128)S(1)}, u32[]{:S(2)}, u32[]{:S(2)}) collective-permute-start(f32[1,3,4,360]{3,2,1,0:T(4,128)S(1)} %pad_maximum_fusion.1), channel_id=1, source_target_pairs={{8,0},{12,4},{16,8},{20,12},{24,16},{28,20},{9,1},{13,5},{17,9},{2... | collective-permute-start | bytes 51848 | tf_op jit(solution)/shard_map/ppermute | solution.py:33
  94.2 15.6 %collective-permute-start.17 = (f32[1,3,4,90,90]{4,2,3,1,0:T(4,128)S(1)}, f32[1,3,4,90,90]{4,2,3,1,0:T(4,128)S(1)}, u32[]{:S(2)}, u32[]{:S(2)}) collective-permute-start(f32[1,3,4,90,90]{4,2,3,1,0:T(4,128)S(1)} %copy.132), channel_id=1, source_target_pairs={{1,0},{2,1},{3,2},{5,4},{6,5},{7,6},{9,8},{10,9},{11,10},{13,12},{... | collective-permute-start | bytes 1166408 | tf_op jit(solution)/shard_map/ppermute | solution.py:23
  95.5 15.5 %collective-permute-start.16 = (f32[1,3,4,90,90]{4,2,3,1,0:T(4,128)S(1)}, f32[1,3,4,90,90]{4,2,3,1,0:T(4,128)}, u32[]{:S(2)}, u32[]{:S(2)}) collective-permute-start(f32[1,3,4,90,90]{4,2,3,1,0:T(4,128)S(1)} %copy.132), channel_id=1, source_target_pairs={{0,1},{1,2},{2,3},{4,5},{5,6},{6,7},{8,9},{9,10},{10,11},{12,13},{... | collective-permute-start | bytes 1166408 | tf_op jit(solution)/shard_map/ppermute | solution.py:21
where the time goes:
time: 150 us; the launch traced here: 149 us
  starting transfers between devices  47 us (31%)
  local copies, waits for them, and re-layouts  33.4 us (22%)
  waiting for transfers between devices  28.1 us (19%)
  blocking collectives  22.4 us (15%)
  other arithmetic  16.3 us (11%)
    ppermute x12, starting transfers between devices, from_behind(): return lax.ppermute(block, axis, route)  29 us
    unnamed x1, blocking collectives  22.4 us
    ppermute x3, starting transfers between devices, padded_2(): lax.ppermute(tail, axis, [(i, (i + 1) % count) for i in range(ends)])  14.2 us
    ppermute x3, waiting for transfers between devices, padded_2(): lax.ppermute(head, axis, [((i + 1) % count, i) for i in range(ends)])  13.7 us
    ppermute x12, waiting for transfers between devices, from_behind(): return lax.ppermute(block, axis, route)  12.1 us
    reshape x1, local copies, waits for them, and re-layouts, shards(): term.reshape(levels_here, tracers, count_here, COARSE, BLOCK, COARSE, BLOCK)  6.28 us
    unnamed x18, local copies, waits for them, and re-layouts  4.37 us
    reduce_sum x1, other arithmetic, shards(): term.reshape(levels_here, tracers, count_here, COARSE, BLOCK, COARSE, BLOCK)  4.35 us
  transfers between devices with their start and end apart: 18, of which 8 were waited for; matrix products, arithmetic and copies ran while one was open for 17% of the time, Pallas kernels for 0%

commit v1 on v0

v1 whole, which is shorter than its diff:
```python
import functools

import jax
import jax.numpy as jnp
from jax import lax
from jax.experimental import pallas as pl
from jax.experimental.pallas import tpu as pltpu
from jax.sharding import PartitionSpec as P

TILE = 90
CELLS = TILE * TILE
SUBSTEPS = 2
BLOCK = 6
COARSE = 15
LANES = 128
COLS = 32
HALF = COLS * LANES
TILES = 4
SIDES = 4
SPOTS = TILES * SIDES
F32 = jnp.float32
I32 = jnp.int32


def position():
    lane = lax.broadcasted_iota(I32, (8, LANES), 1)
    low = lax.broadcasted_iota(I32, (8, LANES), 0) < TILES
    return lane, low


def cell_at(lane, low, v):
    cell = lane + jnp.where(low, 0, HALF) + v * LANES
    y = (cell * 46604) >> 22
    return cell - y * TILE, y


def lane_gather(values, index):
    return jnp.take_along_axis(values, index, axis=1, mode="promise_in_bounds")


def fold(read, write):
    for v in range(COLS):
        write(v, 0, read(v * LANES, LANES))
        start = HALF + v * LANES
        width = min(LANES, CELLS - start)
        part = read(start, width)
        if width < LANES:
            part = jnp.concatenate([part, jnp.zeros((TILES, LANES - width), F32)], axis=1)
        write(v, TILES, part)


def set_guards(ref, plane, low):
    first, last = ref[plane, 1], ref[plane, COLS]
    ref[plane, 0] = jnp.where(low, 0.0, pltpu.roll(last, TILES, 0))
    ref[plane, COLS + 1] = jnp.where(low, pltpu.roll(first, TILES, 0), 0.0)


def inner_sum(ref, plane, v, lane, west, east):
    before, here, after = ref[plane, v], ref[plane, v + 1], ref[plane, v + 2]
    left = pltpu.roll(jnp.where(lane < LANES - 1, here, before), 1, 1)
    right = pltpu.roll(jnp.where(lane >= 1, here, after), LANES - 1, 1)
    up = pltpu.roll(jnp.where(lane < LANES - TILE, here, before), TILE, 1)
    down = pltpu.roll(jnp.where(lane >= TILE, here, after), LANES - TILE, 1)
    return jnp.where(west, 0.0, left) + jnp.where(east, 0.0, right) + (up + down)


def edge_sides(load, planes, lane, low):
    base = TILE * lane - jnp.where(low, 0, HALF)
    index = [(base + shift) & (LANES - 1) for shift in (0, TILE - 1)]
    column = [(base + shift) >> 7 for shift in (0, TILE - 1)]

    def body(v, found):
        hit = [c == v for c in column]
        out = []
        for p in range(planes):
            values = load(p, v)
            for k in range(2):
                out.append(jnp.where(hit[k], lane_gather(values, index[k]), found[2 * p + k]))
        return tuple(out)

    found = lax.fori_loop(0, COLS, body, tuple(jnp.zeros((8, LANES), F32) for _ in range(2 * planes)), unroll=4)
    bottom = CELLS - TILE - HALF + lane
    out = []
    for p in range(planes):
        sides = [jnp.where(lane < TILE, load(p, 0), 0.0)[:TILES]]
        picked = jnp.where(
            (bottom >> 7) == COLS - 2,
            lane_gather(load(p, COLS - 2), bottom & (LANES - 1)),
            lane_gather(load(p, COLS - 1), bottom & (LANES - 1)),
        )
        sides.append(jnp.where(lane < TILE, picked, 0.0)[TILES:])
        for k in range(2):
            sides.append(found[2 * p + k][:TILES] + found[2 * p + k][TILES:])
        out.append(sides)
    return out


def put_sides(ref, start, sides):
    for s in range(SIDES):
        ref[pl.ds(start + s, TILES, stride=SIDES), :] = sides[s]


def halos(near_ref, link_ref, all_ref, rows, channels, out_ref):
    sub = lax.broadcasted_iota(I32, (SPOTS, LANES), 0)
    lane = lax.broadcasted_iota(I32, (SPOTS, LANES), 1)
    turned = jnp.zeros((SPOTS, LANES), I32)
    open_ = jnp.zeros((SPOTS, LANES), I32)
    for t in range(TILES):
        for s in range(SIDES):
            spot = t * SIDES + s
            near, link = near_ref[t, s], link_ref[t, s]
            tile = jnp.maximum(near, 0)
            row = (tile // TILES) * (3 * rows) + (tile % TILES) * SIDES + link // 2
            for level in range(3):
                out_ref[pl.ds(level * rows + spot, channels, stride=SPOTS), :] = all_ref[
                    pl.ds(row + level * rows, channels, stride=SPOTS), :
                ]
            turned = jnp.where(sub == spot, link % 2, turned)
            open_ = jnp.where(sub == spot, (near >= 0).astype(I32), open_)
    back = jnp.clip(TILE - 1 - lane, 0, LANES - 1)
    for k in range(3 * channels):
        for h in range(0, SPOTS, 8):
            at = pl.ds(k * SPOTS + h, 8)
            values = out_ref[at, :]
            values = jnp.where(turned[h : h + 8] == 1, lane_gather(values, back[h : h + 8]), values)
            keep = (open_[h : h + 8] == 1) & (lane[h : h + 8] < TILE)
            out_ref[at, :] = jnp.where(keep, values, 0.0)


def spot_rows(ref, index):
    return ref[pl.ds(index * SPOTS, SPOTS), :]


def edge_change(halo, halo_wet, edge, edge_wet, keep, mix_a, mix_b, tracers, out_ref):
    for c in range(tracers):
        parts = []
        for level in range(3):
            parts.append(keep(c) * (edge_wet(level) * halo(level, c) - edge(level, c) * halo_wet(level)))
        own, first, second = parts
        out_ref[pl.ds(c * SPOTS, SPOTS), :] = own + mix_a * (first - own) + mix_b * (second - own)


def change_planes(ref, tracers):
    out = []
    for c in range(tracers):
        sides = [ref[pl.ds(c * SPOTS + s, TILES, stride=SIDES), :] for s in range(SIDES)]
        out.append([jnp.concatenate([side, side], axis=0) for side in sides])
    return out


def add_columns(planes, v, lane, low):
    x, y = cell_at(lane, low, v)
    y = jnp.minimum(y, LANES - 1)
    west, east = x == 0, x == TILE - 1
    out = []
    for sides in planes:
        out.append(jnp.where(west, lane_gather(sides[2], y), 0.0) + jnp.where(east, lane_gather(sides[3], y), 0.0))
    return out


def add_rows(ref, planes, lane, low):
    place = (CELLS - TILE - HALF) % LANES
    for c, sides in enumerate(planes):
        ref[c, 0] = ref[c, 0] + jnp.where(low, sides[0], 0.0)
        turned = pltpu.roll(sides[1], place, 1)
        ref[c, COLS - 2] = ref[c, COLS - 2] + jnp.where(low | (lane < place), 0.0, turned)
        ref[c, COLS - 1] = ref[c, COLS - 1] + jnp.where(low | (lane >= place + TILE - LANES), 0.0, turned)


def open_kernel(adjoint_ref, weights_ref, vertical_ref, mask_ref, lam_ref, wet_ref, mixing_ref, pack_a, pack_b, spread):
    tracers = lam_ref.shape[0]
    even = lax.axis_index("slab") % 2 == 0
    head = (tracers + 1) * SPOTS

    def write_to(ref, *lead):
        def write(v, row, part):
            ref[(*lead, v, pl.ds(row, TILES), slice(None))] = part

        return write

    fold(lambda a, n: mask_ref[0, :, a : a + n].astype(F32), write_to(wet_ref))
    fold(lambda a, n: weights_ref[0, :, a : a + n], write_to(mixing_ref))
    fold(lambda a, n: vertical_ref[0, :, a : a + n], write_to(spread, tracers))
    for c in range(tracers):
        fold(lambda a, n, c=c: adjoint_ref[0, c, :, a : a + n], write_to(lam_ref, c))
    lane, low = position()

    def body(v, carry):
        wet = wet_ref[v]
        mixing = wet * mixing_ref[v]
        mixing_ref[v] = mixing
        for c in range(tracers):
            spread[c, v] = mixing * lam_ref[c, v]
        vertical = spread[tracers, v]
        at = pl.ds(head + v * 8, 8)
        pack_a[at, :] = wet * jnp.where(even, 1.0, vertical)
        pack_b[at, :] = wet * jnp.where(even, vertical, 1.0)
        spread[tracers, v] = wet
        return carry

    lax.fori_loop(0, COLS, body, 0, unroll=4)
    found = edge_sides(lambda p, v: spread[p, v], tracers + 1, lane, low)
    for p in range(tracers + 1):
        put_sides(pack_a, p * SPOTS, found[p])
        put_sides(pack_b, p * SPOTS, found[p])


def inner_first_kernel(lam_ref, wet_ref, mixing_ref, rate_ref, out_ref, stay_ref, keep_ref, spread):
    tracers = lam_ref.shape[0]
    lane, low = position()
    for c in range(tracers):

        def write(v, row, part, c=c):
            keep_ref[c, v, pl.ds(row, TILES), :] = 1.0 - part

        fold(lambda a, n, c=c: rate_ref[c, :, a : a + n], write)

    def fill(v, carry):
        mixing = mixing_ref[v]
        for c in range(tracers):
            spread[c, v + 1] = mixing * lam_ref[c, v]
        spread[tracers, v + 1] = wet_ref[v]
        return carry

    lax.fori_loop(0, COLS, fill, 0, unroll=4)
    for c in range(tracers + 1):
        set_guards(spread, c, low)

    def body(v, carry):
        x, _ = cell_at(lane, low, v)
        west, east = x == 0, x == TILE - 1
        wet = wet_ref[v]
        stay = 1.0 - mixing_ref[v] * inner_sum(spread, tracers, v, lane, west, east)
        stay_ref[v] = stay
        for c in range(tracers):
            moved = inner_sum(spread, c, v, lane, west, east)
            out_ref[c, v] = (lam_ref[c, v] * stay + wet * moved) * keep_ref[c, v]
        return carry

    lax.fori_loop(0, COLS, body, 0, unroll=2)


def inner_kernel(lam_ref, wet_ref, mixing_ref, stay_ref, keep_ref, out_ref, spread):
    tracers = lam_ref.shape[0]
    lane, low = position()

    def fill(v, carry):
        mixing = mixing_ref[v]
        for c in range(tracers):
            spread[c, v + 1] = mixing * lam_ref[c, v]
        return carry

    lax.fori_loop(0, COLS, fill, 0, unroll=4)
    for c in range(tracers):
        set_guards(spread, c, low)

    def body(v, carry):
        x, _ = cell_at(lane, low, v)
        west, east = x == 0, x == TILE - 1
        wet, stay = wet_ref[v], stay_ref[v]
        for c in range(tracers):
            moved = inner_sum(spread, c, v, lane, west, east)
            out_ref[c, v] = (lam_ref[c, v] * stay + wet * moved) * keep_ref[c, v]
        return carry

    lax.fori_loop(0, COLS, body, 0, unroll=2)


def middle_kernel(
    near_ref, link_ref, all_ref, pack_a, pack_b, got_a, got_b, taken_ref, from_a, from_b, keep_ref, mixing_ref,
    lam_ref, mix_a_ref, mix_b_ref, edge_ref, still_ref, halo_ref, change_ref, spread,
):
    tracers = lam_ref.shape[0]
    channels = tracers + 1
    rows = channels * SPOTS
    lane, low = position()
    halos(near_ref, link_ref, all_ref, rows, channels, halo_ref)

    def mix(v, carry):
        at = pl.ds(rows + v * 8, 8)
        mix_a_ref[v] = pack_a[at, :] * got_a[at, :]
        mix_b_ref[v] = pack_b[at, :] * got_b[at, :]
        return carry

    lax.fori_loop(0, COLS, mix, 0, unroll=4)

    def load(p, v):
        if p < tracers:
            return keep_ref[p, v]
        return (mix_a_ref if p == tracers else mix_b_ref)[v]

    for p, sides in enumerate(edge_sides(load, tracers + 2, lane, low)):
        put_sides(still_ref, p * SPOTS, sides)
    for level in range(3):
        still_ref[pl.ds((tracers + 2 + level) * SPOTS, SPOTS), :] = spot_rows(halo_ref, level * channels + tracers)
    packs = (pack_a, got_a, got_b)
    edge_change(
        lambda level, c: spot_rows(halo_ref, level * channels + c),
        lambda level: spot_rows(halo_ref, level * channels + tracers),
        lambda level, c: spot_rows(packs[level], c),
        lambda level: spot_rows(packs[level], tracers),
        lambda c: spot_rows(still_ref, c),
        spot_rows(still_ref, tracers),
        spot_rows(still_ref, tracers + 1),
        tracers,
        change_ref,
    )
    planes = change_planes(change_ref, tracers)

    def body(v, carry):
        first, second = mix_a_ref[v], mix_b_ref[v]
        extra = add_columns(planes, v, lane, low)
        for c in range(tracers):
            taken = taken_ref[c, v]
            lam_ref[c, v] = taken + first * (from_a[c, v] - taken) + second * (from_b[c, v] - taken) + extra[c]
        return carry

    lax.fori_loop(0, COLS, body, 0, unroll=2)
    add_rows(lam_ref, planes, lane, low)

    def spreads(v, carry):
        for c in range(tracers):
            spread[c, v] = mixing_ref[v] * lam_ref[c, v]
        return carry

    lax.fori_loop(0, COLS, spreads, 0, unroll=4)
    for p, sides in enumerate(edge_sides(lambda p, v: spread[p, v], tracers, lane, low)):
        put_sides(edge_ref, p * SPOTS, sides)


def close_kernel(
    near_ref, link_ref, owner_ref, all_ref, pack_a, got_a, got_b, edge_ref, edge_a, edge_b, still_ref,
    taken_ref, from_a, from_b, mix_a_ref, mix_b_ref, wet_ref, state_ref,
    out_ref, part_ref, halo_ref, change_ref, lam_ref, term_ref, rows_ref, sums_ref,
):
    tracers = taken_ref.shape[0]
    rows = tracers * SPOTS
    lane, low = position()
    halos(near_ref, link_ref, all_ref, rows, tracers, halo_ref)
    packs = (pack_a, got_a, got_b)
    edges = (edge_ref, edge_a, edge_b)
    edge_change(
        lambda level, c: spot_rows(halo_ref, level * tracers + c),
        lambda level: spot_rows(still_ref, tracers + 2 + level),
        lambda level, c: spot_rows(edges[level], c),
        lambda level: spot_rows(packs[level], tracers),
        lambda c: spot_rows(still_ref, c),
        spot_rows(still_ref, tracers),
        spot_rows(still_ref, tracers + 1),
        tracers,
        change_ref,
    )
    planes = change_planes(change_ref, tracers)
    for c in range(tracers):

        def write(v, row, part, c=c):
            term_ref[c, v, pl.ds(row, TILES), :] = part

        fold(lambda a, n, c=c: state_ref[0, c, :, a : a + n], write)

    def body(v, carry):
        first, second = mix_a_ref[v], mix_b_ref[v]
        extra = add_columns(planes, v, lane, low)
        for c in range(tracers):
            taken = taken_ref[c, v]
            lam_ref[c, v] = taken + first * (from_a[c, v] - taken) + second * (from_b[c, v] - taken) + extra[c]
        return carry

    lax.fori_loop(0, COLS, body, 0, unroll=2)
    add_rows(lam_ref, planes, lane, low)

    def terms(v, carry):
        for c in range(tracers):
            term_ref[c, v] = wet_ref[v] * lam_ref[c, v] * term_ref[c, v]
        return carry

    lax.fori_loop(0, COLS, terms, 0, unroll=4)
    for c in range(tracers):
        for v in range(COLS):
            values = lam_ref[c, v]
            out_ref[0, c, :, v * LANES : (v + 1) * LANES] = values[:TILES]
            start = HALF + v * LANES
            width = min(LANES, CELLS - start)
            out_ref[0, c, :, start : start + width] = values[TILES:, :width]
        guard = pltpu.roll(term_ref[c, 0], TILES, 0)
        for block in range(COARSE):
            total = [None, None]
            for y in range(block * BLOCK, (block + 1) * BLOCK):
                half = y * TILE // HALF
                v, shift = divmod(y * TILE - half * HALF, LANES)
                values = term_ref[c, v]
                if shift + TILE > LANES:
                    after = term_ref[c, v + 1] if v + 1 < COLS else guard
                    values = jnp.where(lane >= shift, values, after)
                if shift:
                    values = pltpu.roll(values, LANES - shift, 1)
                total[half] = values if total[half] is None else total[half] + values
            parts = [total[h][h * TILES : (h + 1) * TILES] for h in range(2) if total[h] is not None]
            summed = parts[0] if len(parts) == 1 else parts[0] + parts[1]
            summed = jnp.where(lane[:TILES] < TILE, summed, 0.0)
            rows_ref[pl.ds((c * COARSE + block) * TILES, TILES), :] = summed
    lane_in = lax.broadcasted_iota(I32, (LANES, LANES), 0)
    lane_out = lax.broadcasted_iota(I32, (LANES, LANES), 1)
    low_edge = lane_out * BLOCK
    pick = ((lane_in >= low_edge) & (lane_in < low_edge + BLOCK) & (lane_out < COARSE)).astype(F32)
    sums_ref[...] = jnp.dot(rows_ref[...], pick, precision=lax.Precision.HIGHEST, preferred_element_type=F32)
    for spot in range(8):
        total = jnp.zeros((TILES, LANES), F32)
        for k in range(tracers * COARSE):
            start = k * COARSE - spot * LANES
            if start >= LANES or start + COARSE <= 0:
                continue
            values = sums_ref[pl.ds(k * TILES, TILES), :]
            values = pltpu.roll(values, start % LANES, 1) if start % LANES else values
            if start < 0:
                values = jnp.where(lane[:TILES] < start + COARSE, values, 0.0)
            elif start + COARSE > LANES:
                values = jnp.where(lane[:TILES] >= start, values, 0.0)
            total = total + values
        rows_ref[pl.ds(spot, TILES, stride=8), :] = total
    part_ref[...] = jnp.zeros_like(part_ref)
    me = lax.axis_index("tiles")
    for t in range(TILES):
        owner = owner_ref[me * TILES + t]
        part_ref[owner] = part_ref[owner] + rows_ref[pl.ds(t * 8, 8), :]


def swaps(count):
    return (
        [pair for i in range(0, count - 1, 2) for pair in ((i, i + 1), (i + 1, i))],
        [pair for i in range(1, count - 1, 2) for pair in ((i, i + 1), (i + 1, i))],
    )


def call(kernel, out, scratch, scalars=0, **kwargs):
    def run(*args):
        return pl.pallas_call(
            kernel,
            out_shape=[jax.ShapeDtypeStruct(shape, F32) for shape in out],
            in_specs=[pl.BlockSpec(memory_space=pltpu.SMEM)] * scalars
            + [pl.BlockSpec(memory_space=pltpu.VMEM)] * (len(args) - scalars),
            out_specs=[pl.BlockSpec(memory_space=pltpu.VMEM)] * len(out),
            scratch_shapes=[pltpu.VMEM(shape, F32) for shape in scratch],
            compiler_params=pltpu.CompilerParams(vmem_limit_bytes=48 * 1024 * 1024),
            name=kernel.__name__,
        )(*args)

    return run


def shards(adjoint, state, weights, vertical, mask, rate, neighbours, links, owners):
    tracers = adjoint.shape[1]
    number = lax.axis_size("tiles")
    even_swap, odd_swap = swaps(lax.axis_size("slab"))
    plane = (COLS, 8, LANES)
    planes = (tracers, *plane)
    channels = tracers + 1
    head = channels * SPOTS
    pack = (head + COLS * 8, LANES)

    lam, wet, mixing, pack_a, pack_b = call(
        open_kernel, [planes, plane, plane, pack, pack], [(channels, *plane)]
    )(adjoint, weights, vertical, mask)
    got_a = lax.ppermute(pack_a, "slab", even_swap)
    got_b = lax.ppermute(pack_b, "slab", odd_swap)
    guarded = (COLS + 2, 8, LANES)
    taken, stay, keep = call(inner_first_kernel, [planes, plane, planes], [(channels, *guarded)])(
        lam, wet, mixing, rate
    )
    from_a = lax.ppermute(taken, "slab", even_swap)
    from_b = lax.ppermute(taken, "slab", odd_swap)
    edges = lax.all_gather(jnp.stack([pack_a[:head], got_a[:head], got_b[:head]]), "tiles")
    edges = edges.reshape(number * 3 * head, LANES)
    rows = tracers * SPOTS
    lam, mix_a, mix_b, edge, still = call(
        middle_kernel,
        [planes, plane, plane, (rows, LANES), ((tracers + 5) * SPOTS, LANES)],
        [(3 * head, LANES), (rows, LANES), planes],
        2,
    )(neighbours, links, edges, pack_a, pack_b, got_a, got_b, taken, from_a, from_b, keep, mixing)
    edge_a = lax.ppermute(edge, "slab", even_swap)
    edge_b = lax.ppermute(edge, "slab", odd_swap)
    (taken,) = call(inner_kernel, [planes], [(tracers, *guarded)])(lam, wet, mixing, stay, keep)
    from_a = lax.ppermute(taken, "slab", even_swap)
    from_b = lax.ppermute(taken, "slab", odd_swap)
    edges = lax.all_gather(jnp.stack([edge, edge_a, edge_b]), "tiles")
    edges = edges.reshape(number * 3 * rows, LANES)
    out, part = call(
        close_kernel,
        [adjoint.shape, (number, 8, LANES)],
        [(3 * rows, LANES), (rows, LANES), planes, planes, (tracers * COARSE * TILES + 4, LANES), (tracers * COARSE * TILES + 4, LANES)],
        3,
    )(
        neighbours, links, owners, edges, pack_a, got_a, got_b, edge, edge_a, edge_b, still,
        taken, from_a, from_b, mix_a, mix_b, wet, state,
    )
    part = lax.all_to_all(part, "tiles", 0, 0, tiled=True)
    gradient = part.sum(axis=0).reshape(1, 1, 8 * LANES)[:, :, : tracers * COARSE * COARSE]
    return out, gradient


def solution(mesh):
    placed = (
        P("slab", None, "tiles", None),
        P("slab", None, "tiles", None),
        P("slab", "tiles", None),
        P("slab", "tiles", None),
        P("slab", "tiles", None),
        P(None, "tiles", None),
        P("tiles", None),
        P("tiles", None),
        P(),
    )
    return jax.shard_map(
        shards,
        mesh=mesh,
        in_specs=placed,
        out_specs=(P("slab", None, "tiles", None), P("slab", "tiles", None)),
        check_vma=False,
    )
```

time: 150 us -> 80.7 us (0.54)
  starting transfers between devices: 47 us -> 16.7 us
  local copies, waits for them, and re-layouts: 33.4 us -> 5.63 us
  other arithmetic: 16.3 us -> 0.02 us
  Pallas kernels: 0 us -> 13.1 us
  waiting for transfers between devices: 28.1 us -> 16.2 us
  blocking collectives: 22.4 us -> 27.9 us
    ppermute x18 -> x8, starting transfers between devices: 47 us -> 16.7 us  [the longest x2 9.37 us: shards(): from_a = lax.ppermute(taken, 'slab', even_swap)]
    unnamed x1 -> x0, blocking collectives: 22.4 us -> none
    all_gather x0 -> x2, blocking collectives: none -> 20.5 us  [the longest x1 10.4 us: shards(): lax.all_gather(jnp.stack([pack_a[:head], got_a[:head], got_b[:head]]), 't...]
    reshape x12 -> x0, local copies, waits for them, and re-layouts: 13.8 us -> none  [the longest x1 6.28 us: shards(): term.reshape(levels_here, tracers, count_here, COARSE, BLOCK, COARSE, BLOCK)]
    pallas_call x0 -> x5, Pallas kernels: none -> 13.1 us  [run(): pl.pallas_call(kernel, out_shape=[jax.ShapeDtypeStruct(shape, F32) for sh...]
    ppermute x18 -> x8, waiting for transfers between devices: 28.1 us -> 16.2 us  [the longest x1 9.89 us: shards(): got_a = lax.ppermute(pack_a, 'slab', even_swap)]
    mul x6 -> x0, other arithmetic: 7.82 us -> none  [the longest x2 3.97 us: shards(): taken = horizontal * uptake]
    all_to_all x0 -> x1, blocking collectives: none -> 7.37 us  [shards(): part = lax.all_to_all(part, 'tiles', 0, 0, tiled=True)]
  transfers between devices with their start and end apart: 18 -> 8, of which waited for: 8 -> 2; matrix products, arithmetic and copies ran while one was open for 17% -> 0% of each run, Pallas kernels for 0% -> 0%
where the time goes in v1:
time: 80.7 us; the launch traced here: 80.3 us
  blocking collectives  27.9 us (35%)
  starting transfers between devices  16.7 us (21%)
  waiting for transfers between devices  16.2 us (20%)
  Pallas kernels  13.1 us (16%)
  local copies, waits for them, and re-layouts  5.63 us (7%)
    pallas_call x5, Pallas kernels, run(): pl.pallas_call(kernel, out_shape=[jax.ShapeDtypeStruct(shape, F32) for sh...  13.1 us
    all_gather x1, blocking collectives, shards(): lax.all_gather(jnp.stack([pack_a[:head], got_a[:head], got_b[:head]]), 't...  10.4 us
    all_gather x1, blocking collectives, shards(): edges = lax.all_gather(jnp.stack([edge, edge_a, edge_b]), 'tiles')  10.1 us
    ppermute x1, waiting for transfers between devices, shards(): got_a = lax.ppermute(pack_a, 'slab', even_swap)  9.89 us
    ppermute x2, starting transfers between devices, shards(): from_a = lax.ppermute(taken, 'slab', even_swap)  9.37 us
    all_to_all x1, blocking collectives, shards(): part = lax.all_to_all(part, 'tiles', 0, 0, tiled=True)  7.37 us
    ppermute x1, waiting for transfers between devices, shards(): edge_a = lax.ppermute(edge, 'slab', even_swap)  6.31 us
    unnamed x18, local copies, waits for them, and re-layouts  5.03 us
  transfers between devices with their start and end apart: 8, of which 2 were waited for; matrix products, arithmetic and copies ran while one was open for 0% of the time, Pallas kernels for 0%

profile of v1, /device:TPU:0, one launch (start us, length us, event | category | flops | bytes accessed | tf_op | source)
XLA Modules:
  0.0 80.3 jit_solution(14425098426156759386)
XLA Ops:
  0.6 0.0 copy-start
  0.6 1.0 %copy-done = f32[1,3,4,8100]{3,2,1,0:T(4,128)S(1)} copy-done((f32[1,3,4,8100]{3,2,1,0:T(4,128)S(1)}, f32[1,3,4,8100]{3,2,1,0:T(4,128)}, u32[]{:S(2)}) %copy-start) | copy-done | bytes 388824
  1.6 0.0 copy-start.3
  1.6 0.9 %copy-done.3 = f32[1,4,8100]{2,1,0:T(4,128)S(1)} copy-done((f32[1,4,8100]{2,1,0:T(4,128)S(1)}, f32[1,4,8100]{2,1,0:T(4,128)}, u32[]{:S(2)}) %copy-start.3) | copy-done | bytes 129624
  2.5 0.0 copy-start.4
  2.5 0.9 %copy-done.4 = f32[1,4,8100]{2,1,0:T(4,128)S(1)} copy-done((f32[1,4,8100]{2,1,0:T(4,128)S(1)}, f32[1,4,8100]{2,1,0:T(4,128)}, u32[]{:S(2)}) %copy-start.4) | copy-done | bytes 129624
  3.4 0.0 copy-start.5
  3.4 0.9 %copy-done.5 = s32[1,4,8100]{2,1,0:T(4,128)S(1)} copy-done((s32[1,4,8100]{2,1,0:T(4,128)S(1)}, s32[1,4,8100]{2,1,0:T(4,128)}, u32[]{:S(2)}) %copy-start.5) | copy-done | bytes 129624
  4.3 0.0 copy-start.1
  4.3 1.2 %open_kernel.1 = (f32[3,32,8,128]{3,2,1,0:T(8,128)S(1)}, f32[32,8,128]{2,1,0:T(8,128)S(1)}, f32[32,8,128]{2,1,0:T(8,128)S(1)}, f32[320,128]{1,0:T(8,128)S(1)}, f32[320,128]{1,0:T(8,128)S(1)}) custom-call(f32[1,3,4,8100]{3,2,1,0:T(4,128)S(1)} %copy-done, f32[1,4,8100]{2,1,0:T(4,128)S(1)} %copy-done.3, f32[1,4,8100]{2,1,0:T(4,128)S(1)} %copy-done.4, ...), custom_call_target="tpu_custom_call" | custom-call | tf_op jit(solution)/shard_map/open_kernel/pallas_call | solution.py:437
  5.5 0.0 copy-done.1
  5.5 1.9 %inner_first_kernel.1 = (f32[3,32,8,128]{3,2,1,0:T(8,128)S(1)}, f32[32,8,128]{2,1,0:T(8,128)S(1)}, f32[3,32,8,128]{3,2,1,0:T(8,128)S(1)}) custom-call(f32[3,32,8,128]{3,2,1,0:T(8,128)S(1)} %get-tuple-element.19.lam_ref, f32[32,8,128]{2,1,0:T(8,128)S(1)} %get-tuple-element.20.wet_ref, f32[32,8,128]{2,1,0:T(8,128)S(1)} %get-tuple-element.21.mixing_ref, ...), custom_call_target="tpu_custom_call" | custom-call | tf_op jit(solution)/shard_map/inner_first_kernel/pallas_call | solution.py:437
  7.4 0.7 collective-permute-start.3
  8.1 5.9 %collective-permute-start.2 = (f32[3,32,8,128]{3,2,1,0:T(8,128)S(1)}, f32[3,32,8,128]{3,2,1,0:T(8,128)S(1)}, u32[]{:S(2)}, u32[]{:S(2)}) collective-permute-start(f32[3,32,8,128]{3,2,1,0:T(8,128)S(1)} %get-tuple-element.22.taken_ref), channel_id=1, source_target_pairs={{0,1},{1,0},{2,3},{3,2},{4,5},{5,4},{6,7},{7,6},{8,9},{9,8},{10,11... | collective-permute-start | bytes 1179656 | tf_op jit(solution)/shard_map/ppermute | solution.py:470
  14.0 0.7 collective-permute-start.1
  14.7 1.8 %collective-permute-start = (f32[320,128]{1,0:T(8,128)S(1)}, f32[320,128]{1,0:T(8,128)S(1)}, u32[]{:S(2)}, u32[]{:S(2)}) collective-permute-start(f32[320,128]{1,0:T(8,128)S(1)} %get-tuple-element.17.pack_a), channel_id=1, source_target_pairs={{0,1},{1,0},{2,3},{3,2},{4,5},{5,4},{6,7},{7,6},{8,9},{9,8},{10,11... | collective-permute-start | bytes 491528 | tf_op jit(solution)/shard_map/ppermute | solution.py:464
  16.5 0.0 collective-permute-done.1.got_b
  16.5 9.9 %collective-permute-done.got_a = f32[320,128]{1,0:T(8,128)S(1)} collective-permute-done((f32[320,128]{1,0:T(8,128)S(1)}, f32[320,128]{1,0:T(8,128)S(1)}, u32[]{:S(2)}, u32[]{:S(2)}) %collective-permute-start) | collective-permute-done | bytes 163872 | tf_op jit(solution)/shard_map/ppermute | solution.py:464
  26.4 0.0 copy-start.7
  26.4 10.4 %all-gather = f32[24,64,128]{2,1,0:T(8,128)S(1)} all-gather(f32[3,64,128]{2,1,0:T(8,128)S(1)} %pad_maximum_fusion), channel_id=2, replica_groups=mesh['tiles'=8,'slab'=4] {'tiles'}, dimensions={0}, use_global_device_ids=true | all-gather | bytes 884736 | tf_op jit(solution)/shard_map/all_gather | solution.py:472
  36.8 0.0 copy-start.6
  36.8 0.0 collective-permute-done.3.from_b
  36.8 0.0 collective-permute-done.2.from_a
  36.8 0.0 copy-done.7
  36.8 0.7 copy-done.6
  37.5 4.4 %middle_kernel.1 = (f32[3,32,8,128]{3,2,1,0:T(8,128)S(1)}, f32[32,8,128]{2,1,0:T(8,128)S(1)}, f32[32,8,128]{2,1,0:T(8,128)S(1)}, f32[48,128]{1,0:T(8,128)S(1)}, f32[128,128]{1,0:T(8,128)S(1)}) custom-call(s32[4,4]{1,0:T(4,128)S(1)} %copy-done.6, s32[4,4]{1,0:T(4,128)S(1)} %copy-done.7, f32[1536,128]{1,0:T(8,128)S(1)} %bitcast.12, ...), custom_call_target="tpu_custom_call" | custom-call | tf_op jit(solution)/shard_map/middle_kernel/pallas_call | solution.py:437
  41.9 1.7 %inner_kernel.1.taken_ref = f32[3,32,8,128]{3,2,1,0:T(8,128)S(1)} custom-call(f32[3,32,8,128]{3,2,1,0:T(8,128)S(1)} %get-tuple-element.26.lam_ref, f32[32,8,128]{2,1,0:T(8,128)S(1)} %get-tuple-element.20.wet_ref, f32[32,8,128]{2,1,0:T(8,128)S(1)} %get-tuple-element.21.mixing_ref, f32[32,8,128]{2,1,0:T(8,128)S(1)} %get-tuple-element.27.stay_ref, ...), custom_call_target="tpu_custom_call" | custom-call | tf_op jit(solution)/shard_map/inner_kernel/pallas_call | solution.py:437
  43.6 0.7 collective-permute-start.7
  44.3 3.5 %collective-permute-start.6 = (f32[3,32,8,128]{3,2,1,0:T(8,128)S(1)}, f32[3,32,8,128]{3,2,1,0:T(8,128)S(1)}, u32[]{:S(2)}, u32[]{:S(2)}) collective-permute-start(f32[3,32,8,128]{3,2,1,0:T(8,128)S(1)} %inner_kernel.1.taken_ref), channel_id=1, source_target_pairs={{0,1},{1,0},{2,3},{3,2},{4,5},{5,4},{6,7},{7,6},{8,9},{9,8},{10,11... | collective-permute-start | bytes 1179656 | tf_op jit(solution)/shard_map/ppermute | solution.py:484
  47.7 0.7 collective-permute-start.5
  48.4 2.9 %collective-permute-start.4 = (f32[48,128]{1,0:T(8,128)S(1)}, f32[48,128]{1,0:T(8,128)S(1)}, u32[]{:S(2)}, u32[]{:S(2)}) collective-permute-start(f32[48,128]{1,0:T(8,128)S(1)} %get-tuple-element.24.edge_ref), channel_id=1, source_target_pairs={{0,1},{1,0},{2,3},{3,2},{4,5},{5,4},{6,7},{7,6},{8,9},{9,8},{10,11... | collective-permute-start | bytes 73736 | tf_op jit(solution)/shard_map/ppermute | solution.py:481
  51.3 0.0 collective-permute-done.5.edge_b
  51.3 6.3 %collective-permute-done.4.edge_a = f32[48,128]{1,0:T(8,128)S(1)} collective-permute-done((f32[48,128]{1,0:T(8,128)S(1)}, f32[48,128]{1,0:T(8,128)S(1)}, u32[]{:S(2)}, u32[]{:S(2)}) %collective-permute-start.4) | collective-permute-done | bytes 24608 | tf_op jit(solution)/shard_map/ppermute | solution.py:481
  57.6 0.0 copy-start.2
  57.6 10.1 %all-gather.1 = f32[24,48,128]{2,1,0:T(8,128)S(1)} all-gather(f32[3,48,128]{2,1,0:T(8,128)S(1)} %pad_maximum_fusion.1), channel_id=3, replica_groups=mesh['tiles'=8,'slab'=4] {'tiles'}, dimensions={0}, use_global_device_ids=true | all-gather | bytes 663552 | tf_op jit(solution)/shard_map/all_gather | solution.py:486
  67.7 0.0 collective-permute-done.7.from_b
  67.7 0.0 collective-permute-done.6.from_a
  67.7 0.0 copy-start.8
  67.8 0.0 copy-done.2
  67.8 0.6 copy-done.8
  68.4 3.9 %close_kernel.1 = (f32[1,3,4,8100]{3,2,1,0:T(4,128)}, f32[8,8,128]{2,1,0:T(8,128)S(1)}) custom-call(s32[4,4]{1,0:T(4,128)S(1)} %copy-done.6, s32[4,4]{1,0:T(4,128)S(1)} %copy-done.7, s32[32]{0:T(128)S(1)} %copy-done.8, f32[1152,128]{1,0:T(8,128)S(1)} %bitcast.13, f32[320,128]{1,0:T(8,128)S(1)} %get-tuple-element.17.pack_a, ...), custom_call_target="tpu_custom_call" | custom-call | tf_op jit(solution)/shard_map/close_kernel/pallas_call | solution.py:437
  72.3 7.4 %all_to_all.5 = f32[8,8,128]{2,1,0:T(8,128)S(1)} all-to-all(f32[8,8,128]{2,1,0:T(8,128)S(1)} %get-tuple-element.31), channel_id=1, replica_groups=mesh['tiles'=8,'slab'=4] {'tiles'}, dimensions={0} | all-to-all | bytes 65536 | tf_op jit(solution)/shard_map/all_to_all | solution.py:497
  79.7 0.6 slice.18
  (6 shorter events, 0.0 us)
Async XLA Ops:
  0.6 1.0 %copy-start = (f32[1,3,4,8100]{3,2,1,0:T(4,128)S(1)}, f32[1,3,4,8100]{3,2,1,0:T(4,128)}, u32[]{:S(2)}) copy-start(f32[1,3,4,8100]{3,2,1,0:T(4,128)} %adjoint_ref.1) | copy-start | bytes 1166404
  1.6 0.9 %copy-start.3 = (f32[1,4,8100]{2,1,0:T(4,128)S(1)}, f32[1,4,8100]{2,1,0:T(4,128)}, u32[]{:S(2)}) copy-start(f32[1,4,8100]{2,1,0:T(4,128)} %weights_ref.1) | copy-start | bytes 388804
  2.5 0.9 %copy-start.4 = (f32[1,4,8100]{2,1,0:T(4,128)S(1)}, f32[1,4,8100]{2,1,0:T(4,128)}, u32[]{:S(2)}) copy-start(f32[1,4,8100]{2,1,0:T(4,128)} %vertical_ref.1) | copy-start | bytes 388804
  3.4 0.9 %copy-start.5 = (s32[1,4,8100]{2,1,0:T(4,128)S(1)}, s32[1,4,8100]{2,1,0:T(4,128)}, u32[]{:S(2)}) copy-start(s32[1,4,8100]{2,1,0:T(4,128)} %mask_ref.1) | copy-start | bytes 388804
  4.3 1.2 %copy-start.1 = (f32[3,4,8100]{2,1,0:T(4,128)S(1)}, f32[3,4,8100]{2,1,0:T(4,128)}, u32[]{:S(2)}) copy-start(f32[3,4,8100]{2,1,0:T(4,128)} %rate_ref.1) | copy-start | bytes 1166404
  7.4 29.4 %collective-permute-start.3 = (f32[3,32,8,128]{3,2,1,0:T(8,128)S(1)}, f32[3,32,8,128]{3,2,1,0:T(8,128)S(1)}, u32[]{:S(2)}, u32[]{:S(2)}) collective-permute-start(f32[3,32,8,128]{3,2,1,0:T(8,128)S(1)} %get-tuple-element.22.taken_ref), channel_id=1, source_target_pairs={{1,2},{2,1},{5,6},{6,5},{9,10},{10,9},{13,14},{14,13},{17,18},{18,... | collective-permute-start | bytes 1179656 | tf_op jit(solution)/shard_map/ppermute | solution.py:471
  8.1 28.7 %collective-permute-start.2 = (f32[3,32,8,128]{3,2,1,0:T(8,128)S(1)}, f32[3,32,8,128]{3,2,1,0:T(8,128)S(1)}, u32[]{:S(2)}, u32[]{:S(2)}) collective-permute-start(f32[3,32,8,128]{3,2,1,0:T(8,128)S(1)} %get-tuple-element.22.taken_ref), channel_id=1, source_target_pairs={{0,1},{1,0},{2,3},{3,2},{4,5},{5,4},{6,7},{7,6},{8,9},{9,8},{10,11... | collective-permute-start | bytes 1179656 | tf_op jit(solution)/shard_map/ppermute | solution.py:470
  14.0 2.5 %collective-permute-start.1 = (f32[320,128]{1,0:T(8,128)S(1)}, f32[320,128]{1,0:T(8,128)S(1)}, u32[]{:S(2)}, u32[]{:S(2)}) collective-permute-start(f32[320,128]{1,0:T(8,128)S(1)} %get-tuple-element.18.pack_b), channel_id=1, source_target_pairs={{1,2},{2,1},{5,6},{6,5},{9,10},{10,9},{13,14},{14,13},{17,18},{18,... | collective-permute-start | bytes 491528 | tf_op jit(solution)/shard_map/ppermute | solution.py:465
  14.7 11.7 %collective-permute-start = (f32[320,128]{1,0:T(8,128)S(1)}, f32[320,128]{1,0:T(8,128)S(1)}, u32[]{:S(2)}, u32[]{:S(2)}) collective-permute-start(f32[320,128]{1,0:T(8,128)S(1)} %get-tuple-element.17.pack_a), channel_id=1, source_target_pairs={{0,1},{1,0},{2,3},{3,2},{4,5},{5,4},{6,7},{7,6},{8,9},{9,8},{10,11... | collective-permute-start | bytes 491528 | tf_op jit(solution)/shard_map/ppermute | solution.py:464
  26.4 10.4 %copy-start.7 = (s32[4,4]{1,0:T(4,128)S(1)}, s32[4,4]{1,0:T(4,128)}, u32[]{:S(2)}) copy-start(s32[4,4]{1,0:T(4,128)} %link_ref.3) | copy-start | bytes 196
  36.8 0.7 copy-start.6
  43.6 24.2 %collective-permute-start.7 = (f32[3,32,8,128]{3,2,1,0:T(8,128)S(1)}, f32[3,32,8,128]{3,2,1,0:T(8,128)S(1)}, u32[]{:S(2)}, u32[]{:S(2)}) collective-permute-start(f32[3,32,8,128]{3,2,1,0:T(8,128)S(1)} %inner_kernel.1.taken_ref), channel_id=1, source_target_pairs={{1,2},{2,1},{5,6},{6,5},{9,10},{10,9},{13,14},{14,13},{17,18},{18,... | collective-permute-start | bytes 1179656 | tf_op jit(solution)/shard_map/ppermute | solution.py:485
  44.3 23.5 %collective-permute-start.6 = (f32[3,32,8,128]{3,2,1,0:T(8,128)S(1)}, f32[3,32,8,128]{3,2,1,0:T(8,128)S(1)}, u32[]{:S(2)}, u32[]{:S(2)}) collective-permute-start(f32[3,32,8,128]{3,2,1,0:T(8,128)S(1)} %inner_kernel.1.taken_ref), channel_id=1, source_target_pairs={{0,1},{1,0},{2,3},{3,2},{4,5},{5,4},{6,7},{7,6},{8,9},{9,8},{10,11... | collective-permute-start | bytes 1179656 | tf_op jit(solution)/shard_map/ppermute | solution.py:484
  47.7 3.6 %collective-permute-start.5 = (f32[48,128]{1,0:T(8,128)S(1)}, f32[48,128]{1,0:T(8,128)S(1)}, u32[]{:S(2)}, u32[]{:S(2)}) collective-permute-start(f32[48,128]{1,0:T(8,128)S(1)} %get-tuple-element.24.edge_ref), channel_id=1, source_target_pairs={{1,2},{2,1},{5,6},{6,5},{9,10},{10,9},{13,14},{14,13},{17,18},{18,... | collective-permute-start | bytes 73736 | tf_op jit(solution)/shard_map/ppermute | solution.py:482
  48.4 9.2 %collective-permute-start.4 = (f32[48,128]{1,0:T(8,128)S(1)}, f32[48,128]{1,0:T(8,128)S(1)}, u32[]{:S(2)}, u32[]{:S(2)}) collective-permute-start(f32[48,128]{1,0:T(8,128)S(1)} %get-tuple-element.24.edge_ref), channel_id=1, source_target_pairs={{0,1},{1,0},{2,3},{3,2},{4,5},{5,4},{6,7},{7,6},{8,9},{9,8},{10,11... | collective-permute-start | bytes 73736 | tf_op jit(solution)/shard_map/ppermute | solution.py:481
  57.6 10.1 %copy-start.2 = (f32[1,3,4,8100]{3,2,1,0:T(4,128)S(1)}, f32[1,3,4,8100]{3,2,1,0:T(4,128)}, u32[]{:S(2)}) copy-start(f32[1,3,4,8100]{3,2,1,0:T(4,128)} %state_ref.1) | copy-start | bytes 1166404
  67.7 0.7 copy-start.8

commit v2 on v1

v2 whole, which is shorter than its diff:
```python
import functools

import jax
import jax.numpy as jnp
from jax import lax
from jax.experimental import pallas as pl
from jax.experimental.pallas import tpu as pltpu
from jax.sharding import PartitionSpec as P

TILE = 90
CELLS = TILE * TILE
SUBSTEPS = 2
BLOCK = 6
COARSE = 15
LANES = 128
COLS = 32
HALF = COLS * LANES
TILES = 4
SIDES = 4
SPOTS = TILES * SIDES
FIRST_HIGH = HALF // TILE
UNROLL = 8
F32 = jnp.float32
I32 = jnp.int32


def position():
    lane = lax.broadcasted_iota(I32, (8, LANES), 1)
    low = lax.broadcasted_iota(I32, (8, LANES), 0) < TILES
    return lane, low


def cell_at(lane, low, v):
    cell = lane + jnp.where(low, 0, HALF) + v * LANES
    y = (cell * 46604) >> 22
    return cell - y * TILE, y


def lane_gather(values, index):
    return jnp.take_along_axis(values, index, axis=1, mode="promise_in_bounds")


def loop(body, carry=0):
    return lax.fori_loop(0, COLS, body, carry, unroll=UNROLL)


def fold(read, write):
    for v in range(COLS):
        write(v, 0, read(v * LANES, LANES))
        start = HALF + v * LANES
        width = min(LANES, CELLS - start)
        part = read(start, width)
        if width < LANES:
            part = jnp.concatenate([part, jnp.zeros((TILES, LANES - width), F32)], axis=1)
        write(v, TILES, part)


def set_guards(ref, plane, low):
    first, last = ref[plane, 1], ref[plane, COLS]
    ref[plane, 0] = jnp.where(low, 0.0, pltpu.roll(last, TILES, 0))
    ref[plane, COLS + 1] = jnp.where(low, pltpu.roll(first, TILES, 0), 0.0)


def inner_sum(ref, plane, v, lane, west, east):
    before, here, after = ref[plane, v], ref[plane, v + 1], ref[plane, v + 2]
    left = pltpu.roll(jnp.where(lane < LANES - 1, here, before), 1, 1)
    right = pltpu.roll(jnp.where(lane >= 1, here, after), LANES - 1, 1)
    up = pltpu.roll(jnp.where(lane < LANES - TILE, here, before), TILE, 1)
    down = pltpu.roll(jnp.where(lane >= TILE, here, after), LANES - TILE, 1)
    return jnp.where(west, 0.0, left) + jnp.where(east, 0.0, right) + (up + down)


def edge_sides(load, planes, lane, low):
    step = lane & 63
    base = TILE * step + jnp.where(low, 0, FIRST_HIGH * TILE - HALF) + jnp.where(lane < 64, TILE - 1, TILE)
    index, column = base & (LANES - 1), base >> 7

    def body(v, found):
        hit = column == v
        return tuple(jnp.where(hit, lane_gather(load(p, v), index), found[p]) for p in range(planes))

    found = loop(body, tuple(jnp.zeros((8, LANES), F32) for _ in range(planes)))
    bottom = CELLS - TILE - HALF + lane
    edge = lane < TILE
    first_low = jnp.where(low, lane + 63, lane - FIRST_HIGH + 63) & (LANES - 1)
    last_low = jnp.where(low, lane, lane - FIRST_HIGH) & (LANES - 1)
    out = []
    for p in range(planes):
        top = load(p, 0)
        picked = jnp.where(
            (bottom >> 7) == COLS - 2,
            lane_gather(load(p, COLS - 2), bottom & (LANES - 1)),
            lane_gather(load(p, COLS - 1), bottom & (LANES - 1)),
        )
        west, east = lane_gather(found[p], first_low), lane_gather(found[p], last_low)
        west = jnp.where(low, jnp.where(lane == 0, top, west), west)
        west_low, east_low = west[:TILES], east[:TILES]
        here = lane[:TILES]
        west = jnp.where(here <= FIRST_HIGH, west_low, west[TILES:])
        east = jnp.where(here < FIRST_HIGH, east_low, east[TILES:])
        inside = here < TILE
        out.append(
            [
                jnp.where(inside, top[:TILES], 0.0),
                jnp.where(inside, picked[TILES:], 0.0),
                jnp.where(inside, west, 0.0),
                jnp.where(inside, east, 0.0),
            ]
        )
    return out


def put_sides(ref, start, sides):
    for s in range(SIDES):
        ref[pl.ds(start + s, TILES, stride=SIDES), :] = sides[s]


def halos(near_ref, link_ref, all_ref, rows, channels, out_ref):
    me = lax.axis_index("tiles")
    chip, core = me // 2, me % 2
    sub = lax.broadcasted_iota(I32, (SPOTS, LANES), 0)
    lane = lax.broadcasted_iota(I32, (SPOTS, LANES), 1)
    turned = jnp.zeros((SPOTS, LANES), I32)
    closed = jnp.zeros((SPOTS, LANES), I32)
    for t in range(TILES):
        for s in range(SIDES):
            spot = t * SIDES + s
            near, link = near_ref[t, s], link_ref[t, s]
            tile = jnp.where(near < 0, me * TILES, near)
            device = tile // TILES
            step = device // 2 - chip
            place = jnp.where(step == 0, 0, jnp.where((step == 1) == (chip % 2 == 0), 2, 4))
            place = place + (device % 2 != core).astype(I32)
            row = place * rows + (tile % TILES) * SIDES + link // 2
            out_ref[pl.ds(spot, channels, stride=SPOTS), :] = all_ref[pl.ds(row, channels, stride=SPOTS), :]
            turned = jnp.where(sub == spot, link % 2, turned)
            closed = jnp.where(sub == spot, (near < 0).astype(I32), closed)
    back = jnp.clip(TILE - 1 - lane, 0, LANES - 1)
    for k in range(channels):
        for h in range(0, SPOTS, 8):
            at = pl.ds(k * SPOTS + h, 8)
            values = out_ref[at, :]
            values = jnp.where(turned[h : h + 8] == 1, lane_gather(values, back[h : h + 8]), values)
            out_ref[at, :] = jnp.where((closed[h : h + 8] == 1) | (lane[h : h + 8] >= TILE), 0.0, values)


def spot_rows(ref, index):
    return ref[pl.ds(index * SPOTS, SPOTS), :]


def change_planes(own_ref, first_ref, second_ref, fixed_ref, tracers, scratch, lane, low):
    mix_a = spot_rows(fixed_ref, tracers) * spot_rows(first_ref, tracers)
    mix_b = spot_rows(fixed_ref, tracers + 1) * spot_rows(second_ref, tracers)
    for c in range(tracers):
        own = spot_rows(own_ref, c)
        change = own + mix_a * (spot_rows(first_ref, c) - own) + mix_b * (spot_rows(second_ref, c) - own)
        scratch[pl.ds(c * SPOTS, SPOTS), :] = change
    out = []
    for c in range(tracers):
        sides = [scratch[pl.ds(c * SPOTS + s, TILES, stride=SIDES), :] for s in range(SIDES)]
        sides = [jnp.concatenate([side, side], axis=0) for side in sides]
        west = jnp.where(low, pltpu.roll(sides[2], 63, 1), pltpu.roll(sides[2], 63 - FIRST_HIGH, 1))
        east = jnp.where(low, sides[3], pltpu.roll(sides[3], LANES - FIRST_HIGH, 1))
        out.append([sides[0], sides[1], jnp.where(lane < 63, east, west)])
    return out


def add_columns(planes, v, lane, low):
    x, y = cell_at(lane, low, v)
    west, east = x == 0, x == TILE - 1
    index = (y + jnp.where(west, 63, 0) - jnp.where(low, 0, FIRST_HIGH)) & (LANES - 1)
    edge = west | east
    return [jnp.where(edge, lane_gather(sides[2], index), 0.0) for sides in planes]


def add_rows(ref, planes, lane, low):
    place = (CELLS - TILE - HALF) % LANES
    for c, sides in enumerate(planes):
        ref[c, 0] = ref[c, 0] + jnp.where(low, sides[0], 0.0)
        turned = pltpu.roll(sides[1], place, 1)
        ref[c, COLS - 2] = ref[c, COLS - 2] + jnp.where(low | (lane < place), 0.0, turned)
        ref[c, COLS - 1] = ref[c, COLS - 1] + jnp.where(low | (lane >= place + TILE - LANES), 0.0, turned)


def write_to(ref, *lead):
    def write(v, row, part):
        ref[(*lead, v, pl.ds(row, TILES), slice(None))] = part

    return write


def open_kernel(
    adjoint_hbm, weights_hbm, vertical_hbm, mask_hbm, rate_hbm,
    pack_a, pack_b, edge_ref, wet_ref, mixing_ref, stay_ref, keep_ref,
    adjoint_ref, weights_ref, vertical_ref, mask_ref, rate_ref, lam_ref, spread, sems,
):
    tracers = lam_ref.shape[0]
    copies = [
        pltpu.make_async_copy(source, target, sems.at[i])
        for i, (source, target) in enumerate(
            (
                (mask_hbm, mask_ref),
                (weights_hbm, weights_ref),
                (vertical_hbm, vertical_ref),
                (adjoint_hbm, adjoint_ref),
                (rate_hbm, rate_ref),
            )
        )
    ]
    for copy in copies:
        copy.start()
    even = lax.axis_index("slab") % 2 == 0
    lane, low = position()
    copies[0].wait()
    fold(lambda a, n: mask_ref[0, :, a : a + n].astype(F32), write_to(wet_ref))
    copies[1].wait()
    fold(lambda a, n: weights_ref[0, :, a : a + n], write_to(mixing_ref))
    copies[2].wait()
    fold(lambda a, n: vertical_ref[0, :, a : a + n], write_to(stay_ref))
    copies[3].wait()
    for c in range(tracers):
        fold(lambda a, n, c=c: adjoint_ref[0, c, :, a : a + n], write_to(lam_ref, c))

    def start(v, carry):
        wet = wet_ref[v]
        mixing = wet * mixing_ref[v]
        mixing_ref[v] = mixing
        for c in range(tracers):
            spread[c, v + 1] = mixing * lam_ref[c, v]
        spread[tracers, v + 1] = wet
        vertical = stay_ref[v]
        pack_a[tracers, v] = wet * jnp.where(even, 1.0, vertical)
        pack_b[tracers, v] = wet * jnp.where(even, vertical, 1.0)
        return carry

    loop(start)
    for c in range(tracers + 1):
        set_guards(spread, c, low)
    for p, sides in enumerate(edge_sides(lambda p, v: spread[p, v + 1], tracers + 1, lane, low)):
        put_sides(edge_ref, p * SPOTS, sides)
    copies[4].wait()
    for c in range(tracers):
        fold(lambda a, n, c=c: 1.0 - rate_ref[c, :, a : a + n], write_to(keep_ref, c))

    def body(v, carry):
        x, _ = cell_at(lane, low, v)
        west, east = x == 0, x == TILE - 1
        wet = wet_ref[v]
        stay = 1.0 - mixing_ref[v] * inner_sum(spread, tracers, v, lane, west, east)
        stay_ref[v] = stay
        for c in range(tracers):
            moved = inner_sum(spread, c, v, lane, west, east)
            taken = (lam_ref[c, v] * stay + wet * moved) * keep_ref[c, v]
            pack_a[c, v] = taken
            pack_b[c, v] = taken
        return carry

    loop(body)


def fixed_kernel(keep_ref, pack_a, pack_b, out_ref):
    tracers = keep_ref.shape[0]
    lane, low = position()

    def load(p, v):
        return keep_ref[p, v] if p < tracers else (pack_a if p == tracers else pack_b)[tracers, v]

    for p, sides in enumerate(edge_sides(load, tracers + 2, lane, low)):
        put_sides(out_ref, p * SPOTS, sides)


def halo_kernel(near_ref, link_ref, all_ref, edge_ref, fixed_ref, out_a, out_b, wet_ref, halo_ref):
    channels = edge_ref.shape[0] // SPOTS
    tracers = channels - 1
    halos(near_ref, link_ref, all_ref, channels * SPOTS, channels, halo_ref)
    wet, halo_wet = spot_rows(edge_ref, tracers), spot_rows(halo_ref, tracers)
    wet_ref[pl.ds(0, SPOTS), :] = halo_wet
    wet_ref[pl.ds(SPOTS, SPOTS), :] = wet
    add_halos(halo_ref, edge_ref, fixed_ref, wet, halo_wet, tracers, out_a, out_b)


def halo_again_kernel(near_ref, link_ref, all_ref, edge_ref, fixed_ref, wet_ref, out_a, out_b, halo_ref):
    tracers = edge_ref.shape[0] // SPOTS
    halos(near_ref, link_ref, all_ref, tracers * SPOTS, tracers, halo_ref)
    add_halos(halo_ref, edge_ref, fixed_ref, spot_rows(wet_ref, 1), spot_rows(wet_ref, 0), tracers, out_a, out_b)


def add_halos(halo_ref, edge_ref, fixed_ref, wet, halo_wet, tracers, out_a, out_b):
    for c in range(tracers):
        change = spot_rows(fixed_ref, c) * (wet * spot_rows(halo_ref, c) - spot_rows(edge_ref, c) * halo_wet)
        for out in (out_a, out_b):
            out[pl.ds(c * SPOTS, SPOTS), :] = change
    out_a[pl.ds(tracers * SPOTS, SPOTS), :] = spot_rows(fixed_ref, tracers)
    out_b[pl.ds(tracers * SPOTS, SPOTS), :] = spot_rows(fixed_ref, tracers + 1)


def middle_kernel(
    change_ref, change_a, change_b, fixed_ref, pack_a, pack_b, from_a, from_b, wet_ref, mixing_ref, stay_ref, keep_ref,
    out_ref, edge_ref, mix_a_ref, mix_b_ref, lam_ref, spread, scratch,
):
    tracers = lam_ref.shape[0]
    lane, low = position()
    planes = change_planes(change_ref, change_a, change_b, fixed_ref, tracers, scratch, lane, low)

    def body(v, carry):
        first, second = pack_a[tracers, v] * from_a[tracers, v], pack_b[tracers, v] * from_b[tracers, v]
        mix_a_ref[v] = first
        mix_b_ref[v] = second
        extra = add_columns(planes, v, lane, low)
        for c in range(tracers):
            taken = pack_a[c, v]
            lam_ref[c, v] = taken + first * (from_a[c, v] - taken) + second * (from_b[c, v] - taken) + extra[c]
        return carry

    loop(body)
    add_rows(lam_ref, planes, lane, low)

    def spreads(v, carry):
        for c in range(tracers):
            spread[c, v + 1] = mixing_ref[v] * lam_ref[c, v]
        return carry

    loop(spreads)
    for c in range(tracers):
        set_guards(spread, c, low)
    for p, sides in enumerate(edge_sides(lambda p, v: spread[p, v + 1], tracers, lane, low)):
        put_sides(edge_ref, p * SPOTS, sides)

    def inner(v, carry):
        x, _ = cell_at(lane, low, v)
        west, east = x == 0, x == TILE - 1
        wet, stay = wet_ref[v], stay_ref[v]
        for c in range(tracers):
            moved = inner_sum(spread, c, v, lane, west, east)
            out_ref[c, v] = (lam_ref[c, v] * stay + wet * moved) * keep_ref[c, v]
        return carry

    loop(inner)


def close_kernel(
    owner_ref, change_ref, change_a, change_b, fixed_ref, taken_ref, from_a, from_b, mix_a_ref, mix_b_ref, wet_ref,
    state_ref, out_hbm, part_ref, lam_ref, term_ref, rows_ref, sums_ref, flat_ref, scratch, sems,
):
    tracers = taken_ref.shape[0]
    lane, low = position()
    planes = change_planes(change_ref, change_a, change_b, fixed_ref, tracers, scratch, lane, low)
    for c in range(tracers):
        fold(lambda a, n, c=c: state_ref[0, c, :, a : a + n], write_to(term_ref, c))

    def body(v, carry):
        first, second = mix_a_ref[v], mix_b_ref[v]
        extra = add_columns(planes, v, lane, low)
        for c in range(tracers):
            taken = taken_ref[c, v]
            lam_ref[c, v] = taken + first * (from_a[c, v] - taken) + second * (from_b[c, v] - taken) + extra[c]
        return carry

    loop(body)
    add_rows(lam_ref, planes, lane, low)

    def terms(v, carry):
        for c in range(tracers):
            term_ref[c, v] = wet_ref[v] * lam_ref[c, v] * term_ref[c, v]
        return carry

    loop(terms)
    copies = []
    for c in range(tracers):
        for v in range(COLS):
            values = lam_ref[c, v]
            flat_ref[0, c, :, v * LANES : (v + 1) * LANES] = values[:TILES]
            start = HALF + v * LANES
            width = min(LANES, CELLS - start)
            flat_ref[0, c, :, start : start + width] = values[TILES:, :width]
        copies.append(pltpu.make_async_copy(flat_ref.at[0, c], out_hbm.at[0, c], sems.at[c]))
        copies[-1].start()
    for c in range(tracers):
        guard = pltpu.roll(term_ref[c, 0], TILES, 0)
        for block in range(COARSE):
            total = [None, None]
            for y in range(block * BLOCK, (block + 1) * BLOCK):
                half = y * TILE // HALF
                v, shift = divmod(y * TILE - half * HALF, LANES)
                values = term_ref[c, v]
                if shift + TILE > LANES:
                    after = term_ref[c, v + 1] if v + 1 < COLS else guard
                    values = jnp.where(lane >= shift, values, after)
                if shift:
                    values = pltpu.roll(values, LANES - shift, 1)
                total[half] = values if total[half] is None else total[half] + values
            parts = [total[h][h * TILES : (h + 1) * TILES] for h in range(2) if total[h] is not None]
            summed = parts[0] if len(parts) == 1 else parts[0] + parts[1]
            summed = jnp.where(lane[:TILES] < TILE, summed, 0.0)
            rows_ref[pl.ds((c * COARSE + block) * TILES, TILES), :] = summed
    lane_in = lax.broadcasted_iota(I32, (LANES, LANES), 0)
    lane_out = lax.broadcasted_iota(I32, (LANES, LANES), 1)
    low_edge = lane_out * BLOCK
    pick = ((lane_in >= low_edge) & (lane_in < low_edge + BLOCK) & (lane_out < COARSE)).astype(F32)
    sums_ref[...] = jnp.dot(rows_ref[...], pick, precision=lax.Precision.HIGHEST, preferred_element_type=F32)
    for spot in range(8):
        total = jnp.zeros((TILES, LANES), F32)
        for k in range(tracers * COARSE):
            start = k * COARSE - spot * LANES
            if start >= LANES or start + COARSE <= 0:
                continue
            values = sums_ref[pl.ds(k * TILES, TILES), :]
            values = pltpu.roll(values, start % LANES, 1) if start % LANES else values
            if start < 0:
                values = jnp.where(lane[:TILES] < start + COARSE, values, 0.0)
            elif start + COARSE > LANES:
                values = jnp.where(lane[:TILES] >= start, values, 0.0)
            total = total + values
        rows_ref[pl.ds(spot, TILES, stride=8), :] = total
    part_ref[...] = jnp.zeros_like(part_ref)
    me = lax.axis_index("tiles")
    for t in range(TILES):
        owner = owner_ref[me * TILES + t]
        part_ref[owner] = part_ref[owner] + rows_ref[pl.ds(t * 8, 8), :]
    for copy in copies:
        copy.wait()


def swaps(count, width=1):
    found = []
    for first in (0, 1):
        found.append(
            [
                pair
                for i in range(first, count // width - 1, 2)
                for k in range(width)
                for pair in ((i * width + k, (i + 1) * width + k), ((i + 1) * width + k, i * width + k))
            ]
        )
    return found


VMEM, SMEM, HBM = (pl.BlockSpec(memory_space=space) for space in (pltpu.VMEM, pltpu.SMEM, pltpu.HBM))


def call(kernel, ins, out, scratch, outs=None):
    return pl.pallas_call(
        kernel,
        out_shape=[jax.ShapeDtypeStruct(shape, F32) for shape in out],
        in_specs=ins,
        out_specs=outs or [VMEM] * len(out),
        scratch_shapes=[pltpu.VMEM(shape, F32) if isinstance(shape, tuple) else shape for shape in scratch],
        compiler_params=pltpu.CompilerParams(vmem_limit_bytes=32 * 1024 * 1024),
        name=kernel.__name__,
    )


def shards(adjoint, state, weights, vertical, mask, rate, neighbours, links, owners):
    tracers = adjoint.shape[1]
    number = lax.axis_size("tiles")
    even_swap, odd_swap = swaps(lax.axis_size("slab"))
    core_swap = swaps(2)[0]
    core_swap = [(2 * i + a, 2 * i + b) for i in range(number // 2) for a, b in core_swap]
    even_chips, odd_chips = swaps(number, 2)
    plane = (COLS, 8, LANES)
    planes = (tracers, *plane)
    pack = (tracers + 1, *plane)
    guarded = (COLS + 2, 8, LANES)
    rows = tracers * SPOTS

    def around(edge):
        both = jnp.concatenate([edge, lax.ppermute(edge, "tiles", core_swap)])
        return jnp.concatenate(
            [both, lax.ppermute(both, "tiles", even_chips), lax.ppermute(both, "tiles", odd_chips)]
        )

    def across(first, second):
        return lax.ppermute(first, "slab", even_swap), lax.ppermute(second, "slab", odd_swap)

    pack_a, pack_b, edge, wet, mixing, stay, keep = call(
        open_kernel,
        [HBM] * 5,
        [pack, pack, (rows + SPOTS, LANES), plane, plane, plane, planes],
        [adjoint.shape, weights.shape, vertical.shape, pltpu.VMEM(mask.shape, I32), rate.shape, planes]
        + [(tracers + 1, *guarded), pltpu.SemaphoreType.DMA((5,))],
    )(*(pltpu.with_memory_space_constraint(x, pltpu.HBM) for x in (adjoint, weights, vertical, mask, rate)))
    from_a, from_b = across(pack_a, pack_b)
    near = around(edge)
    (fixed,) = call(fixed_kernel, [VMEM] * 3, [((tracers + 2) * SPOTS, LANES)], [])(keep, pack_a, pack_b)
    change_a, change_b, edge_wet = call(
        halo_kernel,
        [SMEM] * 2 + [VMEM] * 3,
        [(rows + SPOTS, LANES)] * 2 + [(2 * SPOTS, LANES)],
        [(rows + SPOTS, LANES)],
    )(neighbours, links, near, edge, fixed)
    got_a, got_b = across(change_a, change_b)
    taken, edge, mix_a, mix_b = call(
        middle_kernel,
        [VMEM] * 12,
        [planes, (rows, LANES), plane, plane],
        [planes, (tracers, *guarded), (rows, LANES)],
    )(change_a, got_a, got_b, fixed, pack_a, pack_b, from_a, from_b, wet, mixing, stay, keep)
    from_a, from_b = across(taken, taken)
    near = around(edge)
    change_a, change_b = call(
        halo_again_kernel, [SMEM] * 2 + [VMEM] * 4, [(rows + SPOTS, LANES)] * 2, [(rows, LANES)]
    )(neighbours, links, near, edge, fixed, edge_wet)
    got_a, got_b = across(change_a, change_b)
    sums = (tracers * COARSE * TILES + 4, LANES)
    out, part = call(
        close_kernel,
        [SMEM] + [VMEM] * 11,
        [adjoint.shape, (number, 8, LANES)],
        [planes, planes, sums, sums, adjoint.shape, (rows, LANES), pltpu.SemaphoreType.DMA((tracers,))],
        [HBM, VMEM],
    )(owners, change_a, got_a, got_b, fixed, taken, from_a, from_b, mix_a, mix_b, wet, state)
    part = lax.all_to_all(part, "tiles", 0, 0, tiled=True)
    gradient = part.sum(axis=0).reshape(1, 1, 8 * LANES)[:, :, : tracers * COARSE * COARSE]
    return out, gradient


def solution(mesh):
    placed = (
        P("slab", None, "tiles", None),
        P("slab", None, "tiles", None),
        P("slab", "tiles", None),
        P("slab", "tiles", None),
        P("slab", "tiles", None),
        P(None, "tiles", None),
        P("tiles", None),
        P("tiles", None),
        P(),
    )
    return jax.shard_map(
        shards,
        mesh=mesh,
        in_specs=placed,
        out_specs=(P("slab", None, "tiles", None), P("slab", "tiles", None)),
        check_vma=False,
    )
```

time: 80.7 us -> 59.8 us (0.74)
  blocking collectives: 27.9 us -> 7.41 us
  starting transfers between devices: 16.7 us -> 27.5 us
  local copies, waits for them, and re-layouts: 5.63 us -> 1.26 us
  waiting for transfers between devices: 16.2 us -> 12.5 us
  Pallas kernels: 13.1 us -> 9.97 us
    all_gather x2 -> x0, blocking collectives: 20.5 us -> none  [the longest x1 10.4 us: shards(): lax.all_gather(jnp.stack([pack_a[:head], got_a[:head], got_b[:head]]), 't...]
    ppermute x8 -> x14, starting transfers between devices: 16.7 us -> 27.5 us  [the longest x4 15.5 us: across(): lax.ppermute(first, 'slab', even_swap)]
    unnamed x18 -> x10, local copies, waits for them, and re-layouts: 5.03 us -> 0.67 us
    ppermute x8 -> x14, waiting for transfers between devices: 16.2 us -> 12.5 us  [the longest x2 5.6 us: around(): lax.ppermute(both, 'tiles', even_chips)]
    pallas_call x5 -> x6, Pallas kernels: 13.1 us -> 9.97 us  [the longest x1 2.82 us: shards(): call(open_kernel, [HBM] * 5, [pack, pack, (rows + SPOTS, LANES), plane, p...]
  transfers between devices with their start and end apart: 8 -> 14, of which waited for: 2 -> 6; matrix products, arithmetic and copies ran while one was open for 0% -> 0% of each run, Pallas kernels for 0% -> 4%
where the time goes in v2:
time: 59.8 us; the launch traced here: 59.5 us
  starting transfers between devices  27.5 us (46%)
  waiting for transfers between devices  12.5 us (21%)
  Pallas kernels  9.97 us (17%)
  blocking collectives  7.41 us (12%)
  local copies, waits for them, and re-layouts  1.26 us (2%)
  between operations  0.81 us (1%)
    ppermute x4, starting transfers between devices, across(): lax.ppermute(first, 'slab', even_swap)  15.5 us
    ppermute x2, starting transfers between devices, around(): lax.ppermute(both, 'tiles', even_chips)  7.85 us
    all_to_all x1, blocking collectives, shards(): part = lax.all_to_all(part, 'tiles', 0, 0, tiled=True)  7.41 us
    ppermute x2, waiting for transfers between devices, around(): lax.ppermute(both, 'tiles', even_chips)  5.6 us
    ppermute x4, waiting for transfers between devices, across(): lax.ppermute(first, 'slab', even_swap)  4.47 us
    pallas_call x1, Pallas kernels, shards(): call(open_kernel, [HBM] * 5, [pack, pack, (rows + SPOTS, LANES), plane, p...  2.82 us
    ppermute x4, starting transfers between devices, across(): lax.ppermute(second, 'slab', odd_swap)  2.81 us
    pallas_call x1, Pallas kernels, shards(): call(close_kernel, [SMEM] + [VMEM] * 11, [adjoint.shape, (number, 8, LANE...  2.65 us
  transfers between devices with their start and end apart: 14, of which 6 were waited for; matrix products, arithmetic and copies ran while one was open for 0% of the time, Pallas kernels for 4%

profile of v2, /device:TPU:0, one launch (start us, length us, event | category | flops | bytes accessed | tf_op | source)
XLA Modules:
  0.0 59.5 jit_solution(3559085580604168659)
XLA Ops:
  0.6 2.8 %open_kernel.1 = (f32[4,32,8,128]{3,2,1,0:T(8,128)S(1)}, f32[4,32,8,128]{3,2,1,0:T(8,128)S(1)}, f32[64,128]{1,0:T(8,128)S(1)}, f32[32,8,128]{2,1,0:T(8,128)S(1)}...) custom-call(f32[1,3,4,8100]{3,2,1,0:T(4,128)} %adjoint_hbm.1, ...), custom_call_target="tpu_custom_call" | custom-call | tf_op jit(solution)/shard_map/open_kernel/pallas_call | solution.py:475
  3.5 3.1 %collective-permute-start.5 = (f32[4,32,8,128]{3,2,1,0:T(8,128)S(1)}, f32[4,32,8,128]{3,2,1,0:T(8,128)S(1)}, u32[]{:S(2)}, u32[]{:S(2)}) collective-permute-start(f32[4,32,8,128]{3,2,1,0:T(8,128)S(1)} %get-tuple-element.22.pack_a), channel_id=1, source_target_pairs={{0,1},{1,0},{2,3},{3,2},{4,5},{5,4},{6,7},{7,6},{8,9},{9,8},{10,11... | collective-permute-start | bytes 1572872 | tf_op jit(solution)/shard_map/ppermute | solution.py:473
  6.5 0.7 %collective-permute-start.6 = (f32[4,32,8,128]{3,2,1,0:T(8,128)S(1)}, f32[4,32,8,128]{3,2,1,0:T(8,128)S(1)}, u32[]{:S(2)}, u32[]{:S(2)}) collective-permute-start(f32[4,32,8,128]{3,2,1,0:T(8,128)S(1)} %get-tuple-element.23.pack_b), channel_id=1, source_target_pairs={{1,2},{2,1},{5,6},{6,5},{9,10},{10,9},{13,14},{14,13},{17,18},{18,... | collective-permute-start | bytes 1572872 | tf_op jit(solution)/shard_map/ppermute | solution.py:473
  7.2 0.1 collective-permute-start
  7.3 1.2 %collective-permute-done = f32[64,128]{1,0:T(8,128)S(1)} collective-permute-done((f32[64,128]{1,0:T(8,128)S(1)}, f32[64,128]{1,0:T(8,128)S(1)}, u32[]{:S(2)}, u32[]{:S(2)}) %collective-permute-start) | collective-permute-done | bytes 32800 | tf_op jit(solution)/shard_map/ppermute | solution.py:467
  8.5 0.7 %collective-permute-start.2 = (f32[128,128]{1,0:T(8,128)S(1)}, f32[128,128]{1,0:T(8,128)S(1)}, u32[]{:S(2)}, u32[]{:S(2)}) collective-permute-start(f32[128,128]{1,0:T(8,128)S(1)} %constant_dynamic-update-slice_fusion), channel_id=1, source_target_pairs={{8,16},{16,8},{12,20},{20,12},{9,17},{17,9},{13,21},{21,13},{10,18... | collective-permute-start | bytes 196616 | tf_op jit(solution)/shard_map/ppermute | solution.py:469
  9.2 4.3 %collective-permute-start.1 = (f32[128,128]{1,0:T(8,128)S(1)}, f32[128,128]{1,0:T(8,128)S(1)}, u32[]{:S(2)}, u32[]{:S(2)}) collective-permute-start(f32[128,128]{1,0:T(8,128)S(1)} %constant_dynamic-update-slice_fusion), channel_id=1, source_target_pairs={{0,8},{8,0},{4,12},{12,4},{16,24},{24,16},{20,28},{28,20},{1,9},{9... | collective-permute-start | bytes 196616 | tf_op jit(solution)/shard_map/ppermute | solution.py:469
  13.5 0.6 fixed_kernel.1.fixed_ref
  14.0 0.0 copy-start.1
  14.0 0.0 copy-start.2
  14.0 0.0 collective-permute-done.2
  14.1 2.9 %collective-permute-done.1 = f32[128,128]{1,0:T(8,128)S(1)} collective-permute-done((f32[128,128]{1,0:T(8,128)S(1)}, f32[128,128]{1,0:T(8,128)S(1)}, u32[]{:S(2)}, u32[]{:S(2)}) %collective-permute-start.1) | collective-permute-done | bytes 65568 | tf_op jit(solution)/shard_map/ppermute | solution.py:469
  16.9 0.0 copy-done.1
  16.9 0.0 copy-done.2
  17.0 1.1 %halo_kernel.1 = (f32[64,128]{1,0:T(8,128)S(1)}, f32[64,128]{1,0:T(8,128)S(1)}, f32[32,128]{1,0:T(8,128)S(1)}) custom-call(s32[4,4]{1,0:T(4,128)S(1)} %copy-done.1, s32[4,4]{1,0:T(4,128)S(1)} %copy-done.2, f32[384,128]{1,0:T(8,128)S(1)} %pad_maximum_fusion.all_ref, f32[64,128]{1,0:T(8,128)S(1)} %get-tuple-element.20.edge_ref, ...), custom_call_target="tpu_custom_call" | custom-call | tf_op jit(solution)/shard_map/halo_kernel/pallas_call | solution.py:485
  18.0 0.7 %collective-permute-start.4 = (f32[64,128]{1,0:T(8,128)S(1)}, f32[64,128]{1,0:T(8,128)S(1)}, u32[]{:S(2)}, u32[]{:S(2)}) collective-permute-start(f32[64,128]{1,0:T(8,128)S(1)} %get-tuple-element.25), channel_id=1, source_target_pairs={{1,2},{2,1},{5,6},{6,5},{9,10},{10,9},{13,14},{14,13},{17,18},{18,... | collective-permute-start | bytes 98312 | tf_op jit(solution)/shard_map/ppermute | solution.py:473
  18.7 5.7 %collective-permute-start.3 = (f32[64,128]{1,0:T(8,128)S(1)}, f32[64,128]{1,0:T(8,128)S(1)}, u32[]{:S(2)}, u32[]{:S(2)}) collective-permute-start(f32[64,128]{1,0:T(8,128)S(1)} %get-tuple-element.24.change_ref), channel_id=1, source_target_pairs={{0,1},{1,0},{2,3},{3,2},{4,5},{5,4},{6,7},{7,6},{8,9},{9,8},{10,11... | collective-permute-start | bytes 98312 | tf_op jit(solution)/shard_map/ppermute | solution.py:473
  24.4 0.0 collective-permute-done.4.change_b
  24.4 1.9 %collective-permute-done.3.change_a = f32[64,128]{1,0:T(8,128)S(1)} collective-permute-done((f32[64,128]{1,0:T(8,128)S(1)}, f32[64,128]{1,0:T(8,128)S(1)}, u32[]{:S(2)}, u32[]{:S(2)}) %collective-permute-start.3) | collective-permute-done | bytes 32800 | tf_op jit(solution)/shard_map/ppermute | solution.py:473
  26.3 0.0 collective-permute-done.5.from_a
  26.3 0.0 collective-permute-done.6.from_b
  26.3 1.8 %middle_kernel.1 = (f32[3,32,8,128]{3,2,1,0:T(8,128)S(1)}, f32[48,128]{1,0:T(8,128)S(1)}, f32[32,8,128]{2,1,0:T(8,128)S(1)}, f32[32,8,128]{2,1,0:T(8,128)S(1)}) custom-call(f32[64,128]{1,0:T(8,128)S(1)} %get-tuple-element.24.change_ref, f32[64,128]{1,0:T(8,128)S(1)} %collective-permute-done.3.change_a, f32[64,128]{1,0:T(8,128)S(1)} %collective-permute-done.4.change_b, ...), custom_call_target="tpu_custom_call" | custom-call | tf_op jit(solution)/shard_map/middle_kernel/pallas_call | solution.py:492
  28.1 0.0 copy-start
  28.1 0.8 %collective-permute-start.13 = (f32[3,32,8,128]{3,2,1,0:T(8,128)S(1)}, f32[3,32,8,128]{3,2,1,0:T(8,128)S(1)}, u32[]{:S(2)}, u32[]{:S(2)}) collective-permute-start(f32[3,32,8,128]{3,2,1,0:T(8,128)S(1)} %get-tuple-element.33.taken_ref), channel_id=1, source_target_pairs={{1,2},{2,1},{5,6},{6,5},{9,10},{10,9},{13,14},{14,13},{17,18},{18,... | collective-permute-start | bytes 1179656 | tf_op jit(solution)/shard_map/ppermute | solution.py:473
  29.0 5.3 %collective-permute-start.12 = (f32[3,32,8,128]{3,2,1,0:T(8,128)S(1)}, f32[3,32,8,128]{3,2,1,0:T(8,128)S(1)}, u32[]{:S(2)}, u32[]{:S(2)}) collective-permute-start(f32[3,32,8,128]{3,2,1,0:T(8,128)S(1)} %get-tuple-element.33.taken_ref), channel_id=1, source_target_pairs={{0,1},{1,0},{2,3},{3,2},{4,5},{5,4},{6,7},{7,6},{8,9},{9,8},{10,11... | collective-permute-start | bytes 1179656 | tf_op jit(solution)/shard_map/ppermute | solution.py:473
  34.3 0.0 collective-permute-start.7
  34.3 1.2 %collective-permute-done.7 = f32[48,128]{1,0:T(8,128)S(1)} collective-permute-done((f32[48,128]{1,0:T(8,128)S(1)}, f32[48,128]{1,0:T(8,128)S(1)}, u32[]{:S(2)}, u32[]{:S(2)}) %collective-permute-start.7) | collective-permute-done | bytes 24608 | tf_op jit(solution)/shard_map/ppermute | solution.py:467
  35.5 0.7 %collective-permute-start.9 = (f32[96,128]{1,0:T(8,128)S(1)}, f32[96,128]{1,0:T(8,128)S(1)}, u32[]{:S(2)}, u32[]{:S(2)}) collective-permute-start(f32[96,128]{1,0:T(8,128)S(1)} %constant_dynamic-update-slice_fusion.2), channel_id=1, source_target_pairs={{8,16},{16,8},{12,20},{20,12},{9,17},{17,9},{13,21},{21,13},{10,18... | collective-permute-start | bytes 147464 | tf_op jit(solution)/shard_map/ppermute | solution.py:469
  36.1 3.6 %collective-permute-start.8 = (f32[96,128]{1,0:T(8,128)S(1)}, f32[96,128]{1,0:T(8,128)S(1)}, u32[]{:S(2)}, u32[]{:S(2)}) collective-permute-start(f32[96,128]{1,0:T(8,128)S(1)} %constant_dynamic-update-slice_fusion.2), channel_id=1, source_target_pairs={{0,8},{8,0},{4,12},{12,4},{16,24},{24,16},{20,28},{28,20},{1,9},{9... | collective-permute-start | bytes 147464 | tf_op jit(solution)/shard_map/ppermute | solution.py:469
  39.7 0.0 collective-permute-done.9
  39.7 2.7 %collective-permute-done.8 = f32[96,128]{1,0:T(8,128)S(1)} collective-permute-done((f32[96,128]{1,0:T(8,128)S(1)}, f32[96,128]{1,0:T(8,128)S(1)}, u32[]{:S(2)}, u32[]{:S(2)}) %collective-permute-start.8) | collective-permute-done | bytes 49184 | tf_op jit(solution)/shard_map/ppermute | solution.py:469
  42.5 1.1 %halo_again_kernel.1 = (f32[64,128]{1,0:T(8,128)S(1)}, f32[64,128]{1,0:T(8,128)S(1)}) custom-call(s32[4,4]{1,0:T(4,128)S(1)} %copy-done.1, s32[4,4]{1,0:T(4,128)S(1)} %copy-done.2, f32[288,128]{1,0:T(8,128)S(1)} %pad_maximum_fusion.1.all_ref, f32[48,128]{1,0:T(8,128)S(1)} %get-tuple-element.29.edge_ref, f32[80,128]{1,0:T(8,128)S(1)} %fixed_kernel.1.fixed_ref, ...), custom_call_target="tpu_custom_call" | custom-call | tf_op jit(solution)/shard_map/halo_again_kernel/pallas_call | solution.py:500
  43.5 0.7 %collective-permute-start.11 = (f32[64,128]{1,0:T(8,128)S(1)}, f32[64,128]{1,0:T(8,128)S(1)}, u32[]{:S(2)}, u32[]{:S(2)}) collective-permute-start(f32[64,128]{1,0:T(8,128)S(1)} %get-tuple-element.32), channel_id=1, source_target_pairs={{1,2},{2,1},{5,6},{6,5},{9,10},{10,9},{13,14},{14,13},{17,18},{18,... | collective-permute-start | bytes 98312 | tf_op jit(solution)/shard_map/ppermute | solution.py:473
  44.2 1.4 %collective-permute-start.10 = (f32[64,128]{1,0:T(8,128)S(1)}, f32[64,128]{1,0:T(8,128)S(1)}, u32[]{:S(2)}, u32[]{:S(2)}) collective-permute-start(f32[64,128]{1,0:T(8,128)S(1)} %get-tuple-element.31.change_ref), channel_id=1, source_target_pairs={{0,1},{1,0},{2,3},{3,2},{4,5},{5,4},{6,7},{7,6},{8,9},{9,8},{10,11... | collective-permute-start | bytes 98312 | tf_op jit(solution)/shard_map/ppermute | solution.py:473
  45.6 0.0 collective-permute-done.11.change_b
  45.6 2.6 %collective-permute-done.10.change_a = f32[64,128]{1,0:T(8,128)S(1)} collective-permute-done((f32[64,128]{1,0:T(8,128)S(1)}, f32[64,128]{1,0:T(8,128)S(1)}, u32[]{:S(2)}, u32[]{:S(2)}) %collective-permute-start.10) | collective-permute-done | bytes 32800 | tf_op jit(solution)/shard_map/ppermute | solution.py:473
  48.2 0.0 collective-permute-done.13.from_b
  48.2 0.0 collective-permute-done.12.from_a
  48.2 0.0 copy-start.3
  48.2 0.0 copy-done
  48.2 0.6 %copy-done.3 = s32[32]{0:T(128)S(1)} copy-done((s32[32]{0:T(128)S(1)}, s32[32]{0:T(128)}, u32[]{:S(2)}) %copy-start.3) | copy-done | bytes 152
  48.8 2.6 %close_kernel.1 = (f32[1,3,4,8100]{3,2,1,0:T(4,128)}, f32[8,8,128]{2,1,0:T(8,128)S(1)}) custom-call(s32[32]{0:T(128)S(1)} %copy-done.3, f32[64,128]{1,0:T(8,128)S(1)} %get-tuple-element.31.change_ref, f32[64,128]{1,0:T(8,128)S(1)} %collective-permute-done.10.change_a, f32[64,128]{1,0:T(8,128)S(1)} %collective-permute-done.11.change_b, ...), custom_call_target="tpu_custom_call" | custom-call | tf_op jit(solution)/shard_map/close_kernel/pallas_call | solution.py:505
  51.5 7.4 %all_to_all.5 = f32[8,8,128]{2,1,0:T(8,128)S(1)} all-to-all(f32[8,8,128]{2,1,0:T(8,128)S(1)} %get-tuple-element.37), channel_id=1, replica_groups=mesh['tiles'=8,'slab'=4] {'tiles'}, dimensions={0} | all-to-all | bytes 65536 | tf_op jit(solution)/shard_map/all_to_all | solution.py:512
  58.9 0.6 slice.4
  (7 shorter events, 0.0 us)
Async XLA Ops:
  3.5 22.8 %collective-permute-start.5 = (f32[4,32,8,128]{3,2,1,0:T(8,128)S(1)}, f32[4,32,8,128]{3,2,1,0:T(8,128)S(1)}, u32[]{:S(2)}, u32[]{:S(2)}) collective-permute-start(f32[4,32,8,128]{3,2,1,0:T(8,128)S(1)} %get-tuple-element.22.pack_a), channel_id=1, source_target_pairs={{0,1},{1,0},{2,3},{3,2},{4,5},{5,4},{6,7},{7,6},{8,9},{9,8},{10,11... | collective-permute-start | bytes 1572872 | tf_op jit(solution)/shard_map/ppermute | solution.py:473
  6.5 19.7 %collective-permute-start.6 = (f32[4,32,8,128]{3,2,1,0:T(8,128)S(1)}, f32[4,32,8,128]{3,2,1,0:T(8,128)S(1)}, u32[]{:S(2)}, u32[]{:S(2)}) collective-permute-start(f32[4,32,8,128]{3,2,1,0:T(8,128)S(1)} %get-tuple-element.23.pack_b), channel_id=1, source_target_pairs={{1,2},{2,1},{5,6},{6,5},{9,10},{10,9},{13,14},{14,13},{17,18},{18,... | collective-permute-start | bytes 1572872 | tf_op jit(solution)/shard_map/ppermute | solution.py:473
  7.2 1.3 %collective-permute-start = (f32[64,128]{1,0:T(8,128)S(1)}, f32[64,128]{1,0:T(8,128)S(1)}, u32[]{:S(2)}, u32[]{:S(2)}) collective-permute-start(f32[64,128]{1,0:T(8,128)S(1)} %get-tuple-element.20.edge_ref), channel_id=1, source_target_pairs={{0,4},{4,0},{8,12},{12,8},{16,20},{20,16},{24,28},{28,24},{1,5},{5... | collective-permute-start | bytes 98312 | tf_op jit(solution)/shard_map/ppermute | solution.py:467
  8.5 5.5 %collective-permute-start.2 = (f32[128,128]{1,0:T(8,128)S(1)}, f32[128,128]{1,0:T(8,128)S(1)}, u32[]{:S(2)}, u32[]{:S(2)}) collective-permute-start(f32[128,128]{1,0:T(8,128)S(1)} %constant_dynamic-update-slice_fusion), channel_id=1, source_target_pairs={{8,16},{16,8},{12,20},{20,12},{9,17},{17,9},{13,21},{21,13},{10,18... | collective-permute-start | bytes 196616 | tf_op jit(solution)/shard_map/ppermute | solution.py:469
  9.2 7.7 %collective-permute-start.1 = (f32[128,128]{1,0:T(8,128)S(1)}, f32[128,128]{1,0:T(8,128)S(1)}, u32[]{:S(2)}, u32[]{:S(2)}) collective-permute-start(f32[128,128]{1,0:T(8,128)S(1)} %constant_dynamic-update-slice_fusion), channel_id=1, source_target_pairs={{0,8},{8,0},{4,12},{12,4},{16,24},{24,16},{20,28},{28,20},{1,9},{9... | collective-permute-start | bytes 196616 | tf_op jit(solution)/shard_map/ppermute | solution.py:469
  14.0 2.9 %copy-start.1 = (s32[4,4]{1,0:T(4,128)S(1)}, s32[4,4]{1,0:T(4,128)}, u32[]{:S(2)}) copy-start(s32[4,4]{1,0:T(4,128)} %near_ref.3) | copy-start | bytes 196
  14.0 2.9 %copy-start.2 = (s32[4,4]{1,0:T(4,128)S(1)}, s32[4,4]{1,0:T(4,128)}, u32[]{:S(2)}) copy-start(s32[4,4]{1,0:T(4,128)} %link_ref.3) | copy-start | bytes 196
  18.0 6.4 %collective-permute-start.4 = (f32[64,128]{1,0:T(8,128)S(1)}, f32[64,128]{1,0:T(8,128)S(1)}, u32[]{:S(2)}, u32[]{:S(2)}) collective-permute-start(f32[64,128]{1,0:T(8,128)S(1)} %get-tuple-element.25), channel_id=1, source_target_pairs={{1,2},{2,1},{5,6},{6,5},{9,10},{10,9},{13,14},{14,13},{17,18},{18,... | collective-permute-start | bytes 98312 | tf_op jit(solution)/shard_map/ppermute | solution.py:473
  18.7 7.6 %collective-permute-start.3 = (f32[64,128]{1,0:T(8,128)S(1)}, f32[64,128]{1,0:T(8,128)S(1)}, u32[]{:S(2)}, u32[]{:S(2)}) collective-permute-start(f32[64,128]{1,0:T(8,128)S(1)} %get-tuple-element.24.change_ref), channel_id=1, source_target_pairs={{0,1},{1,0},{2,3},{3,2},{4,5},{5,4},{6,7},{7,6},{8,9},{9,8},{10,11... | collective-permute-start | bytes 98312 | tf_op jit(solution)/shard_map/ppermute | solution.py:473
  28.1 20.1 %copy-start = (f32[1,3,4,8100]{3,2,1,0:T(4,128)S(1)}, f32[1,3,4,8100]{3,2,1,0:T(4,128)}, u32[]{:S(2)}) copy-start(f32[1,3,4,8100]{3,2,1,0:T(4,128)} %state_ref.1) | copy-start | bytes 1166404
  28.1 20.0 %collective-permute-start.13 = (f32[3,32,8,128]{3,2,1,0:T(8,128)S(1)}, f32[3,32,8,128]{3,2,1,0:T(8,128)S(1)}, u32[]{:S(2)}, u32[]{:S(2)}) collective-permute-start(f32[3,32,8,128]{3,2,1,0:T(8,128)S(1)} %get-tuple-element.33.taken_ref), channel_id=1, source_target_pairs={{1,2},{2,1},{5,6},{6,5},{9,10},{10,9},{13,14},{14,13},{17,18},{18,... | collective-permute-start | bytes 1179656 | tf_op jit(solution)/shard_map/ppermute | solution.py:473
  29.0 19.2 %collective-permute-start.12 = (f32[3,32,8,128]{3,2,1,0:T(8,128)S(1)}, f32[3,32,8,128]{3,2,1,0:T(8,128)S(1)}, u32[]{:S(2)}, u32[]{:S(2)}) collective-permute-start(f32[3,32,8,128]{3,2,1,0:T(8,128)S(1)} %get-tuple-element.33.taken_ref), channel_id=1, source_target_pairs={{0,1},{1,0},{2,3},{3,2},{4,5},{5,4},{6,7},{7,6},{8,9},{9,8},{10,11... | collective-permute-start | bytes 1179656 | tf_op jit(solution)/shard_map/ppermute | solution.py:473
  34.3 1.2 %collective-permute-start.7 = (f32[48,128]{1,0:T(8,128)S(1)}, f32[48,128]{1,0:T(8,128)S(1)}, u32[]{:S(2)}, u32[]{:S(2)}) collective-permute-start(f32[48,128]{1,0:T(8,128)S(1)} %get-tuple-element.29.edge_ref), channel_id=1, source_target_pairs={{0,4},{4,0},{8,12},{12,8},{16,20},{20,16},{24,28},{28,24},{1,5},{5... | collective-permute-start | bytes 73736 | tf_op jit(solution)/shard_map/ppermute | solution.py:467
  35.5 4.2 %collective-permute-start.9 = (f32[96,128]{1,0:T(8,128)S(1)}, f32[96,128]{1,0:T(8,128)S(1)}, u32[]{:S(2)}, u32[]{:S(2)}) collective-permute-start(f32[96,128]{1,0:T(8,128)S(1)} %constant_dynamic-update-slice_fusion.2), channel_id=1, source_target_pairs={{8,16},{16,8},{12,20},{20,12},{9,17},{17,9},{13,21},{21,13},{10,18... | collective-permute-start | bytes 147464 | tf_op jit(solution)/shard_map/ppermute | solution.py:469
  36.1 6.3 %collective-permute-start.8 = (f32[96,128]{1,0:T(8,128)S(1)}, f32[96,128]{1,0:T(8,128)S(1)}, u32[]{:S(2)}, u32[]{:S(2)}) collective-permute-start(f32[96,128]{1,0:T(8,128)S(1)} %constant_dynamic-update-slice_fusion.2), channel_id=1, source_target_pairs={{0,8},{8,0},{4,12},{12,4},{16,24},{24,16},{20,28},{28,20},{1,9},{9... | collective-permute-start | bytes 147464 | tf_op jit(solution)/shard_map/ppermute | solution.py:469
  43.5 2.1 %collective-permute-start.11 = (f32[64,128]{1,0:T(8,128)S(1)}, f32[64,128]{1,0:T(8,128)S(1)}, u32[]{:S(2)}, u32[]{:S(2)}) collective-permute-start(f32[64,128]{1,0:T(8,128)S(1)} %get-tuple-element.32), channel_id=1, source_target_pairs={{1,2},{2,1},{5,6},{6,5},{9,10},{10,9},{13,14},{14,13},{17,18},{18,... | collective-permute-start | bytes 98312 | tf_op jit(solution)/shard_map/ppermute | solution.py:473
  44.2 4.0 %collective-permute-start.10 = (f32[64,128]{1,0:T(8,128)S(1)}, f32[64,128]{1,0:T(8,128)S(1)}, u32[]{:S(2)}, u32[]{:S(2)}) collective-permute-start(f32[64,128]{1,0:T(8,128)S(1)} %get-tuple-element.31.change_ref), channel_id=1, source_target_pairs={{0,1},{1,0},{2,3},{3,2},{4,5},{5,4},{6,7},{7,6},{8,9},{9,8},{10,11... | collective-permute-start | bytes 98312 | tf_op jit(solution)/shard_map/ppermute | solution.py:473
  48.2 0.7 %copy-start.3 = (s32[32]{0:T(128)S(1)}, s32[32]{0:T(128)}, u32[]{:S(2)}) copy-start(s32[32]{0:T(128)} %owner_ref.1) | copy-start | bytes 388

commit v3 on v2

v3 whole, which is shorter than its diff:
```python
import functools

import jax
import jax.numpy as jnp
from jax import lax
from jax.experimental import pallas as pl
from jax.experimental.pallas import tpu as pltpu
from jax.sharding import PartitionSpec as P

TILE = 90
CELLS = TILE * TILE
SUBSTEPS = 2
BLOCK = 6
COARSE = 15
LANES = 128
COLS = 32
HALF = COLS * LANES
TILES = 4
SIDES = 4
SPOTS = TILES * SIDES
CHANNELS = 4
ROWS = SPOTS * CHANNELS
SHOWN = ROWS + 2 * SIDES * CHANNELS
FIRST_HIGH = HALF // TILE
UNROLL = 8
F32 = jnp.float32
I32 = jnp.int32


def position():
    lane = lax.broadcasted_iota(I32, (8, LANES), 1)
    low = lax.broadcasted_iota(I32, (8, LANES), 0) < TILES
    return lane, low


def cell_at(lane, low, v):
    cell = lane + jnp.where(low, 0, HALF) + v * LANES
    y = (cell * 46604) >> 22
    return cell - y * TILE, y


def lane_gather(values, index):
    return jnp.take_along_axis(values, index, axis=1, mode="promise_in_bounds")


def loop(body, carry=0):
    return lax.fori_loop(0, COLS, body, carry, unroll=UNROLL)


def fold(read, write):
    for v in range(COLS):
        write(v, 0, read(v * LANES, LANES))
        start = HALF + v * LANES
        width = min(LANES, CELLS - start)
        part = read(start, width)
        if width < LANES:
            part = jnp.concatenate([part, jnp.zeros((TILES, LANES - width), F32)], axis=1)
        write(v, TILES, part)


def set_guards(ref, plane, low):
    first, last = ref[plane, 1], ref[plane, COLS]
    ref[plane, 0] = jnp.where(low, 0.0, pltpu.roll(last, TILES, 0))
    ref[plane, COLS + 1] = jnp.where(low, pltpu.roll(first, TILES, 0), 0.0)


def inner_sum(ref, plane, v, lane, west, east):
    before, here, after = ref[plane, v], ref[plane, v + 1], ref[plane, v + 2]
    left = pltpu.roll(jnp.where(lane < LANES - 1, here, before), 1, 1)
    right = pltpu.roll(jnp.where(lane >= 1, here, after), LANES - 1, 1)
    up = pltpu.roll(jnp.where(lane < LANES - TILE, here, before), TILE, 1)
    down = pltpu.roll(jnp.where(lane >= TILE, here, after), LANES - TILE, 1)
    return jnp.where(west, 0.0, left) + jnp.where(east, 0.0, right) + (up + down)


def edge_sides(load, planes, lane, low):
    step = lane & 63
    base = TILE * step + jnp.where(low, 0, FIRST_HIGH * TILE - HALF) + jnp.where(lane < 64, TILE - 1, TILE)
    index, column = base & (LANES - 1), base >> 7

    def body(v, found):
        hit = column == v
        return tuple(jnp.where(hit, lane_gather(load(p, v), index), found[p]) for p in range(planes))

    found = loop(body, tuple(jnp.zeros((8, LANES), F32) for _ in range(planes)))
    bottom = CELLS - TILE - HALF + lane
    edge = lane < TILE
    first_low = jnp.where(low, lane + 63, lane - FIRST_HIGH + 63) & (LANES - 1)
    last_low = jnp.where(low, lane, lane - FIRST_HIGH) & (LANES - 1)
    out = []
    for p in range(planes):
        top = load(p, 0)
        picked = jnp.where(
            (bottom >> 7) == COLS - 2,
            lane_gather(load(p, COLS - 2), bottom & (LANES - 1)),
            lane_gather(load(p, COLS - 1), bottom & (LANES - 1)),
        )
        west, east = lane_gather(found[p], first_low), lane_gather(found[p], last_low)
        west = jnp.where(low, jnp.where(lane == 0, top, west), west)
        west_low, east_low = west[:TILES], east[:TILES]
        here = lane[:TILES]
        west = jnp.where(here <= FIRST_HIGH, west_low, west[TILES:])
        east = jnp.where(here < FIRST_HIGH, east_low, east[TILES:])
        inside = here < TILE
        out.append(
            [
                jnp.where(inside, top[:TILES], 0.0),
                jnp.where(inside, picked[TILES:], 0.0),
                jnp.where(inside, west, 0.0),
                jnp.where(inside, east, 0.0),
            ]
        )
    return out


def put_sides(ref, channel, sides):
    for s in range(SIDES):
        ref[pl.ds(s * CHANNELS + channel, TILES, stride=SIDES * CHANNELS), :] = sides[s]


def channel_rows(ref, channel):
    return ref[pl.ds(channel, SPOTS, stride=CHANNELS), :]


def halos(near_ref, link_ref, all_ref, out_ref):
    me = lax.axis_index("tiles")
    chip, core = me // 2, me % 2
    even = chip % 2 == 0
    turned, closed = [], []
    for t in range(TILES):
        for s in range(SIDES):
            near, link = near_ref[t, s], link_ref[t, s]
            tile = jnp.where(near < 0, me * TILES, near)
            device = tile // TILES
            inner = tile % TILES
            step = device // 2 - chip
            place = jnp.where(step == 0, 0, jnp.where((step == 1) == even, 2 * SHOWN, SHOWN))
            far = jnp.where(inner == 0, ROWS, ROWS + SIDES * CHANNELS)
            row = place + jnp.where(device % 2 == core, inner * (SIDES * CHANNELS), far) + (link // 2) * CHANNELS
            out_ref[pl.ds((t * SIDES + s) * CHANNELS, CHANNELS), :] = all_ref[pl.ds(row, CHANNELS), :]
            turned.append(link % 2)
            closed.append((near < 0).astype(I32))
    lane, low = position()
    back = jnp.clip(TILE - 1 - lane, 0, LANES - 1)
    for k in range(0, SPOTS, 2):
        at = pl.ds(k * CHANNELS, 8)
        values = out_ref[at, :]
        values = jnp.where(jnp.where(low, turned[k], turned[k + 1]) == 1, lane_gather(values, back), values)
        shut = jnp.where(low, closed[k], closed[k + 1]) == 1
        out_ref[at, :] = jnp.where(shut | (lane >= TILE), 0.0, values)


def change_planes(own_a, own_b, got_a, got_b, tracers, scratch, lane, low):
    mix_a = channel_rows(own_a, tracers) * channel_rows(got_a, tracers)
    mix_b = channel_rows(own_b, tracers) * channel_rows(got_b, tracers)
    for c in range(tracers):
        own = channel_rows(own_a, c)
        scratch[pl.ds(c * SPOTS, SPOTS), :] = (
            own + mix_a * (channel_rows(got_a, c) - own) + mix_b * (channel_rows(got_b, c) - own)
        )
    out = []
    for c in range(tracers):
        sides = [scratch[pl.ds(c * SPOTS + s, TILES, stride=SIDES), :] for s in range(SIDES)]
        sides = [jnp.concatenate([side, side], axis=0) for side in sides]
        west = jnp.where(low, pltpu.roll(sides[2], 63, 1), pltpu.roll(sides[2], 63 - FIRST_HIGH, 1))
        east = jnp.where(low, sides[3], pltpu.roll(sides[3], LANES - FIRST_HIGH, 1))
        out.append([sides[0], sides[1], jnp.where(lane < 63, east, west)])
    return out


def add_columns(planes, v, lane, low):
    x, y = cell_at(lane, low, v)
    west, east = x == 0, x == TILE - 1
    index = (y + jnp.where(west, 63, 0) - jnp.where(low, 0, FIRST_HIGH)) & (LANES - 1)
    edge = west | east
    return [jnp.where(edge, lane_gather(sides[2], index), 0.0) for sides in planes]


def add_rows(ref, planes, lane, low):
    place = (CELLS - TILE - HALF) % LANES
    for c, sides in enumerate(planes):
        ref[c, 0] = ref[c, 0] + jnp.where(low, sides[0], 0.0)
        turned = pltpu.roll(sides[1], place, 1)
        ref[c, COLS - 2] = ref[c, COLS - 2] + jnp.where(low | (lane < place), 0.0, turned)
        ref[c, COLS - 1] = ref[c, COLS - 1] + jnp.where(low | (lane >= place + TILE - LANES), 0.0, turned)


def write_to(ref, *lead):
    def write(v, row, part):
        ref[(*lead, v, pl.ds(row, TILES), slice(None))] = part

    return write


def open_kernel(
    adjoint_hbm, weights_hbm, mask_hbm, near_hbm, link_hbm,
    edge_ref, lam_ref, wet_ref, mixing_ref, spread, near_ref, link_ref,
    adjoint_ref, weights_ref, mask_ref, sems,
):
    tracers = lam_ref.shape[0]
    pairs = (
        (mask_hbm, mask_ref),
        (weights_hbm, weights_ref),
        (adjoint_hbm, adjoint_ref),
        (near_hbm, near_ref),
        (link_hbm, link_ref),
    )
    copies = [pltpu.make_async_copy(source, target, sems.at[i]) for i, (source, target) in enumerate(pairs)]
    for copy in copies:
        copy.start()
    lane, low = position()
    copies[0].wait()
    fold(lambda a, n: mask_ref[0, :, a : a + n].astype(F32), write_to(wet_ref))
    copies[1].wait()
    fold(lambda a, n: weights_ref[0, :, a : a + n], write_to(mixing_ref))
    copies[2].wait()
    for c in range(tracers):
        fold(lambda a, n, c=c: adjoint_ref[0, c, :, a : a + n], write_to(lam_ref, c))

    def start(v, carry):
        wet = wet_ref[v]
        mixing = wet * mixing_ref[v]
        mixing_ref[v] = mixing
        for c in range(tracers):
            spread[c, v + 1] = mixing * lam_ref[c, v]
        spread[tracers, v + 1] = wet
        return carry

    loop(start)
    for c in range(tracers + 1):
        set_guards(spread, c, low)
    for p, sides in enumerate(edge_sides(lambda p, v: spread[p, v + 1], tracers + 1, lane, low)):
        put_sides(edge_ref, p, sides)
    copies[3].wait()
    copies[4].wait()


def inner_first_kernel(spread, lam_ref, wet_ref, mixing_ref, vertical_ref, rate_ref, pack_a, pack_b, stay_ref, keep_ref):
    tracers = lam_ref.shape[0]
    even = lax.axis_index("slab") % 2 == 0
    lane, low = position()
    fold(lambda a, n: vertical_ref[0, :, a : a + n], write_to(stay_ref))
    for c in range(tracers):
        fold(lambda a, n, c=c: 1.0 - rate_ref[c, :, a : a + n], write_to(keep_ref, c))

    def body(v, carry):
        x, _ = cell_at(lane, low, v)
        west, east = x == 0, x == TILE - 1
        wet, vertical = wet_ref[v], stay_ref[v]
        pack_a[tracers, v] = wet * jnp.where(even, 1.0, vertical)
        pack_b[tracers, v] = wet * jnp.where(even, vertical, 1.0)
        stay = 1.0 - mixing_ref[v] * inner_sum(spread, tracers, v, lane, west, east)
        stay_ref[v] = stay
        for c in range(tracers):
            moved = inner_sum(spread, c, v, lane, west, east)
            taken = (lam_ref[c, v] * stay + wet * moved) * keep_ref[c, v]
            pack_a[c, v] = taken
            pack_b[c, v] = taken
        return carry

    loop(body)


def inner_kernel(spread, lam_ref, wet_ref, stay_ref, keep_ref, out_ref):
    tracers = lam_ref.shape[0]
    lane, low = position()

    def body(v, carry):
        x, _ = cell_at(lane, low, v)
        west, east = x == 0, x == TILE - 1
        wet, stay = wet_ref[v], stay_ref[v]
        for c in range(tracers):
            moved = inner_sum(spread, c, v, lane, west, east)
            out_ref[c, v] = (lam_ref[c, v] * stay + wet * moved) * keep_ref[c, v]
        return carry

    loop(body)


def fixed_kernel(keep_ref, pack_a, pack_b, out_a, out_b):
    tracers = keep_ref.shape[0]
    lane, low = position()

    def load(p, v):
        return keep_ref[p, v] if p < tracers else (pack_a if p == tracers else pack_b)[tracers, v]

    found = edge_sides(load, tracers + 2, lane, low)
    for c in range(tracers):
        put_sides(out_a, c, found[c])
        put_sides(out_b, c, found[c])
    put_sides(out_a, tracers, found[tracers])
    put_sides(out_b, tracers, found[tracers + 1])


def halo_kernel(near_ref, link_ref, all_ref, edge_ref, fixed_a, fixed_b, out_a, out_b, halo_ref):
    tracers = CHANNELS - 1
    halos(near_ref, link_ref, all_ref, halo_ref)
    wet, halo_wet = channel_rows(edge_ref, tracers), channel_rows(halo_ref, tracers)
    for c in range(tracers):
        change = channel_rows(fixed_a, c) * (wet * channel_rows(halo_ref, c) - channel_rows(edge_ref, c) * halo_wet)
        for out in (out_a, out_b):
            out[pl.ds(c, SPOTS, stride=CHANNELS), :] = change
    out_a[pl.ds(tracers, SPOTS, stride=CHANNELS), :] = channel_rows(fixed_a, tracers)
    out_b[pl.ds(tracers, SPOTS, stride=CHANNELS), :] = channel_rows(fixed_b, tracers)


def mix_first_kernel(pack_a, pack_b, from_a, from_b, lam_ref, mix_a_ref, mix_b_ref):
    tracers = lam_ref.shape[0]

    def body(v, carry):
        first, second = pack_a[tracers, v] * from_a[tracers, v], pack_b[tracers, v] * from_b[tracers, v]
        mix_a_ref[v] = first
        mix_b_ref[v] = second
        for c in range(tracers):
            taken = pack_a[c, v]
            lam_ref[c, v] = taken + first * (from_a[c, v] - taken) + second * (from_b[c, v] - taken)
        return carry

    loop(body)


def mix_kernel(taken_ref, from_a, from_b, mix_a_ref, mix_b_ref, wet_ref, state_ref, lam_ref, term_ref):
    tracers = lam_ref.shape[0]
    for c in range(tracers):
        fold(lambda a, n, c=c: state_ref[0, c, :, a : a + n], write_to(term_ref, c))

    def body(v, carry):
        first, second, wet = mix_a_ref[v], mix_b_ref[v], wet_ref[v]
        for c in range(tracers):
            taken = taken_ref[c, v]
            lam_ref[c, v] = taken + first * (from_a[c, v] - taken) + second * (from_b[c, v] - taken)
            term_ref[c, v] = wet * term_ref[c, v]
        return carry

    loop(body)


def middle_kernel(
    change_a, change_b, got_a, got_b, before_ref, mixing_ref, wet_edge_ref, edge_ref, lam_ref, spread, scratch
):
    tracers = lam_ref.shape[0]
    lane, low = position()
    planes = change_planes(change_a, change_b, got_a, got_b, tracers, scratch, lane, low)

    def body(v, carry):
        extra = add_columns(planes, v, lane, low)
        mixing = mixing_ref[v]
        for c in range(tracers):
            lam = before_ref[c, v] + extra[c]
            lam_ref[c, v] = lam
            spread[c, v + 1] = mixing * lam
        return carry

    loop(body)
    add_rows(lam_ref, planes, lane, low)
    for c in range(tracers):
        for v in (0, COLS - 2, COLS - 1):
            spread[c, v + 1] = mixing_ref[v] * lam_ref[c, v]
        set_guards(spread, c, low)
    for p, sides in enumerate(edge_sides(lambda p, v: spread[p, v + 1], tracers, lane, low)):
        put_sides(edge_ref, p, sides)
    edge_ref[pl.ds(tracers, SPOTS, stride=CHANNELS), :] = channel_rows(wet_edge_ref, tracers)


def close_kernel(
    owner_hbm, change_a, change_b, got_a, got_b, before_ref, weighted_ref,
    out_hbm, part_ref, lam_ref, term_ref, rows_ref, sums_ref, flat_ref, scratch, owner_ref, sems,
):
    tracers = lam_ref.shape[0]
    owner_copy = pltpu.make_async_copy(owner_hbm, owner_ref, sems.at[tracers])
    owner_copy.start()
    lane, low = position()
    planes = change_planes(change_a, change_b, got_a, got_b, tracers, scratch, lane, low)

    def body(v, carry):
        extra = add_columns(planes, v, lane, low)
        for c in range(tracers):
            lam = before_ref[c, v] + extra[c]
            lam_ref[c, v] = lam
            term_ref[c, v] = weighted_ref[c, v] * lam
        return carry

    loop(body)
    add_rows(lam_ref, planes, lane, low)
    for c in range(tracers):
        for v in (0, COLS - 2, COLS - 1):
            term_ref[c, v] = weighted_ref[c, v] * lam_ref[c, v]
    copies = []
    for c in range(tracers):
        for v in range(COLS):
            values = lam_ref[c, v]
            flat_ref[0, c, :, v * LANES : (v + 1) * LANES] = values[:TILES]
            start = HALF + v * LANES
            width = min(LANES, CELLS - start)
            flat_ref[0, c, :, start : start + width] = values[TILES:, :width]
        copies.append(pltpu.make_async_copy(flat_ref.at[0, c], out_hbm.at[0, c], sems.at[c]))
        copies[-1].start()
    for c in range(tracers):
        guard = pltpu.roll(term_ref[c, 0], TILES, 0)
        for block in range(COARSE):
            total = [None, None]
            for y in range(block * BLOCK, (block + 1) * BLOCK):
                half = y * TILE // HALF
                v, shift = divmod(y * TILE - half * HALF, LANES)
                values = term_ref[c, v]
                if shift + TILE > LANES:
                    after = term_ref[c, v + 1] if v + 1 < COLS else guard
                    values = jnp.where(lane >= shift, values, after)
                if shift:
                    values = pltpu.roll(values, LANES - shift, 1)
                total[half] = values if total[half] is None else total[half] + values
            parts = [total[h][h * TILES : (h + 1) * TILES] for h in range(2) if total[h] is not None]
            summed = parts[0] if len(parts) == 1 else parts[0] + parts[1]
            summed = jnp.where(lane[:TILES] < TILE, summed, 0.0)
            rows_ref[pl.ds((c * COARSE + block) * TILES, TILES), :] = summed
    lane_in = lax.broadcasted_iota(I32, (LANES, LANES), 0)
    lane_out = lax.broadcasted_iota(I32, (LANES, LANES), 1)
    low_edge = lane_out * BLOCK
    pick = ((lane_in >= low_edge) & (lane_in < low_edge + BLOCK) & (lane_out < COARSE)).astype(F32)
    sums_ref[...] = jnp.dot(rows_ref[...], pick, precision=lax.Precision.HIGHEST, preferred_element_type=F32)
    for spot in range(8):
        total = jnp.zeros((TILES, LANES), F32)
        for k in range(tracers * COARSE):
            start = k * COARSE - spot * LANES
            if start >= LANES or start + COARSE <= 0:
                continue
            values = sums_ref[pl.ds(k * TILES, TILES), :]
            values = pltpu.roll(values, start % LANES, 1) if start % LANES else values
            if start < 0:
                values = jnp.where(lane[:TILES] < start + COARSE, values, 0.0)
            elif start + COARSE > LANES:
                values = jnp.where(lane[:TILES] >= start, values, 0.0)
            total = total + values
        rows_ref[pl.ds(spot, TILES, stride=8), :] = total
    part_ref[...] = jnp.zeros_like(part_ref)
    me = lax.axis_index("tiles")
    owner_copy.wait()
    for t in range(TILES):
        owner = owner_ref[me * TILES + t]
        part_ref[owner] = part_ref[owner] + rows_ref[pl.ds(t * 8, 8), :]
    for copy in copies:
        copy.wait()


def swaps(count, width=1):
    found = []
    for first in (0, 1):
        found.append(
            [
                pair
                for i in range(first, count // width - 1, 2)
                for k in range(width)
                for pair in ((i * width + k, (i + 1) * width + k), ((i + 1) * width + k, i * width + k))
            ]
        )
    return found


VMEM, SMEM, HBM = (pl.BlockSpec(memory_space=space) for space in (pltpu.VMEM, pltpu.SMEM, pltpu.HBM))


def call(kernel, ins, out, scratch, outs=None):
    return pl.pallas_call(
        kernel,
        out_shape=[jax.ShapeDtypeStruct(shape, F32) if isinstance(shape, tuple) else shape for shape in out],
        in_specs=ins,
        out_specs=outs or [VMEM] * len(out),
        scratch_shapes=[pltpu.VMEM(shape, F32) if isinstance(shape, tuple) else shape for shape in scratch],
        compiler_params=pltpu.CompilerParams(vmem_limit_bytes=32 * 1024 * 1024),
        name=kernel.__name__,
    )


def shards(adjoint, state, weights, vertical, mask, rate, neighbours, links, owners):
    tracers = adjoint.shape[1]
    number = lax.axis_size("tiles")
    even_swap, odd_swap = swaps(lax.axis_size("slab"))
    core_swap = [(2 * i + a, 2 * i + 1 - a) for i in range(number // 2) for a in range(2)]
    even_chips, odd_chips = swaps(number, 2)
    passing = swaps(number, 4)[0]
    plane = (COLS, 8, LANES)
    planes = (tracers, *plane)
    pack = (tracers + 1, *plane)
    guarded = (COLS + 2, 8, LANES)
    edges = (ROWS, LANES)
    block = SIDES * CHANNELS

    def around(edge, other):
        shown = jnp.concatenate([edge, other[:block], other[ROWS - block :]])
        even = lax.ppermute(shown, "tiles", even_chips)
        if number == 8:
            odd = lax.ppermute(even, "tiles", passing)
        else:
            odd = lax.ppermute(shown, "tiles", odd_chips)
        return jnp.concatenate([shown, odd, even])

    def across(first, second):
        return lax.ppermute(first, "slab", even_swap), lax.ppermute(second, "slab", odd_swap)

    table = jax.ShapeDtypeStruct(neighbours.shape, I32)
    edge, lam, wet, mixing, spread, neighbours, links = call(
        open_kernel,
        [HBM] * 5,
        [edges, planes, plane, plane, (tracers + 1, *guarded), table, table],
        [adjoint.shape, weights.shape, pltpu.VMEM(mask.shape, I32), pltpu.SemaphoreType.DMA((5,))],
    )(*(pltpu.with_memory_space_constraint(x, pltpu.HBM) for x in (adjoint, weights, mask, neighbours, links)))
    other = lax.ppermute(edge, "tiles", core_swap)
    pack_a, pack_b, stay, keep = call(inner_first_kernel, [VMEM] * 6, [pack, pack, plane, planes], [])(
        spread, lam, wet, mixing, vertical, rate
    )
    pack_a, pack_b, other = lax.optimization_barrier((pack_a, pack_b, other))
    from_a, from_b = across(pack_a, pack_b)
    near = around(edge, other)
    fixed_a, fixed_b = call(fixed_kernel, [VMEM] * 3, [edges] * 2, [])(keep, pack_a, pack_b)
    halo = call(halo_kernel, [SMEM] * 2 + [VMEM] * 4, [edges] * 2, [edges])
    change_a, change_b = halo(neighbours, links, near, edge, fixed_a, fixed_b)
    got_a, got_b = across(change_a, change_b)
    before, mix_a, mix_b = call(mix_first_kernel, [VMEM] * 4, [planes, plane, plane], [])(
        pack_a, pack_b, from_a, from_b
    )
    edge, lam, spread = call(middle_kernel, [VMEM] * 7, [edges, planes, (tracers, *guarded)], [edges])(
        change_a, change_b, got_a, got_b, before, mixing, edge
    )
    other = lax.ppermute(edge, "tiles", core_swap)
    (taken,) = call(inner_kernel, [VMEM] * 5, [planes], [])(spread, lam, wet, stay, keep)
    taken, other = lax.optimization_barrier((taken, other))
    from_a, from_b = across(taken, taken)
    near = around(edge, other)
    change_a, change_b = halo(neighbours, links, near, edge, fixed_a, fixed_b)
    got_a, got_b = across(change_a, change_b)
    before, weighted = call(mix_kernel, [VMEM] * 7, [planes, planes], [])(
        taken, from_a, from_b, mix_a, mix_b, wet, state
    )
    sums = (tracers * COARSE * TILES + 4, LANES)
    out, part = call(
        close_kernel,
        [HBM] + [VMEM] * 6,
        [adjoint.shape, (number, 8, LANES)],
        [planes, planes, sums, sums, adjoint.shape, edges]
        + [pltpu.SMEM(owners.shape, I32), pltpu.SemaphoreType.DMA((tracers + 1,))],
        [HBM, VMEM],
    )(pltpu.with_memory_space_constraint(owners, pltpu.HBM), change_a, change_b, got_a, got_b, before, weighted)
    part = lax.all_to_all(part, "tiles", 0, 0, tiled=True)
    gradient = part.sum(axis=0).reshape(1, 1, 8 * LANES)[:, :, : tracers * COARSE * COARSE]
    return out, gradient


def solution(mesh):
    placed = (
        P("slab", None, "tiles", None),
        P("slab", None, "tiles", None),
        P("slab", "tiles", None),
        P("slab", "tiles", None),
        P("slab", "tiles", None),
        P(None, "tiles", None),
        P("tiles", None),
        P("tiles", None),
        P(),
    )
    return jax.shard_map(
        shards,
        mesh=mesh,
        in_specs=placed,
        out_specs=(P("slab", None, "tiles", None), P("slab", "tiles", None)),
        check_vma=False,
    )
```

time: 59.8 us -> 51.8 us (0.87)
  the two profiles are of different devices: /device:TPU:0 before, /device:TPU:8 now
where the time goes in v3:
time: 51.8 us; the launch traced here: 51.6 us
  starting transfers between devices  20.2 us (39%)
  waiting for transfers between devices  11.9 us (23%)
  Pallas kernels  9.51 us (18%)
  blocking collectives  8.36 us (16%)
  between operations  0.87 us (2%)
  local copies, waits for them, and re-layouts  0.63 us (1%)
    ppermute x4, starting transfers between devices, across(): lax.ppermute(second, 'slab', odd_swap)  14.2 us
    all_to_all x1, blocking collectives, shards(): part = lax.all_to_all(part, 'tiles', 0, 0, tiled=True)  8.36 us
    ppermute x4, waiting for transfers between devices, across(): lax.ppermute(second, 'slab', odd_swap)  5.32 us
    ppermute x2, waiting for transfers between devices, around(): odd = lax.ppermute(even, 'tiles', passing)  4.58 us
    ppermute x2, starting transfers between devices, around(): odd = lax.ppermute(even, 'tiles', passing)  3.17 us
    ppermute x2, starting transfers between devices, around(): even = lax.ppermute(shown, 'tiles', even_chips)  2.16 us
    pallas_call x2, Pallas kernels, shards(): change_a, change_b = halo(neighbours, links, near, edge, fixed_a, fixed_b)  2.1 us
    pallas_call x1, Pallas kernels, shards(): call(close_kernel, [HBM] + [VMEM] * 6, [adjoint.shape, (number, 8, LANES)...  1.95 us
  transfers between devices with their start and end apart: 14, of which 9 were waited for; matrix products, arithmetic and copies ran while one was open for 0% of the time, Pallas kernels for 9%

profile of v3, /device:TPU:8, one launch (start us, length us, event | category | flops | bytes accessed | tf_op | source)
XLA Modules:
  0.0 51.6 jit_solution(8113941733294619464)
XLA Ops:
  0.6 0.0 copy-start
  0.6 0.0 copy-start.2
  0.7 1.9 %open_kernel.1 = (f32[64,128]{1,0:T(8,128)S(1)}, f32[3,32,8,128]{3,2,1,0:T(8,128)S(1)}, f32[32,8,128]{2,1,0:T(8,128)S(1)}, f32[32,8,128]{2,1,0:T(8,128)S(1)}, f3...) custom-call(f32[1,3,4,8100]{3,2,1,0:T(4,128)} %adjoint_hbm.1, f32[1,4,8100]{2,1,0:T(4,128)} %weights_hbm.1, ...), custom_call_target="tpu_custom_call" | custom-call | tf_op jit(solution)/shard_map/open_kernel/pallas_call | solution.py:501
  2.5 0.1 collective-permute-start
  2.6 0.0 copy-done
  2.6 0.0 copy-done.2
  2.6 0.9 %inner_first_kernel.1 = (f32[4,32,8,128]{3,2,1,0:T(8,128)S(1)}, f32[4,32,8,128]{3,2,1,0:T(8,128)S(1)}, f32[32,8,128]{2,1,0:T(8,128)S(1)}, f32[3,32,8,128]{3,2,1,0:T(8,128)S(1)}) custom-call(f32[4,34,8,128]{3,2,1,0:T(8,128)S(1)} %get-tuple-element.37.spread, f32[3,32,8,128]{3,2,1,0:T(8,128)S(1)} %get-tuple-element.38.lam_ref, ...), custom_call_target="tpu_custom_call" | custom-call | tf_op jit(solution)/shard_map/inner_first_kernel/pallas_call | solution.py:508
  3.6 0.2 collective-permute-done
  3.8 1.6 %collective-permute-start.1 = (f32[96,128]{1,0:T(8,128)S(1)}, f32[96,128]{1,0:T(8,128)S(1)}, u32[]{:S(2)}, u32[]{:S(2)}) collective-permute-start(f32[96,128]{1,0:T(8,128)S(1)} %pad_maximum_fusion), channel_id=1, source_target_pairs={{0,8},{8,0},{4,12},{12,4},{16,24},{24,16},{20,28},{28,20},{1,9},{9... | collective-permute-start | bytes 147464 | tf_op jit(solution)/shard_map/ppermute | solution.py:490
  5.4 0.4 collective-permute-start.5
  5.8 4.6 %collective-permute-start.6 = (f32[4,32,8,128]{3,2,1,0:T(8,128)S(1)}, f32[4,32,8,128]{3,2,1,0:T(8,128)S(1)}, u32[]{:S(2)}, u32[]{:S(2)}) collective-permute-start(f32[4,32,8,128]{3,2,1,0:T(8,128)S(1)} %get-tuple-element.46.pack_b), channel_id=1, source_target_pairs={{1,2},{2,1},{5,6},{6,5},{9,10},{10,9},{13,14},{14,13},{17,18},{18,... | collective-permute-start | bytes 1572872 | tf_op jit(solution)/shard_map/ppermute | solution.py:498
  10.4 0.0 collective-permute-done.1
  10.4 1.6 %collective-permute-start.2 = (f32[96,128]{1,0:T(8,128)S(1)}, f32[96,128]{1,0:T(8,128)S(1)}, u32[]{:S(2)}, u32[]{:S(2)}) collective-permute-start(f32[96,128]{1,0:T(8,128)S(1)} %collective-permute-done.1), channel_id=1, source_target_pairs={{0,16},{16,0},{4,20},{20,4},{8,24},{24,8},{12,28},{28,12},{1,17},{... | collective-permute-start | bytes 147464 | tf_op jit(solution)/shard_map/ppermute | solution.py:492
  12.0 0.6 %fixed_kernel.1 = (f32[64,128]{1,0:T(8,128)S(1)}, f32[64,128]{1,0:T(8,128)S(1)}) custom-call(f32[3,32,8,128]{3,2,1,0:T(8,128)S(1)} %get-tuple-element.44.keep_ref, f32[4,32,8,128]{3,2,1,0:T(8,128)S(1)} %get-tuple-element.45.pack_a, f32[4,32,8,128]{3,2,1,0:T(8,128)S(1)} %get-tuple-element.46.pack_b), custom_call_target="tpu_custom_call" | custom-call | tf_op jit(solution)/shard_map/fixed_kernel/pallas_call | solution.py:514
  12.6 2.0 %collective-permute-done.2 = f32[96,128]{1,0:T(8,128)S(1)} collective-permute-done((f32[96,128]{1,0:T(8,128)S(1)}, f32[96,128]{1,0:T(8,128)S(1)}, u32[]{:S(2)}, u32[]{:S(2)}) %collective-permute-start.2) | collective-permute-done | bytes 49184 | tf_op jit(solution)/shard_map/ppermute | solution.py:492
  14.6 1.1 %halo_kernel.2 = (f32[64,128]{1,0:T(8,128)S(1)}, f32[64,128]{1,0:T(8,128)S(1)}) custom-call(s32[4,4]{1,0:T(4,128)S(1)} %get-tuple-element.34.near_ref, s32[4,4]{1,0:T(4,128)S(1)} %get-tuple-element.35.link_ref, f32[288,128]{1,0:T(8,128)S(1)} %constant_dynamic-update-slice_fusion.all_ref, f32[64,128]{1,0:T(8,128)S(1)} %get-tuple-element.36.edge_ref.wet_edge_ref, ...), custom_call_target="tpu_custom_call" | custom-call | tf_op jit(solution)/shard_map/halo_kernel/pallas_call | solution.py:516
  15.6 0.0 collective-permute-start.3
  15.7 2.5 %collective-permute-start.4 = (f32[64,128]{1,0:T(8,128)S(1)}, f32[64,128]{1,0:T(8,128)S(1)}, u32[]{:S(2)}, u32[]{:S(2)}) collective-permute-start(f32[64,128]{1,0:T(8,128)S(1)} %get-tuple-element.50.change_b), channel_id=1, source_target_pairs={{1,2},{2,1},{5,6},{6,5},{9,10},{10,9},{13,14},{14,13},{17,18},{18,... | collective-permute-start | bytes 98312 | tf_op jit(solution)/shard_map/ppermute | solution.py:498
  18.2 1.3 %collective-permute-done.5.from_a = f32[4,32,8,128]{3,2,1,0:T(8,128)S(1)} collective-permute-done((f32[4,32,8,128]{3,2,1,0:T(8,128)S(1)}, f32[4,32,8,128]{3,2,1,0:T(8,128)S(1)}, u32[]{:S(2)}, u32[]{:S(2)}) %collective-permute-start.5) | collective-permute-done | bytes 524320 | tf_op jit(solution)/shard_map/ppermute | solution.py:498
  19.6 3.0 %collective-permute-done.6.from_b = f32[4,32,8,128]{3,2,1,0:T(8,128)S(1)} collective-permute-done((f32[4,32,8,128]{3,2,1,0:T(8,128)S(1)}, f32[4,32,8,128]{3,2,1,0:T(8,128)S(1)}, u32[]{:S(2)}, u32[]{:S(2)}) %collective-permute-start.6) | collective-permute-done | bytes 524320 | tf_op jit(solution)/shard_map/ppermute | solution.py:498
  22.6 0.1 mix_first_kernel.1
  22.7 0.0 collective-permute-done.3.got_a
  22.7 0.2 collective-permute-done.4.got_b
  22.9 1.1 %middle_kernel.1 = (f32[64,128]{1,0:T(8,128)S(1)}, f32[3,32,8,128]{3,2,1,0:T(8,128)S(1)}, f32[3,34,8,128]{3,2,1,0:T(8,128)S(1)}) custom-call(f32[64,128]{1,0:T(8,128)S(1)} %get-tuple-element.49.change_a, f32[64,128]{1,0:T(8,128)S(1)} %get-tuple-element.50.change_b, f32[64,128]{1,0:T(8,128)S(1)} %collective-permute-done.3.got_a, ...), custom_call_target="tpu_custom_call" | custom-call | tf_op jit(solution)/shard_map/middle_kernel/pallas_call | solution.py:521
  24.0 0.1 collective-permute-start.7
  24.1 0.7 %inner_kernel.1.taken_ref = f32[3,32,8,128]{3,2,1,0:T(8,128)S(1)} custom-call(f32[3,34,8,128]{3,2,1,0:T(8,128)S(1)} %get-tuple-element.53.spread, f32[3,32,8,128]{3,2,1,0:T(8,128)S(1)} %get-tuple-element.54.lam_ref, f32[32,8,128]{2,1,0:T(8,128)S(1)} %get-tuple-element.39.wet_ref, f32[32,8,128]{2,1,0:T(8,128)S(1)} %get-tuple-element.55.stay_ref, ...), custom_call_target="tpu_custom_call" | custom-call | tf_op jit(solution)/shard_map/inner_kernel/pallas_call | solution.py:525
  24.8 0.0 copy-start.1
  24.8 0.5 collective-permute-done.7
  25.3 0.6 %collective-permute-start.8 = (f32[96,128]{1,0:T(8,128)S(1)}, f32[96,128]{1,0:T(8,128)S(1)}, u32[]{:S(2)}, u32[]{:S(2)}) collective-permute-start(f32[96,128]{1,0:T(8,128)S(1)} %pad_maximum_fusion.1), channel_id=1, source_target_pairs={{0,8},{8,0},{4,12},{12,4},{16,24},{24,16},{20,28},{28,20},{1,9},{9... | collective-permute-start | bytes 147464 | tf_op jit(solution)/shard_map/ppermute | solution.py:490
  25.9 0.0 collective-permute-start.12
  25.9 3.6 %collective-permute-start.13 = (f32[3,32,8,128]{3,2,1,0:T(8,128)S(1)}, f32[3,32,8,128]{3,2,1,0:T(8,128)S(1)}, u32[]{:S(2)}, u32[]{:S(2)}) collective-permute-start(f32[3,32,8,128]{3,2,1,0:T(8,128)S(1)} %inner_kernel.1.taken_ref), channel_id=1, source_target_pairs={{1,2},{2,1},{5,6},{6,5},{9,10},{10,9},{13,14},{14,13},{17,18},{18,... | collective-permute-start | bytes 1179656 | tf_op jit(solution)/shard_map/ppermute | solution.py:498
  29.5 0.0 collective-permute-done.8
  29.6 1.6 %collective-permute-start.9 = (f32[96,128]{1,0:T(8,128)S(1)}, f32[96,128]{1,0:T(8,128)S(1)}, u32[]{:S(2)}, u32[]{:S(2)}) collective-permute-start(f32[96,128]{1,0:T(8,128)S(1)} %collective-permute-done.8), channel_id=1, source_target_pairs={{0,16},{16,0},{4,20},{20,4},{8,24},{24,8},{12,28},{28,12},{1,17},{... | collective-permute-start | bytes 147464 | tf_op jit(solution)/shard_map/ppermute | solution.py:492
  31.1 2.6 %collective-permute-done.9 = f32[96,128]{1,0:T(8,128)S(1)} collective-permute-done((f32[96,128]{1,0:T(8,128)S(1)}, f32[96,128]{1,0:T(8,128)S(1)}, u32[]{:S(2)}, u32[]{:S(2)}) %collective-permute-start.9) | collective-permute-done | bytes 49184 | tf_op jit(solution)/shard_map/ppermute | solution.py:492
  33.7 1.1 %halo_kernel.3 = (f32[64,128]{1,0:T(8,128)S(1)}, f32[64,128]{1,0:T(8,128)S(1)}) custom-call(s32[4,4]{1,0:T(4,128)S(1)} %get-tuple-element.34.near_ref, s32[4,4]{1,0:T(4,128)S(1)} %get-tuple-element.35.link_ref, f32[288,128]{1,0:T(8,128)S(1)} %constant_dynamic-update-slice_fusion.5.all_ref, f32[64,128]{1,0:T(8,128)S(1)} %get-tuple-element.52.edge_ref, ...), custom_call_target="tpu_custom_call" | custom-call | tf_op jit(solution)/shard_map/halo_kernel/pallas_call | solution.py:529
  34.8 0.0 collective-permute-start.10
  34.8 3.5 %collective-permute-start.11 = (f32[64,128]{1,0:T(8,128)S(1)}, f32[64,128]{1,0:T(8,128)S(1)}, u32[]{:S(2)}, u32[]{:S(2)}) collective-permute-start(f32[64,128]{1,0:T(8,128)S(1)} %get-tuple-element.58.change_b), channel_id=1, source_target_pairs={{1,2},{2,1},{5,6},{6,5},{9,10},{10,9},{13,14},{14,13},{17,18},{18,... | collective-permute-start | bytes 98312 | tf_op jit(solution)/shard_map/ppermute | solution.py:498
  38.3 0.0 collective-permute-done.12.from_a
  38.3 0.7 %collective-permute-done.13.from_b = f32[3,32,8,128]{3,2,1,0:T(8,128)S(1)} collective-permute-done((f32[3,32,8,128]{3,2,1,0:T(8,128)S(1)}, f32[3,32,8,128]{3,2,1,0:T(8,128)S(1)}, u32[]{:S(2)}, u32[]{:S(2)}) %collective-permute-start.13) | collective-permute-done | bytes 393248 | tf_op jit(solution)/shard_map/ppermute | solution.py:498
  39.0 0.0 copy-done.1
  39.0 0.2 mix_kernel.1
  39.2 0.0 collective-permute-done.10.got_a
  39.2 1.4 %collective-permute-done.11.got_b = f32[64,128]{1,0:T(8,128)S(1)} collective-permute-done((f32[64,128]{1,0:T(8,128)S(1)}, f32[64,128]{1,0:T(8,128)S(1)}, u32[]{:S(2)}, u32[]{:S(2)}) %collective-permute-start.11) | collective-permute-done | bytes 32800 | tf_op jit(solution)/shard_map/ppermute | solution.py:498
  40.6 1.9 %close_kernel.1 = (f32[1,3,4,8100]{3,2,1,0:T(4,128)}, f32[8,8,128]{2,1,0:T(8,128)S(1)}) custom-call(s32[32]{0:T(128)} %owner_hbm.1, f32[64,128]{1,0:T(8,128)S(1)} %get-tuple-element.57.change_a, f32[64,128]{1,0:T(8,128)S(1)} %get-tuple-element.58.change_b, f32[64,128]{1,0:T(8,128)S(1)} %collective-permute-done.10.got_a, ...), custom_call_target="tpu_custom_call" | custom-call | tf_op jit(solution)/shard_map/close_kernel/pallas_call | solution.py:535
  42.6 8.4 %all_to_all.5 = f32[8,8,128]{2,1,0:T(8,128)S(1)} all-to-all(f32[8,8,128]{2,1,0:T(8,128)S(1)} %get-tuple-element.65), channel_id=1, replica_groups=mesh['tiles'=8,'slab'=4] {'tiles'}, dimensions={0} | all-to-all | bytes 65536 | tf_op jit(solution)/shard_map/all_to_all | solution.py:543
  51.0 0.6 %slice.20 = f32[1,1,675]{2,1,0:T(1,128)} slice(f32[1,1,1024]{2,1,0:T(1,128)S(1)} %bitcast.1), slice={[0:1], [0:1], [0:675]} | slice | bytes 5400 | tf_op jit(solution)/shard_map/slice | solution.py:544
  (13 shorter events, 0.1 us)
Async XLA Ops:
  0.6 2.0 %copy-start = (f32[3,4,8100]{2,1,0:T(4,128)S(1)}, f32[3,4,8100]{2,1,0:T(4,128)}, u32[]{:S(2)}) copy-start(f32[3,4,8100]{2,1,0:T(4,128)} %rate_ref.1) | copy-start | bytes 1166404
  0.6 2.0 %copy-start.2 = (f32[1,4,8100]{2,1,0:T(4,128)S(1)}, f32[1,4,8100]{2,1,0:T(4,128)}, u32[]{:S(2)}) copy-start(f32[1,4,8100]{2,1,0:T(4,128)} %vertical_ref.1) | copy-start | bytes 388804
  2.5 1.3 %collective-permute-start = (f32[64,128]{1,0:T(8,128)S(1)}, f32[64,128]{1,0:T(8,128)S(1)}, u32[]{:S(2)}, u32[]{:S(2)}) collective-permute-start(f32[64,128]{1,0:T(8,128)S(1)} %get-tuple-element.36.edge_ref.wet_edge_ref), channel_id=1, source_target_pairs={{0,4},{4,0},{8,12},{12,8},{16,20},{20,16},{24,28},{28,24},{1,5},{5... | collective-permute-start | bytes 98312 | tf_op jit(solution)/shard_map/ppermute | solution.py:507
  3.8 6.6 %collective-permute-start.1 = (f32[96,128]{1,0:T(8,128)S(1)}, f32[96,128]{1,0:T(8,128)S(1)}, u32[]{:S(2)}, u32[]{:S(2)}) collective-permute-start(f32[96,128]{1,0:T(8,128)S(1)} %pad_maximum_fusion), channel_id=1, source_target_pairs={{0,8},{8,0},{4,12},{12,4},{16,24},{24,16},{20,28},{28,20},{1,9},{9... | collective-permute-start | bytes 147464 | tf_op jit(solution)/shard_map/ppermute | solution.py:490
  5.4 14.2 %collective-permute-start.5 = (f32[4,32,8,128]{3,2,1,0:T(8,128)S(1)}, f32[4,32,8,128]{3,2,1,0:T(8,128)S(1)}, u32[]{:S(2)}, u32[]{:S(2)}) collective-permute-start(f32[4,32,8,128]{3,2,1,0:T(8,128)S(1)} %get-tuple-element.45.pack_a), channel_id=1, source_target_pairs={{0,1},{1,0},{2,3},{3,2},{4,5},{5,4},{6,7},{7,6},{8,9},{9,8},{10,11... | collective-permute-start | bytes 1572872 | tf_op jit(solution)/shard_map/ppermute | solution.py:498
  5.8 16.8 %collective-permute-start.6 = (f32[4,32,8,128]{3,2,1,0:T(8,128)S(1)}, f32[4,32,8,128]{3,2,1,0:T(8,128)S(1)}, u32[]{:S(2)}, u32[]{:S(2)}) collective-permute-start(f32[4,32,8,128]{3,2,1,0:T(8,128)S(1)} %get-tuple-element.46.pack_b), channel_id=1, source_target_pairs={{1,2},{2,1},{5,6},{6,5},{9,10},{10,9},{13,14},{14,13},{17,18},{18,... | collective-permute-start | bytes 1572872 | tf_op jit(solution)/shard_map/ppermute | solution.py:498
  10.4 4.2 %collective-permute-start.2 = (f32[96,128]{1,0:T(8,128)S(1)}, f32[96,128]{1,0:T(8,128)S(1)}, u32[]{:S(2)}, u32[]{:S(2)}) collective-permute-start(f32[96,128]{1,0:T(8,128)S(1)} %collective-permute-done.1), channel_id=1, source_target_pairs={{0,16},{16,0},{4,20},{20,4},{8,24},{24,8},{12,28},{28,12},{1,17},{... | collective-permute-start | bytes 147464 | tf_op jit(solution)/shard_map/ppermute | solution.py:492
  15.6 7.1 %collective-permute-start.3 = (f32[64,128]{1,0:T(8,128)S(1)}, f32[64,128]{1,0:T(8,128)S(1)}, u32[]{:S(2)}, u32[]{:S(2)}) collective-permute-start(f32[64,128]{1,0:T(8,128)S(1)} %get-tuple-element.49.change_a), channel_id=1, source_target_pairs={{0,1},{1,0},{2,3},{3,2},{4,5},{5,4},{6,7},{7,6},{8,9},{9,8},{10,11... | collective-permute-start | bytes 98312 | tf_op jit(solution)/shard_map/ppermute | solution.py:498
  15.7 7.2 %collective-permute-start.4 = (f32[64,128]{1,0:T(8,128)S(1)}, f32[64,128]{1,0:T(8,128)S(1)}, u32[]{:S(2)}, u32[]{:S(2)}) collective-permute-start(f32[64,128]{1,0:T(8,128)S(1)} %get-tuple-element.50.change_b), channel_id=1, source_target_pairs={{1,2},{2,1},{5,6},{6,5},{9,10},{10,9},{13,14},{14,13},{17,18},{18,... | collective-permute-start | bytes 98312 | tf_op jit(solution)/shard_map/ppermute | solution.py:498
  24.0 1.3 %collective-permute-start.7 = (f32[64,128]{1,0:T(8,128)S(1)}, f32[64,128]{1,0:T(8,128)S(1)}, u32[]{:S(2)}, u32[]{:S(2)}) collective-permute-start(f32[64,128]{1,0:T(8,128)S(1)} %get-tuple-element.52.edge_ref), channel_id=1, source_target_pairs={{0,4},{4,0},{8,12},{12,8},{16,20},{20,16},{24,28},{28,24},{1,5},{5... | collective-permute-start | bytes 98312 | tf_op jit(solution)/shard_map/ppermute | solution.py:524
  24.8 14.2 %copy-start.1 = (f32[1,3,4,8100]{3,2,1,0:T(4,128)S(1)}, f32[1,3,4,8100]{3,2,1,0:T(4,128)}, u32[]{:S(2)}) copy-start(f32[1,3,4,8100]{3,2,1,0:T(4,128)} %state_ref.1) | copy-start | bytes 1166404
  25.3 4.2 %collective-permute-start.8 = (f32[96,128]{1,0:T(8,128)S(1)}, f32[96,128]{1,0:T(8,128)S(1)}, u32[]{:S(2)}, u32[]{:S(2)}) collective-permute-start(f32[96,128]{1,0:T(8,128)S(1)} %pad_maximum_fusion.1), channel_id=1, source_target_pairs={{0,8},{8,0},{4,12},{12,4},{16,24},{24,16},{20,28},{28,20},{1,9},{9... | collective-permute-start | bytes 147464 | tf_op jit(solution)/shard_map/ppermute | solution.py:490
  25.9 12.4 %collective-permute-start.12 = (f32[3,32,8,128]{3,2,1,0:T(8,128)S(1)}, f32[3,32,8,128]{3,2,1,0:T(8,128)S(1)}, u32[]{:S(2)}, u32[]{:S(2)}) collective-permute-start(f32[3,32,8,128]{3,2,1,0:T(8,128)S(1)} %inner_kernel.1.taken_ref), channel_id=1, source_target_pairs={{0,1},{1,0},{2,3},{3,2},{4,5},{5,4},{6,7},{7,6},{8,9},{9,8},{10,11... | collective-permute-start | bytes 1179656 | tf_op jit(solution)/shard_map/ppermute | solution.py:498
  25.9 13.1 %collective-permute-start.13 = (f32[3,32,8,128]{3,2,1,0:T(8,128)S(1)}, f32[3,32,8,128]{3,2,1,0:T(8,128)S(1)}, u32[]{:S(2)}, u32[]{:S(2)}) collective-permute-start(f32[3,32,8,128]{3,2,1,0:T(8,128)S(1)} %inner_kernel.1.taken_ref), channel_id=1, source_target_pairs={{1,2},{2,1},{5,6},{6,5},{9,10},{10,9},{13,14},{14,13},{17,18},{18,... | collective-permute-start | bytes 1179656 | tf_op jit(solution)/shard_map/ppermute | solution.py:498
  29.6 4.2 %collective-permute-start.9 = (f32[96,128]{1,0:T(8,128)S(1)}, f32[96,128]{1,0:T(8,128)S(1)}, u32[]{:S(2)}, u32[]{:S(2)}) collective-permute-start(f32[96,128]{1,0:T(8,128)S(1)} %collective-permute-done.8), channel_id=1, source_target_pairs={{0,16},{16,0},{4,20},{20,4},{8,24},{24,8},{12,28},{28,12},{1,17},{... | collective-permute-start | bytes 147464 | tf_op jit(solution)/shard_map/ppermute | solution.py:492
  34.8 4.4 %collective-permute-start.10 = (f32[64,128]{1,0:T(8,128)S(1)}, f32[64,128]{1,0:T(8,128)S(1)}, u32[]{:S(2)}, u32[]{:S(2)}) collective-permute-start(f32[64,128]{1,0:T(8,128)S(1)} %get-tuple-element.57.change_a), channel_id=1, source_target_pairs={{0,1},{1,0},{2,3},{3,2},{4,5},{5,4},{6,7},{7,6},{8,9},{9,8},{10,11... | collective-permute-start | bytes 98312 | tf_op jit(solution)/shard_map/ppermute | solution.py:498
  34.8 5.8 %collective-permute-start.11 = (f32[64,128]{1,0:T(8,128)S(1)}, f32[64,128]{1,0:T(8,128)S(1)}, u32[]{:S(2)}, u32[]{:S(2)}) collective-permute-start(f32[64,128]{1,0:T(8,128)S(1)} %get-tuple-element.58.change_b), channel_id=1, source_target_pairs={{1,2},{2,1},{5,6},{6,5},{9,10},{10,9},{13,14},{14,13},{17,18},{18,... | collective-permute-start | bytes 98312 | tf_op jit(solution)/shard_map/ppermute | solution.py:498

commit v4 on v3

--- a/solution.py
+++ b/solution.py
@@ -20,9 +20,16 @@
 SPOTS = TILES * SIDES
 CHANNELS = 4
 ROWS = SPOTS * CHANNELS
-SHOWN = ROWS + 2 * SIDES * CHANNELS
+TILE_ROWS = SIDES * CHANNELS
+SHOWN = ROWS + TILE_ROWS
+OWN = 0 + SHOWN
+ODD = 0 + SHOWN + SHOWN
+EVEN = 0
+OTHER = 0 + SHOWN + SHOWN + SHOWN
+CLOSED = -8
+TURNED = 1 << 16
 FIRST_HIGH = HALF // TILE
-UNROLL = 8
+UNROLL = 32
 F32 = jnp.float32
 I32 = jnp.int32
 
@@ -118,36 +125,58 @@
         ref[pl.ds(s * CHANNELS + channel, TILES, stride=SIDES * CHANNELS), :] = sides[s]
 
 
+def put_given(edge_ref, give_ref):
+    first, last = edge_ref[pl.ds(0, TILE_ROWS), :], edge_ref[pl.ds(ROWS - TILE_ROWS, TILE_ROWS), :]
+    start = lax.axis_index("tiles") % 2 == 0
+    give_ref[pl.ds(0, TILE_ROWS), :] = jnp.where(start, first, last)
+    give_ref[pl.ds(TILE_ROWS, TILE_ROWS), :] = jnp.where(start, last, first)
+
+
 def channel_rows(ref, channel):
     return ref[pl.ds(channel, SPOTS, stride=CHANNELS), :]
 
 
-def halos(near_ref, link_ref, all_ref, out_ref):
+def halo_places(table_ref, out_ref):
     me = lax.axis_index("tiles")
     chip, core = me // 2, me % 2
     even = chip % 2 == 0
-    turned, closed = [], []
+    places = []
     for t in range(TILES):
         for s in range(SIDES):
-            near, link = near_ref[t, s], link_ref[t, s]
-            tile = jnp.where(near < 0, me * TILES, near)
-            device = tile // TILES
-            inner = tile % TILES
+            code = table_ref[t, s]
+            tile, link = code >> 3, code & 7
+            device, inner = tile // TILES, tile % TILES
             step = device // 2 - chip
-            place = jnp.where(step == 0, 0, jnp.where((step == 1) == even, 2 * SHOWN, SHOWN))
-            far = jnp.where(inner == 0, ROWS, ROWS + SIDES * CHANNELS)
-            row = place + jnp.where(device % 2 == core, inner * (SIDES * CHANNELS), far) + (link // 2) * CHANNELS
-            out_ref[pl.ds((t * SIDES + s) * CHANNELS, CHANNELS), :] = all_ref[pl.ds(row, CHANNELS), :]
-            turned.append(link % 2)
-            closed.append((near < 0).astype(I32))
-    lane, low = position()
+            start = jnp.where((step == 1) == even, EVEN, ODD)
+            own = jnp.where(device == me, OWN + inner * TILE_ROWS, OTHER)
+            beside = start + jnp.where(device % 2 == core, inner * TILE_ROWS, ROWS)
+            row = jnp.where(step == 0, own, beside) + (link // 2) * CHANNELS
+            places.append(jnp.where(code < 0, CLOSED, row + (link % 2) * TURNED))
+    _, low = position()
+    channel = lax.broadcasted_iota(I32, (8, LANES), 0) % CHANNELS
+    for k in range(0, SPOTS, 2):
+        out_ref[pl.ds(k * CHANNELS, 8), :] = jnp.where(low, places[k], places[k + 1]) + channel
+
+
+def halos(place_ref, all_ref, out_ref):
+    lane, _ = position()
     back = jnp.clip(TILE - 1 - lane, 0, LANES - 1)
-    for k in range(0, SPOTS, 2):
-        at = pl.ds(k * CHANNELS, 8)
-        values = out_ref[at, :]
-        values = jnp.where(jnp.where(low, turned[k], turned[k + 1]) == 1, lane_gather(values, back), values)
-        shut = jnp.where(low, closed[k], closed[k + 1]) == 1
-        out_ref[at, :] = jnp.where(shut | (lane >= TILE), 0.0, values)
+    for t in range(TILES):
+        starts = [start + t * TILE_ROWS for start in (ODD, EVEN)]
+        starts += [OWN + k * TILE_ROWS for k in (t - 1, t + 1) if 0 <= k < TILES]
+        if t in (0, TILES - 1):
+            starts += [OTHER, ODD + ROWS, EVEN + ROWS]
+        chunks = [start // 8 + k for start in starts for k in range(TILE_ROWS // 8)]
+        for h in range(TILE_ROWS // 8):
+            at = pl.ds(t * TILE_ROWS + h * 8, 8)
+            place = place_ref[at, :]
+            chunk, row = (place & (TURNED - 1)) >> 3, place & 7
+            found = jnp.zeros((8, LANES), F32)
+            for k in chunks:
+                picked = jnp.take_along_axis(all_ref[pl.ds(k * 8, 8), :], row, axis=0, mode="promise_in_bounds")
+                found = jnp.where(chunk == k, picked, found)
+            found = jnp.where((place >> 16) == 1, lane_gather(found, back), found)
+            out_ref[at, :] = jnp.where(lane < TILE, found, 0.0)
 
 
 def change_planes(own_a, own_b, got_a, got_b, tracers, scratch, lane, low):
@@ -194,8 +223,8 @@
 
 def open_kernel(
     adjoint_hbm, weights_hbm, mask_hbm, near_hbm, link_hbm,
-    edge_ref, lam_ref, wet_ref, mixing_ref, spread, near_ref, link_ref,
-    adjoint_ref, weights_ref, mask_ref, sems,
+    edge_ref, give_ref, lam_ref, wet_ref, mixing_ref, spread, table_ref,
+    adjoint_ref, weights_ref, mask_ref, near_ref, link_ref, sems,
 ):
     tracers = lam_ref.shape[0]
     pairs = (
@@ -231,8 +260,10 @@
         set_guards(spread, c, low)
     for p, sides in enumerate(edge_sides(lambda p, v: spread[p, v + 1], tracers + 1, lane, low)):
         put_sides(edge_ref, p, sides)
+    put_given(edge_ref, give_ref)
     copies[3].wait()
     copies[4].wait()
+    table_ref[...] = near_ref[...] * 8 + link_ref[...]
 
 
 def inner_first_kernel(spread, lam_ref, wet_ref, mixing_ref, vertical_ref, rate_ref, pack_a, pack_b, stay_ref, keep_ref):
@@ -277,9 +308,10 @@
     loop(body)
 
 
-def fixed_kernel(keep_ref, pack_a, pack_b, out_a, out_b):
+def fixed_kernel(table_ref, keep_ref, pack_a, pack_b, out_a, out_b, place_ref):
     tracers = keep_ref.shape[0]
     lane, low = position()
+    halo_places(table_ref, place_ref)
 
     def load(p, v):
         return keep_ref[p, v] if p < tracers else (pack_a if p == tracers else pack_b)[tracers, v]
@@ -292,9 +324,9 @@
     put_sides(out_b, tracers, found[tracers + 1])
 
 
-def halo_kernel(near_ref, link_ref, all_ref, edge_ref, fixed_a, fixed_b, out_a, out_b, halo_ref):
+def halo_kernel(place_ref, all_ref, edge_ref, fixed_a, fixed_b, out_a, out_b, halo_ref):
     tracers = CHANNELS - 1
-    halos(near_ref, link_ref, all_ref, halo_ref)
+    halos(place_ref, all_ref, halo_ref)
     wet, halo_wet = channel_rows(edge_ref, tracers), channel_rows(halo_ref, tracers)
     for c in range(tracers):
         change = channel_rows(fixed_a, c) * (wet * channel_rows(halo_ref, c) - channel_rows(edge_ref, c) * halo_wet)
@@ -304,7 +336,7 @@
     out_b[pl.ds(tracers, SPOTS, stride=CHANNELS), :] = channel_rows(fixed_b, tracers)
 
 
-def mix_first_kernel(pack_a, pack_b, from_a, from_b, lam_ref, mix_a_ref, mix_b_ref):
+def mix_first_kernel(pack_a, pack_b, from_b, from_a, lam_ref, mix_a_ref, mix_b_ref):
     tracers = lam_ref.shape[0]
 
     def body(v, carry):
@@ -336,7 +368,7 @@
 
 
 def middle_kernel(
-    change_a, change_b, got_a, got_b, before_ref, mixing_ref, wet_edge_ref, edge_ref, lam_ref, spread, scratch
+    change_a, change_b, got_a, got_b, before_ref, mixing_ref, wet_edge_ref, edge_ref, give_ref, lam_ref, spread, scratch
 ):
     tracers = lam_ref.shape[0]
     lane, low = position()
@@ -360,6 +392,7 @@
     for p, sides in enumerate(edge_sides(lambda p, v: spread[p, v + 1], tracers, lane, low)):
         put_sides(edge_ref, p, sides)
     edge_ref[pl.ds(tracers, SPOTS, stride=CHANNELS), :] = channel_rows(wet_edge_ref, tracers)
+    put_given(edge_ref, give_ref)
 
 
 def close_kernel(
@@ -416,8 +449,14 @@
     lane_in = lax.broadcasted_iota(I32, (LANES, LANES), 0)
     lane_out = lax.broadcasted_iota(I32, (LANES, LANES), 1)
     low_edge = lane_out * BLOCK
-    pick = ((lane_in >= low_edge) & (lane_in < low_edge + BLOCK) & (lane_out < COARSE)).astype(F32)
-    sums_ref[...] = jnp.dot(rows_ref[...], pick, precision=lax.Precision.HIGHEST, preferred_element_type=F32)
+    pick = ((lane_in >= low_edge) & (lane_in < low_edge + BLOCK) & (lane_out < COARSE)).astype(jnp.bfloat16)
+    left = rows_ref[...]
+    summed = jnp.zeros_like(left)
+    for _ in range(3):
+        part = left.astype(jnp.bfloat16)
+        summed = summed + jnp.dot(part, pick, preferred_element_type=F32)
+        left = left - part.astype(F32)
+    sums_ref[...] = summed
     for spot in range(8):
         total = jnp.zeros((TILES, LANES), F32)
         for k in range(tracers * COARSE):
@@ -483,50 +522,53 @@
     pack = (tracers + 1, *plane)
     guarded = (COLS + 2, 8, LANES)
     edges = (ROWS, LANES)
-    block = SIDES * CHANNELS
+    given = (2 * TILE_ROWS, LANES)
 
     def around(edge, other):
-        shown = jnp.concatenate([edge, other[:block], other[ROWS - block :]])
+        shown = jnp.concatenate([edge, other[:TILE_ROWS]])
         even = lax.ppermute(shown, "tiles", even_chips)
         if number == 8:
             odd = lax.ppermute(even, "tiles", passing)
         else:
             odd = lax.ppermute(shown, "tiles", odd_chips)
-        return jnp.concatenate([shown, odd, even])
+        return jnp.concatenate([even, shown, odd, other[TILE_ROWS:]])
 
     def across(first, second):
         return lax.ppermute(first, "slab", even_swap), lax.ppermute(second, "slab", odd_swap)
 
-    table = jax.ShapeDtypeStruct(neighbours.shape, I32)
-    edge, lam, wet, mixing, spread, neighbours, links = call(
+    edge, give, lam, wet, mixing, spread, table = call(
         open_kernel,
         [HBM] * 5,
-        [edges, planes, plane, plane, (tracers + 1, *guarded), table, table],
-        [adjoint.shape, weights.shape, pltpu.VMEM(mask.shape, I32), pltpu.SemaphoreType.DMA((5,))],
+        [edges, given, planes, plane, plane, (tracers + 1, *guarded), jax.ShapeDtypeStruct(links.shape, I32)],
+        [adjoint.shape, weights.shape]
+        + [pltpu.VMEM(table.shape, I32) for table in (mask, neighbours, links)]
+        + [pltpu.SemaphoreType.DMA((5,))],
     )(*(pltpu.with_memory_space_constraint(x, pltpu.HBM) for x in (adjoint, weights, mask, neighbours, links)))
-    other = lax.ppermute(edge, "tiles", core_swap)
+    other = lax.ppermute(give, "tiles", core_swap)
     pack_a, pack_b, stay, keep = call(inner_first_kernel, [VMEM] * 6, [pack, pack, plane, planes], [])(
         spread, lam, wet, mixing, vertical, rate
     )
     pack_a, pack_b, other = lax.optimization_barrier((pack_a, pack_b, other))
     from_a, from_b = across(pack_a, pack_b)
     near = around(edge, other)
-    fixed_a, fixed_b = call(fixed_kernel, [VMEM] * 3, [edges] * 2, [])(keep, pack_a, pack_b)
-    halo = call(halo_kernel, [SMEM] * 2 + [VMEM] * 4, [edges] * 2, [edges])
-    change_a, change_b = halo(neighbours, links, near, edge, fixed_a, fixed_b)
+    fixed_a, fixed_b, places = call(
+        fixed_kernel, [SMEM] + [VMEM] * 3, [edges] * 2 + [jax.ShapeDtypeStruct(edges, I32)], []
+    )(table, keep, pack_a, pack_b)
+    halo = call(halo_kernel, [VMEM] * 5, [edges] * 2, [edges])
+    change_a, change_b = halo(places, near, edge, fixed_a, fixed_b)
     got_a, got_b = across(change_a, change_b)
     before, mix_a, mix_b = call(mix_first_kernel, [VMEM] * 4, [planes, plane, plane], [])(
-        pack_a, pack_b, from_a, from_b
-    )
-    edge, lam, spread = call(middle_kernel, [VMEM] * 7, [edges, planes, (tracers, *guarded)], [edges])(
+        pack_a, pack_b, from_b, from_a
+    )
+    edge, give, lam, spread = call(middle_kernel, [VMEM] * 7, [edges, given, planes, (tracers, *guarded)], [edges])(
         change_a, change_b, got_a, got_b, before, mixing, edge
     )
-    other = lax.ppermute(edge, "tiles", core_swap)
+    other = lax.ppermute(give, "tiles", core_swap)
     (taken,) = call(inner_kernel, [VMEM] * 5, [planes], [])(spread, lam, wet, stay, keep)
     taken, other = lax.optimization_barrier((taken, other))
     from_a, from_b = across(taken, taken)
     near = around(edge, other)
-    change_a, change_b = halo(neighbours, links, near, edge, fixed_a, fixed_b)
+    change_a, change_b = halo(places, near, edge, fixed_a, fixed_b)
     got_a, got_b = across(change_a, change_b)
     before, weighted = call(mix_kernel, [VMEM] * 7, [planes, planes], [])(
         taken, from_a, from_b, mix_a, mix_b, wet, state

time: 51.8 us -> 49.4 us (0.954)
  the two profiles are of different devices: /device:TPU:8 before, /device:TPU:0 now
where the time goes in v4:
time: 49.4 us; the launch traced here: 48.5 us
  starting transfers between devices  17.8 us (36%)
  waiting for transfers between devices  14.6 us (30%)
  blocking collectives  8.32 us (17%)
  Pallas kernels  6.33 us (13%)
  between operations  0.79 us (2%)
  local copies, waits for them, and re-layouts  0.63 us (1%)
    all_to_all x1, blocking collectives, shards(): part = lax.all_to_all(part, 'tiles', 0, 0, tiled=True)  8.32 us
    ppermute x4, starting transfers between devices, across(): lax.ppermute(first, 'slab', even_swap)  8.06 us
    ppermute x4, waiting for transfers between devices, across(): lax.ppermute(first, 'slab', even_swap)  7.69 us
    ppermute x2, waiting for transfers between devices, around(): odd = lax.ppermute(even, 'tiles', passing)  4.96 us
    ppermute x2, starting transfers between devices, around(): even = lax.ppermute(shown, 'tiles', even_chips)  3.37 us
    ppermute x2, starting transfers between devices, around(): odd = lax.ppermute(even, 'tiles', passing)  3.17 us
    ppermute x4, starting transfers between devices, across(): lax.ppermute(second, 'slab', odd_swap)  2.67 us
    pallas_call x1, Pallas kernels, shards(): call(open_kernel, [HBM] * 5, [edges, given, planes, plane, plane, (tracer...  1.61 us
  transfers between devices with their start and end apart: 14, of which 9 were waited for; matrix products, arithmetic and copies ran while one was open for 0% of the time, Pallas kernels for 5%

profile of v4, /device:TPU:0, one launch (start us, length us, event | category | flops | bytes accessed | tf_op | source)
XLA Modules:
  0.0 48.5 jit_solution(13363606979637760589)
XLA Ops:
  0.6 0.0 copy-start.2
  0.6 0.0 copy-start
  0.7 1.6 %open_kernel.1 = (f32[64,128]{1,0:T(8,128)S(1)}, f32[32,128]{1,0:T(8,128)S(1)}, f32[3,32,8,128]{3,2,1,0:T(8,128)S(1)}, f32[32,8,128]{2,1,0:T(8,128)S(1)}, f32[32...) custom-call(f32[1,3,4,8100]{3,2,1,0:T(4,128)} %adjoint_hbm.1, f32[1,4,8100]{2,1,0:T(4,128)} %weights_hbm.1, ...), custom_call_target="tpu_custom_call" | custom-call | tf_op jit(solution)/shard_map/open_kernel/pallas_call | solution.py:539
  2.3 0.5 %collective-permute-start = (f32[32,128]{1,0:T(8,128)S(1)}, f32[32,128]{1,0:T(8,128)S(1)}, u32[]{:S(2)}, u32[]{:S(2)}) collective-permute-start(f32[32,128]{1,0:T(8,128)S(1)} %get-tuple-element.44), channel_id=1, source_target_pairs={{0,4},{4,0},{8,12},{12,8},{16,20},{20,16},{24,28},{28,24},{1,5},{5... | collective-permute-start | bytes 49160 | tf_op jit(solution)/shard_map/ppermute | solution.py:547
  2.8 0.0 copy-done.2
  2.8 0.0 copy-done
  2.8 0.6 %inner_first_kernel.1 = (f32[4,32,8,128]{3,2,1,0:T(8,128)S(1)}, f32[4,32,8,128]{3,2,1,0:T(8,128)S(1)}, f32[32,8,128]{2,1,0:T(8,128)S(1)}, f32[3,32,8,128]{3,2,1,0:T(8,128)S(1)}) custom-call(f32[4,34,8,128]{3,2,1,0:T(8,128)S(1)} %get-tuple-element.37.spread, f32[3,32,8,128]{3,2,1,0:T(8,128)S(1)} %get-tuple-element.38.lam_ref, ...), custom_call_target="tpu_custom_call" | custom-call | tf_op jit(solution)/shard_map/inner_first_kernel/pallas_call | solution.py:548
  3.4 0.2 collective-permute-done
  3.6 2.8 %collective-permute-start.1 = (f32[80,128]{1,0:T(8,128)S(1)}, f32[80,128]{1,0:T(8,128)S(1)}, u32[]{:S(2)}, u32[]{:S(2)}) collective-permute-start(f32[80,128]{1,0:T(8,128)S(1)} %pad_maximum_fusion), channel_id=1, source_target_pairs={{0,8},{8,0},{4,12},{12,4},{16,24},{24,16},{20,28},{28,20},{1,9},{9... | collective-permute-start | bytes 122888 | tf_op jit(solution)/shard_map/ppermute | solution.py:529
  6.5 0.7 %collective-permute-start.5 = (f32[4,32,8,128]{3,2,1,0:T(8,128)S(1)}, f32[4,32,8,128]{3,2,1,0:T(8,128)S(1)}, u32[]{:S(2)}, u32[]{:S(2)}) collective-permute-start(f32[4,32,8,128]{3,2,1,0:T(8,128)S(1)} %get-tuple-element.46.pack_b), channel_id=1, source_target_pairs={{1,2},{2,1},{5,6},{6,5},{9,10},{10,9},{13,14},{14,13},{17,18},{18,... | collective-permute-start | bytes 1572872 | tf_op jit(solution)/shard_map/ppermute | solution.py:537
  7.2 4.4 %collective-permute-start.6 = (f32[4,32,8,128]{3,2,1,0:T(8,128)S(1)}, f32[4,32,8,128]{3,2,1,0:T(8,128)S(1)}, u32[]{:S(2)}, u32[]{:S(2)}) collective-permute-start(f32[4,32,8,128]{3,2,1,0:T(8,128)S(1)} %get-tuple-element.45.pack_a), channel_id=1, source_target_pairs={{0,1},{1,0},{2,3},{3,2},{4,5},{5,4},{6,7},{7,6},{8,9},{9,8},{10,11... | collective-permute-start | bytes 1572872 | tf_op jit(solution)/shard_map/ppermute | solution.py:537
  11.6 0.9 %fixed_kernel.1 = (f32[64,128]{1,0:T(8,128)S(1)}, f32[64,128]{1,0:T(8,128)S(1)}, s32[64,128]{1,0:T(8,128)S(1)}) custom-call(s32[4,4]{1,0:T(4,128)S(1)} %get-tuple-element.36.table_ref, f32[3,32,8,128]{3,2,1,0:T(8,128)S(1)} %get-tuple-element.41.keep_ref, f32[4,32,8,128]{3,2,1,0:T(8,128)S(1)} %get-tuple-element.45.pack_a, ...), custom_call_target="tpu_custom_call" | custom-call | tf_op jit(solution)/shard_map/fixed_kernel/pallas_call | solution.py:554
  12.5 0.0 collective-permute-done.1
  12.6 1.6 %collective-permute-start.2 = (f32[80,128]{1,0:T(8,128)S(1)}, f32[80,128]{1,0:T(8,128)S(1)}, u32[]{:S(2)}, u32[]{:S(2)}) collective-permute-start(f32[80,128]{1,0:T(8,128)S(1)} %collective-permute-done.1), channel_id=1, source_target_pairs={{0,16},{16,0},{4,20},{20,4},{8,24},{24,8},{12,28},{28,12},{1,17},{... | collective-permute-start | bytes 122888 | tf_op jit(solution)/shard_map/ppermute | solution.py:531
  14.2 2.5 %collective-permute-done.2 = f32[80,128]{1,0:T(8,128)S(1)} collective-permute-done((f32[80,128]{1,0:T(8,128)S(1)}, f32[80,128]{1,0:T(8,128)S(1)}, u32[]{:S(2)}, u32[]{:S(2)}) %collective-permute-start.2) | collective-permute-done | bytes 40992 | tf_op jit(solution)/shard_map/ppermute | solution.py:531
  16.6 0.1 halo_kernel.2
  16.8 0.1 collective-permute-start.3
  16.9 0.7 %collective-permute-start.4 = (f32[64,128]{1,0:T(8,128)S(1)}, f32[64,128]{1,0:T(8,128)S(1)}, u32[]{:S(2)}, u32[]{:S(2)}) collective-permute-start(f32[64,128]{1,0:T(8,128)S(1)} %get-tuple-element.53.change_b), channel_id=1, source_target_pairs={{1,2},{2,1},{5,6},{6,5},{9,10},{10,9},{13,14},{14,13},{17,18},{18,... | collective-permute-start | bytes 98312 | tf_op jit(solution)/shard_map/ppermute | solution.py:537
  17.5 0.0 collective-permute-done.5.from_b
  17.5 6.1 %collective-permute-done.6.from_a = f32[4,32,8,128]{3,2,1,0:T(8,128)S(1)} collective-permute-done((f32[4,32,8,128]{3,2,1,0:T(8,128)S(1)}, f32[4,32,8,128]{3,2,1,0:T(8,128)S(1)}, u32[]{:S(2)}, u32[]{:S(2)}) %collective-permute-start.6) | collective-permute-done | bytes 524320 | tf_op jit(solution)/shard_map/ppermute | solution.py:537
  23.6 0.1 mix_first_kernel.1
  23.7 0.3 collective-permute-done.3.got_a
  24.0 0.0 collective-permute-done.4.got_b
  24.0 0.6 %middle_kernel.1 = (f32[64,128]{1,0:T(8,128)S(1)}, f32[32,128]{1,0:T(8,128)S(1)}, f32[3,32,8,128]{3,2,1,0:T(8,128)S(1)}, f32[3,34,8,128]{3,2,1,0:T(8,128)S(1)}) custom-call(f32[64,128]{1,0:T(8,128)S(1)} %get-tuple-element.52.change_a, f32[64,128]{1,0:T(8,128)S(1)} %get-tuple-element.53.change_b, f32[64,128]{1,0:T(8,128)S(1)} %collective-permute-done.3.got_a, ...), custom_call_target="tpu_custom_call" | custom-call | tf_op jit(solution)/shard_map/middle_kernel/pallas_call | solution.py:563
  24.6 0.1 collective-permute-start.7
  24.6 0.5 inner_kernel.1.taken_ref
  25.1 0.0 copy-start.1
  25.1 0.7 %collective-permute-done.7 = f32[32,128]{1,0:T(8,128)S(1)} collective-permute-done((f32[32,128]{1,0:T(8,128)S(1)}, f32[32,128]{1,0:T(8,128)S(1)}, u32[]{:S(2)}, u32[]{:S(2)}) %collective-permute-start.7) | collective-permute-done | bytes 16416 | tf_op jit(solution)/shard_map/ppermute | solution.py:566
  25.8 0.5 %collective-permute-start.8 = (f32[80,128]{1,0:T(8,128)S(1)}, f32[80,128]{1,0:T(8,128)S(1)}, u32[]{:S(2)}, u32[]{:S(2)}) collective-permute-start(f32[80,128]{1,0:T(8,128)S(1)} %pad_maximum_fusion.1), channel_id=1, source_target_pairs={{0,8},{8,0},{4,12},{12,4},{16,24},{24,16},{20,28},{28,20},{1,9},{9... | collective-permute-start | bytes 122888 | tf_op jit(solution)/shard_map/ppermute | solution.py:529
  26.3 1.7 %collective-permute-start.12 = (f32[3,32,8,128]{3,2,1,0:T(8,128)S(1)}, f32[3,32,8,128]{3,2,1,0:T(8,128)S(1)}, u32[]{:S(2)}, u32[]{:S(2)}) collective-permute-start(f32[3,32,8,128]{3,2,1,0:T(8,128)S(1)} %inner_kernel.1.taken_ref), channel_id=1, source_target_pairs={{0,1},{1,0},{2,3},{3,2},{4,5},{5,4},{6,7},{7,6},{8,9},{9,8},{10,11... | collective-permute-start | bytes 1179656 | tf_op jit(solution)/shard_map/ppermute | solution.py:537
  28.1 0.7 %collective-permute-start.13 = (f32[3,32,8,128]{3,2,1,0:T(8,128)S(1)}, f32[3,32,8,128]{3,2,1,0:T(8,128)S(1)}, u32[]{:S(2)}, u32[]{:S(2)}) collective-permute-start(f32[3,32,8,128]{3,2,1,0:T(8,128)S(1)} %inner_kernel.1.taken_ref), channel_id=1, source_target_pairs={{1,2},{2,1},{5,6},{6,5},{9,10},{10,9},{13,14},{14,13},{17,18},{18,... | collective-permute-start | bytes 1179656 | tf_op jit(solution)/shard_map/ppermute | solution.py:537
  28.8 1.0 %collective-permute-done.8 = f32[80,128]{1,0:T(8,128)S(1)} collective-permute-done((f32[80,128]{1,0:T(8,128)S(1)}, f32[80,128]{1,0:T(8,128)S(1)}, u32[]{:S(2)}, u32[]{:S(2)}) %collective-permute-start.8) | collective-permute-done | bytes 40992 | tf_op jit(solution)/shard_map/ppermute | solution.py:529
  29.8 1.6 %collective-permute-start.9 = (f32[80,128]{1,0:T(8,128)S(1)}, f32[80,128]{1,0:T(8,128)S(1)}, u32[]{:S(2)}, u32[]{:S(2)}) collective-permute-start(f32[80,128]{1,0:T(8,128)S(1)} %collective-permute-done.8), channel_id=1, source_target_pairs={{0,16},{16,0},{4,20},{20,4},{8,24},{24,8},{12,28},{28,12},{1,17},{... | collective-permute-start | bytes 122888 | tf_op jit(solution)/shard_map/ppermute | solution.py:531
  31.4 2.5 %collective-permute-done.9 = f32[80,128]{1,0:T(8,128)S(1)} collective-permute-done((f32[80,128]{1,0:T(8,128)S(1)}, f32[80,128]{1,0:T(8,128)S(1)}, u32[]{:S(2)}, u32[]{:S(2)}) %collective-permute-start.9) | collective-permute-done | bytes 40992 | tf_op jit(solution)/shard_map/ppermute | solution.py:531
  33.9 0.1 halo_kernel.3
  34.0 1.8 %collective-permute-start.10 = (f32[64,128]{1,0:T(8,128)S(1)}, f32[64,128]{1,0:T(8,128)S(1)}, u32[]{:S(2)}, u32[]{:S(2)}) collective-permute-start(f32[64,128]{1,0:T(8,128)S(1)} %get-tuple-element.61.change_a), channel_id=1, source_target_pairs={{0,1},{1,0},{2,3},{3,2},{4,5},{5,4},{6,7},{7,6},{8,9},{9,8},{10,11... | collective-permute-start | bytes 98312 | tf_op jit(solution)/shard_map/ppermute | solution.py:537
  35.8 0.7 %collective-permute-start.11 = (f32[64,128]{1,0:T(8,128)S(1)}, f32[64,128]{1,0:T(8,128)S(1)}, u32[]{:S(2)}, u32[]{:S(2)}) collective-permute-start(f32[64,128]{1,0:T(8,128)S(1)} %get-tuple-element.62.change_b), channel_id=1, source_target_pairs={{1,2},{2,1},{5,6},{6,5},{9,10},{10,9},{13,14},{14,13},{17,18},{18,... | collective-permute-start | bytes 98312 | tf_op jit(solution)/shard_map/ppermute | solution.py:537
  36.5 1.1 %collective-permute-done.12.from_a = f32[3,32,8,128]{3,2,1,0:T(8,128)S(1)} collective-permute-done((f32[3,32,8,128]{3,2,1,0:T(8,128)S(1)}, f32[3,32,8,128]{3,2,1,0:T(8,128)S(1)}, u32[]{:S(2)}, u32[]{:S(2)}) %collective-permute-start.12) | collective-permute-done | bytes 393248 | tf_op jit(solution)/shard_map/ppermute | solution.py:537
  37.6 0.0 collective-permute-done.13.from_b
  37.6 0.0 copy-done.1
  37.6 0.2 mix_kernel.1
  37.8 0.2 collective-permute-done.10.got_a
  38.0 0.0 collective-permute-done.11.got_b
  38.0 1.6 %close_kernel.1 = (f32[1,3,4,8100]{3,2,1,0:T(4,128)}, f32[8,8,128]{2,1,0:T(8,128)S(1)}) custom-call(s32[32]{0:T(128)} %owner_hbm.1, f32[64,128]{1,0:T(8,128)S(1)} %get-tuple-element.61.change_a, f32[64,128]{1,0:T(8,128)S(1)} %get-tuple-element.62.change_b, f32[64,128]{1,0:T(8,128)S(1)} %collective-permute-done.10.got_a, ...), custom_call_target="tpu_custom_call" | custom-call | tf_op jit(solution)/shard_map/close_kernel/pallas_call | solution.py:577
  39.6 8.3 %all_to_all.5 = f32[8,8,128]{2,1,0:T(8,128)S(1)} all-to-all(f32[8,8,128]{2,1,0:T(8,128)S(1)} %get-tuple-element.69), channel_id=1, replica_groups=mesh['tiles'=8,'slab'=4] {'tiles'}, dimensions={0} | all-to-all | bytes 65536 | tf_op jit(solution)/shard_map/all_to_all | solution.py:585
  47.9 0.6 %slice.20 = f32[1,1,675]{2,1,0:T(1,128)} slice(f32[1,1,1024]{2,1,0:T(1,128)S(1)} %bitcast.1), slice={[0:1], [0:1], [0:675]} | slice | bytes 5400 | tf_op jit(solution)/shard_map/slice | solution.py:586
  (15 shorter events, 0.1 us)
Async XLA Ops:
  0.6 2.2 %copy-start.2 = (f32[1,4,8100]{2,1,0:T(4,128)S(1)}, f32[1,4,8100]{2,1,0:T(4,128)}, u32[]{:S(2)}) copy-start(f32[1,4,8100]{2,1,0:T(4,128)} %vertical_ref.1) | copy-start | bytes 388804
  0.6 2.1 %copy-start = (f32[3,4,8100]{2,1,0:T(4,128)S(1)}, f32[3,4,8100]{2,1,0:T(4,128)}, u32[]{:S(2)}) copy-start(f32[3,4,8100]{2,1,0:T(4,128)} %rate_ref.1) | copy-start | bytes 1166404
  2.3 1.4 %collective-permute-start = (f32[32,128]{1,0:T(8,128)S(1)}, f32[32,128]{1,0:T(8,128)S(1)}, u32[]{:S(2)}, u32[]{:S(2)}) collective-permute-start(f32[32,128]{1,0:T(8,128)S(1)} %get-tuple-element.44), channel_id=1, source_target_pairs={{0,4},{4,0},{8,12},{12,8},{16,20},{20,16},{24,28},{28,24},{1,5},{5... | collective-permute-start | bytes 49160 | tf_op jit(solution)/shard_map/ppermute | solution.py:547
  3.6 8.9 %collective-permute-start.1 = (f32[80,128]{1,0:T(8,128)S(1)}, f32[80,128]{1,0:T(8,128)S(1)}, u32[]{:S(2)}, u32[]{:S(2)}) collective-permute-start(f32[80,128]{1,0:T(8,128)S(1)} %pad_maximum_fusion), channel_id=1, source_target_pairs={{0,8},{8,0},{4,12},{12,4},{16,24},{24,16},{20,28},{28,20},{1,9},{9... | collective-permute-start | bytes 122888 | tf_op jit(solution)/shard_map/ppermute | solution.py:529
  6.5 11.1 %collective-permute-start.5 = (f32[4,32,8,128]{3,2,1,0:T(8,128)S(1)}, f32[4,32,8,128]{3,2,1,0:T(8,128)S(1)}, u32[]{:S(2)}, u32[]{:S(2)}) collective-permute-start(f32[4,32,8,128]{3,2,1,0:T(8,128)S(1)} %get-tuple-element.46.pack_b), channel_id=1, source_target_pairs={{1,2},{2,1},{5,6},{6,5},{9,10},{10,9},{13,14},{14,13},{17,18},{18,... | collective-permute-start | bytes 1572872 | tf_op jit(solution)/shard_map/ppermute | solution.py:537
  7.2 16.5 %collective-permute-start.6 = (f32[4,32,8,128]{3,2,1,0:T(8,128)S(1)}, f32[4,32,8,128]{3,2,1,0:T(8,128)S(1)}, u32[]{:S(2)}, u32[]{:S(2)}) collective-permute-start(f32[4,32,8,128]{3,2,1,0:T(8,128)S(1)} %get-tuple-element.45.pack_a), channel_id=1, source_target_pairs={{0,1},{1,0},{2,3},{3,2},{4,5},{5,4},{6,7},{7,6},{8,9},{9,8},{10,11... | collective-permute-start | bytes 1572872 | tf_op jit(solution)/shard_map/ppermute | solution.py:537
  12.6 4.1 %collective-permute-start.2 = (f32[80,128]{1,0:T(8,128)S(1)}, f32[80,128]{1,0:T(8,128)S(1)}, u32[]{:S(2)}, u32[]{:S(2)}) collective-permute-start(f32[80,128]{1,0:T(8,128)S(1)} %collective-permute-done.1), channel_id=1, source_target_pairs={{0,16},{16,0},{4,20},{20,4},{8,24},{24,8},{12,28},{28,12},{1,17},{... | collective-permute-start | bytes 122888 | tf_op jit(solution)/shard_map/ppermute | solution.py:531
  16.8 7.2 %collective-permute-start.3 = (f32[64,128]{1,0:T(8,128)S(1)}, f32[64,128]{1,0:T(8,128)S(1)}, u32[]{:S(2)}, u32[]{:S(2)}) collective-permute-start(f32[64,128]{1,0:T(8,128)S(1)} %get-tuple-element.52.change_a), channel_id=1, source_target_pairs={{0,1},{1,0},{2,3},{3,2},{4,5},{5,4},{6,7},{7,6},{8,9},{9,8},{10,11... | collective-permute-start | bytes 98312 | tf_op jit(solution)/shard_map/ppermute | solution.py:537
  16.9 7.1 %collective-permute-start.4 = (f32[64,128]{1,0:T(8,128)S(1)}, f32[64,128]{1,0:T(8,128)S(1)}, u32[]{:S(2)}, u32[]{:S(2)}) collective-permute-start(f32[64,128]{1,0:T(8,128)S(1)} %get-tuple-element.53.change_b), channel_id=1, source_target_pairs={{1,2},{2,1},{5,6},{6,5},{9,10},{10,9},{13,14},{14,13},{17,18},{18,... | collective-permute-start | bytes 98312 | tf_op jit(solution)/shard_map/ppermute | solution.py:537
  24.6 1.2 %collective-permute-start.7 = (f32[32,128]{1,0:T(8,128)S(1)}, f32[32,128]{1,0:T(8,128)S(1)}, u32[]{:S(2)}, u32[]{:S(2)}) collective-permute-start(f32[32,128]{1,0:T(8,128)S(1)} %get-tuple-element.59), channel_id=1, source_target_pairs={{0,4},{4,0},{8,12},{12,8},{16,20},{20,16},{24,28},{28,24},{1,5},{5... | collective-permute-start | bytes 49160 | tf_op jit(solution)/shard_map/ppermute | solution.py:566
  25.1 12.5 %copy-start.1 = (f32[1,3,4,8100]{3,2,1,0:T(4,128)S(1)}, f32[1,3,4,8100]{3,2,1,0:T(4,128)}, u32[]{:S(2)}) copy-start(f32[1,3,4,8100]{3,2,1,0:T(4,128)} %state_ref.1) | copy-start | bytes 1166404
  25.8 4.0 %collective-permute-start.8 = (f32[80,128]{1,0:T(8,128)S(1)}, f32[80,128]{1,0:T(8,128)S(1)}, u32[]{:S(2)}, u32[]{:S(2)}) collective-permute-start(f32[80,128]{1,0:T(8,128)S(1)} %pad_maximum_fusion.1), channel_id=1, source_target_pairs={{0,8},{8,0},{4,12},{12,4},{16,24},{24,16},{20,28},{28,20},{1,9},{9... | collective-permute-start | bytes 122888 | tf_op jit(solution)/shard_map/ppermute | solution.py:529
  26.3 11.3 %collective-permute-start.12 = (f32[3,32,8,128]{3,2,1,0:T(8,128)S(1)}, f32[3,32,8,128]{3,2,1,0:T(8,128)S(1)}, u32[]{:S(2)}, u32[]{:S(2)}) collective-permute-start(f32[3,32,8,128]{3,2,1,0:T(8,128)S(1)} %inner_kernel.1.taken_ref), channel_id=1, source_target_pairs={{0,1},{1,0},{2,3},{3,2},{4,5},{5,4},{6,7},{7,6},{8,9},{9,8},{10,11... | collective-permute-start | bytes 1179656 | tf_op jit(solution)/shard_map/ppermute | solution.py:537
  28.1 9.5 %collective-permute-start.13 = (f32[3,32,8,128]{3,2,1,0:T(8,128)S(1)}, f32[3,32,8,128]{3,2,1,0:T(8,128)S(1)}, u32[]{:S(2)}, u32[]{:S(2)}) collective-permute-start(f32[3,32,8,128]{3,2,1,0:T(8,128)S(1)} %inner_kernel.1.taken_ref), channel_id=1, source_target_pairs={{1,2},{2,1},{5,6},{6,5},{9,10},{10,9},{13,14},{14,13},{17,18},{18,... | collective-permute-start | bytes 1179656 | tf_op jit(solution)/shard_map/ppermute | solution.py:537
  29.8 4.1 %collective-permute-start.9 = (f32[80,128]{1,0:T(8,128)S(1)}, f32[80,128]{1,0:T(8,128)S(1)}, u32[]{:S(2)}, u32[]{:S(2)}) collective-permute-start(f32[80,128]{1,0:T(8,128)S(1)} %collective-permute-done.8), channel_id=1, source_target_pairs={{0,16},{16,0},{4,20},{20,4},{8,24},{24,8},{12,28},{28,12},{1,17},{... | collective-permute-start | bytes 122888 | tf_op jit(solution)/shard_map/ppermute | solution.py:531
  34.0 4.0 %collective-permute-start.10 = (f32[64,128]{1,0:T(8,128)S(1)}, f32[64,128]{1,0:T(8,128)S(1)}, u32[]{:S(2)}, u32[]{:S(2)}) collective-permute-start(f32[64,128]{1,0:T(8,128)S(1)} %get-tuple-element.61.change_a), channel_id=1, source_target_pairs={{0,1},{1,0},{2,3},{3,2},{4,5},{5,4},{6,7},{7,6},{8,9},{9,8},{10,11... | collective-permute-start | bytes 98312 | tf_op jit(solution)/shard_map/ppermute | solution.py:537
  35.8 2.2 %collective-permute-start.11 = (f32[64,128]{1,0:T(8,128)S(1)}, f32[64,128]{1,0:T(8,128)S(1)}, u32[]{:S(2)}, u32[]{:S(2)}) collective-permute-start(f32[64,128]{1,0:T(8,128)S(1)} %get-tuple-element.62.change_b), channel_id=1, source_target_pairs={{1,2},{2,1},{5,6},{6,5},{9,10},{10,9},{13,14},{14,13},{17,18},{18,... | collective-permute-start | bytes 98312 | tf_op jit(solution)/shard_map/ppermute | solution.py:537

commit v5 on v4

--- a/solution.py
+++ b/solution.py
@@ -22,10 +22,8 @@
 ROWS = SPOTS * CHANNELS
 TILE_ROWS = SIDES * CHANNELS
 SHOWN = ROWS + TILE_ROWS
-OWN = 0 + SHOWN
-ODD = 0 + SHOWN + SHOWN
-EVEN = 0
-OTHER = 0 + SHOWN + SHOWN + SHOWN
+FIRST = {"odd": 0, "even": SHOWN, "shown": SHOWN + SHOWN, "other": SHOWN + SHOWN + SHOWN}
+SECOND = {"even": 0, "shown": SHOWN, "odd": SHOWN + SHOWN, "other": SHOWN + SHOWN + SHOWN}
 CLOSED = -8
 TURNED = 1 << 16
 FIRST_HIGH = HALF // TILE
@@ -136,7 +134,7 @@
     return ref[pl.ds(channel, SPOTS, stride=CHANNELS), :]
 
 
-def halo_places(table_ref, out_ref):
+def halo_places(table_ref, out_ref, layout):
     me = lax.axis_index("tiles")
     chip, core = me // 2, me % 2
     even = chip % 2 == 0
@@ -147,8 +145,8 @@
             tile, link = code >> 3, code & 7
             device, inner = tile // TILES, tile % TILES
             step = device // 2 - chip
-            start = jnp.where((step == 1) == even, EVEN, ODD)
-            own = jnp.where(device == me, OWN + inner * TILE_ROWS, OTHER)
+            start = jnp.where((step == 1) == even, layout["even"], layout["odd"])
+            own = jnp.where(device == me, layout["shown"] + inner * TILE_ROWS, layout["other"])
             beside = start + jnp.where(device % 2 == core, inner * TILE_ROWS, ROWS)
             row = jnp.where(step == 0, own, beside) + (link // 2) * CHANNELS
             places.append(jnp.where(code < 0, CLOSED, row + (link % 2) * TURNED))
@@ -158,14 +156,14 @@
         out_ref[pl.ds(k * CHANNELS, 8), :] = jnp.where(low, places[k], places[k + 1]) + channel
 
 
-def halos(place_ref, all_ref, out_ref):
+def halos(place_ref, all_ref, out_ref, layout):
     lane, _ = position()
     back = jnp.clip(TILE - 1 - lane, 0, LANES - 1)
     for t in range(TILES):
-        starts = [start + t * TILE_ROWS for start in (ODD, EVEN)]
-        starts += [OWN + k * TILE_ROWS for k in (t - 1, t + 1) if 0 <= k < TILES]
+        starts = [start + t * TILE_ROWS for start in (layout["odd"], layout["even"])]
+        starts += [layout["shown"] + k * TILE_ROWS for k in (t - 1, t + 1) if 0 <= k < TILES]
         if t in (0, TILES - 1):
-            starts += [OTHER, ODD + ROWS, EVEN + ROWS]
+            starts += [layout["other"], layout["odd"] + ROWS, layout["even"] + ROWS]
         chunks = [start // 8 + k for start in starts for k in range(TILE_ROWS // 8)]
         for h in range(TILE_ROWS // 8):
             at = pl.ds(t * TILE_ROWS + h * 8, 8)
@@ -268,7 +266,12 @@
 
 def inner_first_kernel(spread, lam_ref, wet_ref, mixing_ref, vertical_ref, rate_ref, pack_a, pack_b, stay_ref, keep_ref):
     tracers = lam_ref.shape[0]
-    even = lax.axis_index("slab") % 2 == 0
+    level, levels = lax.axis_index("slab"), lax.axis_size("slab")
+    even = level % 2 == 0
+    has_a = (level // 2 * 2 + 1 < levels).astype(F32)
+    has_b = ((level >= 1) & ((level + 1) // 2 * 2 < levels)).astype(F32)
+    for_a = has_a * jnp.where(even, 1.0, 0.0), has_a * jnp.where(even, 0.0, 1.0)
+    for_b = has_b * jnp.where(even, 0.0, 1.0), has_b * jnp.where(even, 1.0, 0.0)
     lane, low = position()
     fold(lambda a, n: vertical_ref[0, :, a : a + n], write_to(stay_ref))
     for c in range(tracers):
@@ -278,8 +281,8 @@
         x, _ = cell_at(lane, low, v)
         west, east = x == 0, x == TILE - 1
         wet, vertical = wet_ref[v], stay_ref[v]
-        pack_a[tracers, v] = wet * jnp.where(even, 1.0, vertical)
-        pack_b[tracers, v] = wet * jnp.where(even, vertical, 1.0)
+        pack_a[tracers, v] = wet * (for_a[0] + for_a[1] * vertical)
+        pack_b[tracers, v] = wet * (for_b[0] + for_b[1] * vertical)
         stay = 1.0 - mixing_ref[v] * inner_sum(spread, tracers, v, lane, west, east)
         stay_ref[v] = stay
         for c in range(tracers):
@@ -308,10 +311,11 @@
     loop(body)
 
 
-def fixed_kernel(table_ref, keep_ref, pack_a, pack_b, out_a, out_b, place_ref):
+def fixed_kernel(table_ref, keep_ref, pack_a, pack_b, out_a, out_b, first_ref, second_ref):
     tracers = keep_ref.shape[0]
     lane, low = position()
-    halo_places(table_ref, place_ref)
+    halo_places(table_ref, first_ref, FIRST)
+    halo_places(table_ref, second_ref, SECOND)
 
     def load(p, v):
         return keep_ref[p, v] if p < tracers else (pack_a if p == tracers else pack_b)[tracers, v]
@@ -324,9 +328,9 @@
     put_sides(out_b, tracers, found[tracers + 1])
 
 
-def halo_kernel(place_ref, all_ref, edge_ref, fixed_a, fixed_b, out_a, out_b, halo_ref):
+def halo_kernel(layout, place_ref, all_ref, edge_ref, fixed_a, fixed_b, out_a, out_b, halo_ref):
     tracers = CHANNELS - 1
-    halos(place_ref, all_ref, halo_ref)
+    halos(place_ref, all_ref, halo_ref, layout)
     wet, halo_wet = channel_rows(edge_ref, tracers), channel_rows(halo_ref, tracers)
     for c in range(tracers):
         change = channel_rows(fixed_a, c) * (wet * channel_rows(halo_ref, c) - channel_rows(edge_ref, c) * halo_wet)
@@ -506,15 +510,19 @@
         out_specs=outs or [VMEM] * len(out),
         scratch_shapes=[pltpu.VMEM(shape, F32) if isinstance(shape, tuple) else shape for shape in scratch],
         compiler_params=pltpu.CompilerParams(vmem_limit_bytes=32 * 1024 * 1024),
-        name=kernel.__name__,
+        name=getattr(kernel, "func", kernel).__name__,
     )
 
 
 def shards(adjoint, state, weights, vertical, mask, rate, neighbours, links, owners):
     tracers = adjoint.shape[1]
     number = lax.axis_size("tiles")
-    even_swap, odd_swap = swaps(lax.axis_size("slab"))
+    levels = lax.axis_size("slab")
+    even_swap, odd_swap = ([(k * levels + i, k * levels + j) for i, j in pairs for k in range(number)] for pairs in swaps(levels))
     core_swap = [(2 * i + a, 2 * i + 1 - a) for i in range(number // 2) for a in range(2)]
+    for pairs in (even_swap, odd_swap):
+        alone = set(range(levels)) - {i % levels for i, _ in pairs}
+        pairs.extend((a * levels + i, b * levels + i) for i in sorted(alone) for a, b in core_swap)
     even_chips, odd_chips = swaps(number, 2)
     passing = swaps(number, 4)[0]
     plane = (COLS, 8, LANES)
@@ -524,17 +532,18 @@
     edges = (ROWS, LANES)
     given = (2 * TILE_ROWS, LANES)
 
-    def around(edge, other):
+    def around(edge, other, layout):
         shown = jnp.concatenate([edge, other[:TILE_ROWS]])
         even = lax.ppermute(shown, "tiles", even_chips)
         if number == 8:
             odd = lax.ppermute(even, "tiles", passing)
         else:
             odd = lax.ppermute(shown, "tiles", odd_chips)
-        return jnp.concatenate([even, shown, odd, other[TILE_ROWS:]])
+        parts = {"even": even, "shown": shown, "odd": odd, "other": other[TILE_ROWS:]}
+        return jnp.concatenate([parts[name] for name in layout])
 
     def across(first, second):
-        return lax.ppermute(first, "slab", even_swap), lax.ppermute(second, "slab", odd_swap)
+        return lax.ppermute(first, ("tiles", "slab"), even_swap), lax.ppermute(second, ("tiles", "slab"), odd_swap)
 
     edge, give, lam, wet, mixing, spread, table = call(
         open_kernel,
@@ -550,12 +559,15 @@
     )
     pack_a, pack_b, other = lax.optimization_barrier((pack_a, pack_b, other))
     from_a, from_b = across(pack_a, pack_b)
-    near = around(edge, other)
-    fixed_a, fixed_b, places = call(
-        fixed_kernel, [SMEM] + [VMEM] * 3, [edges] * 2 + [jax.ShapeDtypeStruct(edges, I32)], []
+    near = around(edge, other, FIRST)
+    fixed_a, fixed_b, first, second = call(
+        fixed_kernel, [SMEM] + [VMEM] * 3, [edges] * 2 + [jax.ShapeDtypeStruct(edges, I32)] * 2, []
     )(table, keep, pack_a, pack_b)
-    halo = call(halo_kernel, [VMEM] * 5, [edges] * 2, [edges])
-    change_a, change_b = halo(places, near, edge, fixed_a, fixed_b)
+
+    def halo(layout, *args):
+        return call(functools.partial(halo_kernel, layout), [VMEM] * 5, [edges] * 2, [edges])(*args)
+
+    change_a, change_b = halo(FIRST, first, near, edge, fixed_a, fixed_b)
     got_a, got_b = across(change_a, change_b)
     before, mix_a, mix_b = call(mix_first_kernel, [VMEM] * 4, [planes, plane, plane], [])(
         pack_a, pack_b, from_b, from_a
@@ -567,8 +579,8 @@
     (taken,) = call(inner_kernel, [VMEM] * 5, [planes], [])(spread, lam, wet, stay, keep)
     taken, other = lax.optimization_barrier((taken, other))
     from_a, from_b = across(taken, taken)
-    near = around(edge, other)
-    change_a, change_b = halo(places, near, edge, fixed_a, fixed_b)
+    near = around(edge, other, SECOND)
+    change_a, change_b = halo(SECOND, second, near, edge, fixed_a, fixed_b)
     got_a, got_b = across(change_a, change_b)
     before, weighted = call(mix_kernel, [VMEM] * 7, [planes, planes], [])(
         taken, from_a, from_b, mix_a, mix_b, wet, state

time: 49.4 us -> 45.6 us (0.923); the launches traced: 48.5 us -> 45.4 us
  starting transfers between devices: 17.8 us -> 14.9 us
  blocking collectives: 8.32 us -> 7.45 us
    ppermute x8, starting transfers between devices: 10.7 us -> 8.2 us  [the longest x4 7.83 us: across(): lax.ppermute(first, ('tiles', 'slab'), even_swap)]
    ppermute x2, waiting for transfers between devices: 1.05 us -> 3.27 us  [around(): even = lax.ppermute(shown, 'tiles', even_chips)]
    ppermute x2, waiting for transfers between devices: 4.96 us -> 3.65 us  [around(): odd = lax.ppermute(even, 'tiles', passing)]
    all_to_all x1, blocking collectives: 8.32 us -> 7.45 us  [shards(): part = lax.all_to_all(part, 'tiles', 0, 0, tiled=True)]
    ppermute x8, waiting for transfers between devices: 7.7 us -> 7.16 us  [the longest x4 7.15 us: across(): lax.ppermute(first, ('tiles', 'slab'), even_swap)]
  transfers between devices with their start and end apart: 14 -> 14, of which waited for: 9 -> 10; matrix products, arithmetic and copies ran while one was open for 0% -> 0% of each run, Pallas kernels for 5% -> 6%
where the time goes in v5:
time: 45.6 us; the launch traced here: 45.4 us
  starting transfers between devices  14.9 us (33%)
  waiting for transfers between devices  14.9 us (33%)
  blocking collectives  7.45 us (16%)
  Pallas kernels  6.7 us (15%)
  between operations  0.75 us (2%)
  local copies, waits for them, and re-layouts  0.61 us (1%)
    ppermute x4, starting transfers between devices, across(): lax.ppermute(first, ('tiles', 'slab'), even_swap)  7.83 us
    all_to_all x1, blocking collectives, shards(): part = lax.all_to_all(part, 'tiles', 0, 0, tiled=True)  7.45 us
    ppermute x4, waiting for transfers between devices, across(): lax.ppermute(first, ('tiles', 'slab'), even_swap)  7.15 us
    ppermute x2, waiting for transfers between devices, around(): odd = lax.ppermute(even, 'tiles', passing)  3.65 us
    ppermute x2, waiting for transfers between devices, around(): even = lax.ppermute(shown, 'tiles', even_chips)  3.27 us
    ppermute x2, starting transfers between devices, around(): odd = lax.ppermute(even, 'tiles', passing)  3.1 us
    ppermute x2, starting transfers between devices, around(): even = lax.ppermute(shown, 'tiles', even_chips)  2.98 us
    pallas_call x1, Pallas kernels, shards(): call(open_kernel, [HBM] * 5, [edges, given, planes, plane, plane, (tracer...  1.61 us
  transfers between devices with their start and end apart: 14, of which 10 were waited for; matrix products, arithmetic and copies ran while one was open for 0% of the time, Pallas kernels for 6%

profile of v5, /device:TPU:0, one launch (start us, length us, event | category | flops | bytes accessed | tf_op | source)
XLA Modules:
  0.0 45.4 jit_solution(219967464702615897)
XLA Ops:
  0.6 0.0 copy-start.2
  0.6 0.0 copy-start
  0.7 1.6 %open_kernel.1 = (f32[64,128]{1,0:T(8,128)S(1)}, f32[32,128]{1,0:T(8,128)S(1)}, f32[3,32,8,128]{3,2,1,0:T(8,128)S(1)}, f32[32,8,128]{2,1,0:T(8,128)S(1)}, f32[32...) custom-call(f32[1,3,4,8100]{3,2,1,0:T(4,128)} %adjoint_hbm.1, f32[1,4,8100]{2,1,0:T(4,128)} %weights_hbm.1, ...), custom_call_target="tpu_custom_call" | custom-call | tf_op jit(solution)/shard_map/open_kernel/pallas_call | solution.py:548
  2.3 0.5 %collective-permute-start = (f32[32,128]{1,0:T(8,128)S(1)}, f32[32,128]{1,0:T(8,128)S(1)}, u32[]{:S(2)}, u32[]{:S(2)}) collective-permute-start(f32[32,128]{1,0:T(8,128)S(1)} %get-tuple-element.45), channel_id=1, source_target_pairs={{0,4},{4,0},{8,12},{12,8},{16,20},{20,16},{24,28},{28,24},{1,5},{5... | collective-permute-start | bytes 49160 | tf_op jit(solution)/shard_map/ppermute | solution.py:556
  2.8 0.0 copy-done.2
  2.8 0.0 copy-done
  2.8 0.7 %inner_first_kernel.1 = (f32[4,32,8,128]{3,2,1,0:T(8,128)S(1)}, f32[4,32,8,128]{3,2,1,0:T(8,128)S(1)}, f32[32,8,128]{2,1,0:T(8,128)S(1)}, f32[3,32,8,128]{3,2,1,0:T(8,128)S(1)}) custom-call(f32[4,34,8,128]{3,2,1,0:T(8,128)S(1)} %get-tuple-element.38.spread, f32[3,32,8,128]{3,2,1,0:T(8,128)S(1)} %get-tuple-element.39.lam_ref, ...), custom_call_target="tpu_custom_call" | custom-call | tf_op jit(solution)/shard_map/inner_first_kernel/pallas_call | solution.py:557
  3.4 0.2 collective-permute-done
  3.6 0.3 collective-permute-start.5
  4.0 4.1 %collective-permute-start.6 = (f32[4,32,8,128]{3,2,1,0:T(8,128)S(1)}, f32[4,32,8,128]{3,2,1,0:T(8,128)S(1)}, u32[]{:S(2)}, u32[]{:S(2)}) collective-permute-start(f32[4,32,8,128]{3,2,1,0:T(8,128)S(1)} %get-tuple-element.46.pack_a), channel_id=1, source_target_pairs={{0,1},{4,5},{8,9},{12,13},{16,17},{20,21},{24,25},{28,29},{1,0},{5... | collective-permute-start | bytes 1572872 | tf_op jit(solution)/shard_map/ppermute | solution.py:546
  8.1 1.5 %collective-permute-start.1 = (f32[80,128]{1,0:T(8,128)S(1)}, f32[80,128]{1,0:T(8,128)S(1)}, u32[]{:S(2)}, u32[]{:S(2)}) collective-permute-start(f32[80,128]{1,0:T(8,128)S(1)} %pad_maximum_fusion.1), channel_id=1, source_target_pairs={{0,8},{8,0},{4,12},{12,4},{16,24},{24,16},{20,28},{28,20},{1,9},{9... | collective-permute-start | bytes 122888 | tf_op jit(solution)/shard_map/ppermute | solution.py:537
  9.6 2.5 %collective-permute-done.1 = f32[80,128]{1,0:T(8,128)S(1)} collective-permute-done((f32[80,128]{1,0:T(8,128)S(1)}, f32[80,128]{1,0:T(8,128)S(1)}, u32[]{:S(2)}, u32[]{:S(2)}) %collective-permute-start.1) | collective-permute-done | bytes 40992 | tf_op jit(solution)/shard_map/ppermute | solution.py:537
  12.1 1.5 %collective-permute-start.2 = (f32[80,128]{1,0:T(8,128)S(1)}, f32[80,128]{1,0:T(8,128)S(1)}, u32[]{:S(2)}, u32[]{:S(2)}) collective-permute-start(f32[80,128]{1,0:T(8,128)S(1)} %collective-permute-done.1), channel_id=1, source_target_pairs={{0,16},{16,0},{4,20},{20,4},{8,24},{24,8},{12,28},{28,12},{1,17},{... | collective-permute-start | bytes 122888 | tf_op jit(solution)/shard_map/ppermute | solution.py:539
  13.6 1.3 %fixed_kernel.1 = (f32[64,128]{1,0:T(8,128)S(1)}, f32[64,128]{1,0:T(8,128)S(1)}, s32[64,128]{1,0:T(8,128)S(1)}, s32[64,128]{1,0:T(8,128)S(1)}) custom-call(s32[4,4]{1,0:T(4,128)S(1)} %get-tuple-element.37.table_ref, f32[3,32,8,128]{3,2,1,0:T(8,128)S(1)} %get-tuple-element.42.keep_ref, f32[4,32,8,128]{3,2,1,0:T(8,128)S(1)} %get-tuple-element.46.pack_a, ...), custom_call_target="tpu_custom_call" | custom-call | tf_op jit(solution)/shard_map/fixed_kernel/pallas_call | solution.py:563
  15.0 1.2 %collective-permute-done.2 = f32[80,128]{1,0:T(8,128)S(1)} collective-permute-done((f32[80,128]{1,0:T(8,128)S(1)}, f32[80,128]{1,0:T(8,128)S(1)}, u32[]{:S(2)}, u32[]{:S(2)}) %collective-permute-start.2) | collective-permute-done | bytes 40992 | tf_op jit(solution)/shard_map/ppermute | solution.py:539
  16.1 0.1 halo_kernel.2
  16.3 0.1 collective-permute-start.3
  16.4 0.0 collective-permute-start.4
  16.4 0.0 collective-permute-done.5.from_b
  16.4 4.0 %collective-permute-done.6.from_a = f32[4,32,8,128]{3,2,1,0:T(8,128)S(1)} collective-permute-done((f32[4,32,8,128]{3,2,1,0:T(8,128)S(1)}, f32[4,32,8,128]{3,2,1,0:T(8,128)S(1)}, u32[]{:S(2)}, u32[]{:S(2)}) %collective-permute-start.6) | collective-permute-done | bytes 524320 | tf_op jit(solution)/shard_map/ppermute | solution.py:546
  20.4 0.1 mix_first_kernel.1
  20.5 0.3 collective-permute-done.3.got_a
  20.8 0.0 collective-permute-done.4.got_b
  20.8 0.6 %middle_kernel.1 = (f32[64,128]{1,0:T(8,128)S(1)}, f32[32,128]{1,0:T(8,128)S(1)}, f32[3,32,8,128]{3,2,1,0:T(8,128)S(1)}, f32[3,34,8,128]{3,2,1,0:T(8,128)S(1)}) custom-call(f32[64,128]{1,0:T(8,128)S(1)} %get-tuple-element.54.change_a, f32[64,128]{1,0:T(8,128)S(1)} %get-tuple-element.55.change_b, f32[64,128]{1,0:T(8,128)S(1)} %collective-permute-done.3.got_a, ...), custom_call_target="tpu_custom_call" | custom-call | tf_op jit(solution)/shard_map/middle_kernel/pallas_call | solution.py:575
  21.4 0.1 collective-permute-start.7
  21.4 0.5 %inner_kernel.1.taken_ref = f32[3,32,8,128]{3,2,1,0:T(8,128)S(1)} custom-call(f32[3,34,8,128]{3,2,1,0:T(8,128)S(1)} %get-tuple-element.58.spread, f32[3,32,8,128]{3,2,1,0:T(8,128)S(1)} %get-tuple-element.59.lam_ref, f32[32,8,128]{2,1,0:T(8,128)S(1)} %get-tuple-element.40.wet_ref, f32[32,8,128]{2,1,0:T(8,128)S(1)} %get-tuple-element.60.stay_ref, ...), custom_call_target="tpu_custom_call" | custom-call | tf_op jit(solution)/shard_map/inner_kernel/pallas_call | solution.py:579
  21.9 0.0 copy-start.1
  21.9 0.7 %collective-permute-done.7 = f32[32,128]{1,0:T(8,128)S(1)} collective-permute-done((f32[32,128]{1,0:T(8,128)S(1)}, f32[32,128]{1,0:T(8,128)S(1)}, u32[]{:S(2)}, u32[]{:S(2)}) %collective-permute-start.7) | collective-permute-done | bytes 16416 | tf_op jit(solution)/shard_map/ppermute | solution.py:578
  22.6 1.5 %collective-permute-start.8 = (f32[80,128]{1,0:T(8,128)S(1)}, f32[80,128]{1,0:T(8,128)S(1)}, u32[]{:S(2)}, u32[]{:S(2)}) collective-permute-start(f32[80,128]{1,0:T(8,128)S(1)} %pad_maximum_fusion.2), channel_id=1, source_target_pairs={{0,8},{8,0},{4,12},{12,4},{16,24},{24,16},{20,28},{28,20},{1,9},{9... | collective-permute-start | bytes 122888 | tf_op jit(solution)/shard_map/ppermute | solution.py:537
  24.1 1.7 %collective-permute-start.12 = (f32[3,32,8,128]{3,2,1,0:T(8,128)S(1)}, f32[3,32,8,128]{3,2,1,0:T(8,128)S(1)}, u32[]{:S(2)}, u32[]{:S(2)}) collective-permute-start(f32[3,32,8,128]{3,2,1,0:T(8,128)S(1)} %inner_kernel.1.taken_ref), channel_id=1, source_target_pairs={{0,1},{4,5},{8,9},{12,13},{16,17},{20,21},{24,25},{28,29},{1,0},{5... | collective-permute-start | bytes 1179656 | tf_op jit(solution)/shard_map/ppermute | solution.py:546
  25.9 0.0 collective-permute-start.13
  25.9 0.8 %collective-permute-done.8 = f32[80,128]{1,0:T(8,128)S(1)} collective-permute-done((f32[80,128]{1,0:T(8,128)S(1)}, f32[80,128]{1,0:T(8,128)S(1)}, u32[]{:S(2)}, u32[]{:S(2)}) %collective-permute-start.8) | collective-permute-done | bytes 40992 | tf_op jit(solution)/shard_map/ppermute | solution.py:537
  26.6 1.6 %collective-permute-start.9 = (f32[80,128]{1,0:T(8,128)S(1)}, f32[80,128]{1,0:T(8,128)S(1)}, u32[]{:S(2)}, u32[]{:S(2)}) collective-permute-start(f32[80,128]{1,0:T(8,128)S(1)} %collective-permute-done.8), channel_id=1, source_target_pairs={{0,16},{16,0},{4,20},{20,4},{8,24},{24,8},{12,28},{28,12},{1,17},{... | collective-permute-start | bytes 122888 | tf_op jit(solution)/shard_map/ppermute | solution.py:539
  28.2 2.5 %collective-permute-done.9 = f32[80,128]{1,0:T(8,128)S(1)} collective-permute-done((f32[80,128]{1,0:T(8,128)S(1)}, f32[80,128]{1,0:T(8,128)S(1)}, u32[]{:S(2)}, u32[]{:S(2)}) %collective-permute-start.9) | collective-permute-done | bytes 40992 | tf_op jit(solution)/shard_map/ppermute | solution.py:539
  30.7 0.1 halo_kernel.3
  30.8 1.8 %collective-permute-start.10 = (f32[64,128]{1,0:T(8,128)S(1)}, f32[64,128]{1,0:T(8,128)S(1)}, u32[]{:S(2)}, u32[]{:S(2)}) collective-permute-start(f32[64,128]{1,0:T(8,128)S(1)} %get-tuple-element.63.change_a), channel_id=1, source_target_pairs={{0,1},{4,5},{8,9},{12,13},{16,17},{20,21},{24,25},{28,29},{1,0},{5... | collective-permute-start | bytes 98312 | tf_op jit(solution)/shard_map/ppermute | solution.py:546
  32.6 0.0 collective-permute-start.11
  32.6 2.7 %collective-permute-done.12.from_a = f32[3,32,8,128]{3,2,1,0:T(8,128)S(1)} collective-permute-done((f32[3,32,8,128]{3,2,1,0:T(8,128)S(1)}, f32[3,32,8,128]{3,2,1,0:T(8,128)S(1)}, u32[]{:S(2)}, u32[]{:S(2)}) %collective-permute-start.12) | collective-permute-done | bytes 393248 | tf_op jit(solution)/shard_map/ppermute | solution.py:546
  35.4 0.0 collective-permute-done.13.from_b
  35.4 0.0 copy-done.1
  35.4 0.2 mix_kernel.1
  35.5 0.2 collective-permute-done.10.got_a
  35.7 0.0 collective-permute-done.11.got_b
  35.7 1.6 %close_kernel.1 = (f32[1,3,4,8100]{3,2,1,0:T(4,128)}, f32[8,8,128]{2,1,0:T(8,128)S(1)}) custom-call(s32[32]{0:T(128)} %owner_hbm.1, f32[64,128]{1,0:T(8,128)S(1)} %get-tuple-element.63.change_a, f32[64,128]{1,0:T(8,128)S(1)} %get-tuple-element.64.change_b, f32[64,128]{1,0:T(8,128)S(1)} %collective-permute-done.10.got_a, ...), custom_call_target="tpu_custom_call" | custom-call | tf_op jit(solution)/shard_map/close_kernel/pallas_call | solution.py:589
  37.3 7.5 %all_to_all.5 = f32[8,8,128]{2,1,0:T(8,128)S(1)} all-to-all(f32[8,8,128]{2,1,0:T(8,128)S(1)} %get-tuple-element.71), channel_id=1, replica_groups=mesh['tiles'=8,'slab'=4] {'tiles'}, dimensions={0} | all-to-all | bytes 65536 | tf_op jit(solution)/shard_map/all_to_all | solution.py:597
  44.8 0.6 %slice.18 = f32[1,1,675]{2,1,0:T(1,128)} slice(f32[1,1,1024]{2,1,0:T(1,128)S(1)} %bitcast.1), slice={[0:1], [0:1], [0:675]} | slice | bytes 5400 | tf_op jit(solution)/shard_map/slice | solution.py:598
  (11 shorter events, 0.0 us)
Async XLA Ops:
  0.6 2.2 %copy-start.2 = (f32[1,4,8100]{2,1,0:T(4,128)S(1)}, f32[1,4,8100]{2,1,0:T(4,128)}, u32[]{:S(2)}) copy-start(f32[1,4,8100]{2,1,0:T(4,128)} %vertical_ref.1) | copy-start | bytes 388804
  0.6 2.1 %copy-start = (f32[3,4,8100]{2,1,0:T(4,128)S(1)}, f32[3,4,8100]{2,1,0:T(4,128)}, u32[]{:S(2)}) copy-start(f32[3,4,8100]{2,1,0:T(4,128)} %rate_ref.1) | copy-start | bytes 1166404
  2.3 1.4 %collective-permute-start = (f32[32,128]{1,0:T(8,128)S(1)}, f32[32,128]{1,0:T(8,128)S(1)}, u32[]{:S(2)}, u32[]{:S(2)}) collective-permute-start(f32[32,128]{1,0:T(8,128)S(1)} %get-tuple-element.45), channel_id=1, source_target_pairs={{0,4},{4,0},{8,12},{12,8},{16,20},{20,16},{24,28},{28,24},{1,5},{5... | collective-permute-start | bytes 49160 | tf_op jit(solution)/shard_map/ppermute | solution.py:556
  3.6 12.8 %collective-permute-start.5 = (f32[4,32,8,128]{3,2,1,0:T(8,128)S(1)}, f32[4,32,8,128]{3,2,1,0:T(8,128)S(1)}, u32[]{:S(2)}, u32[]{:S(2)}) collective-permute-start(f32[4,32,8,128]{3,2,1,0:T(8,128)S(1)} %get-tuple-element.47.pack_b), channel_id=1, source_target_pairs={{1,2},{5,6},{9,10},{13,14},{17,18},{21,22},{25,26},{29,30},{2,1},{... | collective-permute-start | bytes 1572872 | tf_op jit(solution)/shard_map/ppermute | solution.py:546
  4.0 16.5 %collective-permute-start.6 = (f32[4,32,8,128]{3,2,1,0:T(8,128)S(1)}, f32[4,32,8,128]{3,2,1,0:T(8,128)S(1)}, u32[]{:S(2)}, u32[]{:S(2)}) collective-permute-start(f32[4,32,8,128]{3,2,1,0:T(8,128)S(1)} %get-tuple-element.46.pack_a), channel_id=1, source_target_pairs={{0,1},{4,5},{8,9},{12,13},{16,17},{20,21},{24,25},{28,29},{1,0},{5... | collective-permute-start | bytes 1572872 | tf_op jit(solution)/shard_map/ppermute | solution.py:546
  8.1 4.0 %collective-permute-start.1 = (f32[80,128]{1,0:T(8,128)S(1)}, f32[80,128]{1,0:T(8,128)S(1)}, u32[]{:S(2)}, u32[]{:S(2)}) collective-permute-start(f32[80,128]{1,0:T(8,128)S(1)} %pad_maximum_fusion.1), channel_id=1, source_target_pairs={{0,8},{8,0},{4,12},{12,4},{16,24},{24,16},{20,28},{28,20},{1,9},{9... | collective-permute-start | bytes 122888 | tf_op jit(solution)/shard_map/ppermute | solution.py:537
  12.1 4.0 %collective-permute-start.2 = (f32[80,128]{1,0:T(8,128)S(1)}, f32[80,128]{1,0:T(8,128)S(1)}, u32[]{:S(2)}, u32[]{:S(2)}) collective-permute-start(f32[80,128]{1,0:T(8,128)S(1)} %collective-permute-done.1), channel_id=1, source_target_pairs={{0,16},{16,0},{4,20},{20,4},{8,24},{24,8},{12,28},{28,12},{1,17},{... | collective-permute-start | bytes 122888 | tf_op jit(solution)/shard_map/ppermute | solution.py:539
  16.3 4.5 %collective-permute-start.3 = (f32[64,128]{1,0:T(8,128)S(1)}, f32[64,128]{1,0:T(8,128)S(1)}, u32[]{:S(2)}, u32[]{:S(2)}) collective-permute-start(f32[64,128]{1,0:T(8,128)S(1)} %get-tuple-element.54.change_a), channel_id=1, source_target_pairs={{0,1},{4,5},{8,9},{12,13},{16,17},{20,21},{24,25},{28,29},{1,0},{5... | collective-permute-start | bytes 98312 | tf_op jit(solution)/shard_map/ppermute | solution.py:546
  16.4 4.4 %collective-permute-start.4 = (f32[64,128]{1,0:T(8,128)S(1)}, f32[64,128]{1,0:T(8,128)S(1)}, u32[]{:S(2)}, u32[]{:S(2)}) collective-permute-start(f32[64,128]{1,0:T(8,128)S(1)} %get-tuple-element.55.change_b), channel_id=1, source_target_pairs={{1,2},{5,6},{9,10},{13,14},{17,18},{21,22},{25,26},{29,30},{2,1},{... | collective-permute-start | bytes 98312 | tf_op jit(solution)/shard_map/ppermute | solution.py:546
  21.4 1.2 %collective-permute-start.7 = (f32[32,128]{1,0:T(8,128)S(1)}, f32[32,128]{1,0:T(8,128)S(1)}, u32[]{:S(2)}, u32[]{:S(2)}) collective-permute-start(f32[32,128]{1,0:T(8,128)S(1)} %get-tuple-element.61), channel_id=1, source_target_pairs={{0,4},{4,0},{8,12},{12,8},{16,20},{20,16},{24,28},{28,24},{1,5},{5... | collective-permute-start | bytes 49160 | tf_op jit(solution)/shard_map/ppermute | solution.py:578
  21.9 13.5 %copy-start.1 = (f32[1,3,4,8100]{3,2,1,0:T(4,128)S(1)}, f32[1,3,4,8100]{3,2,1,0:T(4,128)}, u32[]{:S(2)}) copy-start(f32[1,3,4,8100]{3,2,1,0:T(4,128)} %state_ref.1) | copy-start | bytes 1166404
  22.6 4.0 %collective-permute-start.8 = (f32[80,128]{1,0:T(8,128)S(1)}, f32[80,128]{1,0:T(8,128)S(1)}, u32[]{:S(2)}, u32[]{:S(2)}) collective-permute-start(f32[80,128]{1,0:T(8,128)S(1)} %pad_maximum_fusion.2), channel_id=1, source_target_pairs={{0,8},{8,0},{4,12},{12,4},{16,24},{24,16},{20,28},{28,20},{1,9},{9... | collective-permute-start | bytes 122888 | tf_op jit(solution)/shard_map/ppermute | solution.py:537
  24.1 11.3 %collective-permute-start.12 = (f32[3,32,8,128]{3,2,1,0:T(8,128)S(1)}, f32[3,32,8,128]{3,2,1,0:T(8,128)S(1)}, u32[]{:S(2)}, u32[]{:S(2)}) collective-permute-start(f32[3,32,8,128]{3,2,1,0:T(8,128)S(1)} %inner_kernel.1.taken_ref), channel_id=1, source_target_pairs={{0,1},{4,5},{8,9},{12,13},{16,17},{20,21},{24,25},{28,29},{1,0},{5... | collective-permute-start | bytes 1179656 | tf_op jit(solution)/shard_map/ppermute | solution.py:546
  25.9 9.5 %collective-permute-start.13 = (f32[3,32,8,128]{3,2,1,0:T(8,128)S(1)}, f32[3,32,8,128]{3,2,1,0:T(8,128)S(1)}, u32[]{:S(2)}, u32[]{:S(2)}) collective-permute-start(f32[3,32,8,128]{3,2,1,0:T(8,128)S(1)} %inner_kernel.1.taken_ref), channel_id=1, source_target_pairs={{1,2},{5,6},{9,10},{13,14},{17,18},{21,22},{25,26},{29,30},{2,1},{... | collective-permute-start | bytes 1179656 | tf_op jit(solution)/shard_map/ppermute | solution.py:546
  26.6 4.1 %collective-permute-start.9 = (f32[80,128]{1,0:T(8,128)S(1)}, f32[80,128]{1,0:T(8,128)S(1)}, u32[]{:S(2)}, u32[]{:S(2)}) collective-permute-start(f32[80,128]{1,0:T(8,128)S(1)} %collective-permute-done.8), channel_id=1, source_target_pairs={{0,16},{16,0},{4,20},{20,4},{8,24},{24,8},{12,28},{28,12},{1,17},{... | collective-permute-start | bytes 122888 | tf_op jit(solution)/shard_map/ppermute | solution.py:539
  30.8 4.9 %collective-permute-start.10 = (f32[64,128]{1,0:T(8,128)S(1)}, f32[64,128]{1,0:T(8,128)S(1)}, u32[]{:S(2)}, u32[]{:S(2)}) collective-permute-start(f32[64,128]{1,0:T(8,128)S(1)} %get-tuple-element.63.change_a), channel_id=1, source_target_pairs={{0,1},{4,5},{8,9},{12,13},{16,17},{20,21},{24,25},{28,29},{1,0},{5... | collective-permute-start | bytes 98312 | tf_op jit(solution)/shard_map/ppermute | solution.py:546
  32.6 3.1 %collective-permute-start.11 = (f32[64,128]{1,0:T(8,128)S(1)}, f32[64,128]{1,0:T(8,128)S(1)}, u32[]{:S(2)}, u32[]{:S(2)}) collective-permute-start(f32[64,128]{1,0:T(8,128)S(1)} %get-tuple-element.64.change_b), channel_id=1, source_target_pairs={{1,2},{5,6},{9,10},{13,14},{17,18},{21,22},{25,26},{29,30},{2,1},{... | collective-permute-start | bytes 98312 | tf_op jit(solution)/shard_map/ppermute | solution.py:546

commit v6 on v4

--- a/solution.py
+++ b/solution.py
@@ -1,5 +1,3 @@
-import functools
-
 import jax
 import jax.numpy as jnp
 from jax import lax
@@ -9,7 +7,6 @@
 
 TILE = 90
 CELLS = TILE * TILE
-SUBSTEPS = 2
 BLOCK = 6
 COARSE = 15
 LANES = 128
@@ -22,10 +19,10 @@
 ROWS = SPOTS * CHANNELS
 TILE_ROWS = SIDES * CHANNELS
 SHOWN = ROWS + TILE_ROWS
-OWN = 0 + SHOWN
-ODD = 0 + SHOWN + SHOWN
-EVEN = 0
-OTHER = 0 + SHOWN + SHOWN + SHOWN
+ODD = 0
+EVEN = SHOWN
+OWN = 2 * SHOWN
+OTHER = 3 * SHOWN
 CLOSED = -8
 TURNED = 1 << 16
 FIRST_HIGH = HALF // TILE
@@ -268,7 +265,12 @@
 
 def inner_first_kernel(spread, lam_ref, wet_ref, mixing_ref, vertical_ref, rate_ref, pack_a, pack_b, stay_ref, keep_ref):
     tracers = lam_ref.shape[0]
-    even = lax.axis_index("slab") % 2 == 0
+    level, levels = lax.axis_index("slab"), lax.axis_size("slab")
+    even = level % 2 == 0
+    has_a = (level // 2 * 2 + 1 < levels).astype(F32)
+    has_b = ((level >= 1) & ((level + 1) // 2 * 2 < levels)).astype(F32)
+    for_a = has_a * jnp.where(even, 1.0, 0.0), has_a * jnp.where(even, 0.0, 1.0)
+    for_b = has_b * jnp.where(even, 0.0, 1.0), has_b * jnp.where(even, 1.0, 0.0)
     lane, low = position()
     fold(lambda a, n: vertical_ref[0, :, a : a + n], write_to(stay_ref))
     for c in range(tracers):
@@ -278,8 +280,8 @@
         x, _ = cell_at(lane, low, v)
         west, east = x == 0, x == TILE - 1
         wet, vertical = wet_ref[v], stay_ref[v]
-        pack_a[tracers, v] = wet * jnp.where(even, 1.0, vertical)
-        pack_b[tracers, v] = wet * jnp.where(even, vertical, 1.0)
+        pack_a[tracers, v] = wet * (for_a[0] + for_a[1] * vertical)
+        pack_b[tracers, v] = wet * (for_b[0] + for_b[1] * vertical)
         stay = 1.0 - mixing_ref[v] * inner_sum(spread, tracers, v, lane, west, east)
         stay_ref[v] = stay
         for c in range(tracers):
@@ -513,10 +515,14 @@
 def shards(adjoint, state, weights, vertical, mask, rate, neighbours, links, owners):
     tracers = adjoint.shape[1]
     number = lax.axis_size("tiles")
-    even_swap, odd_swap = swaps(lax.axis_size("slab"))
+    levels = lax.axis_size("slab")
+    even_swap, odd_swap = ([(k * levels + i, k * levels + j) for i, j in pairs for k in range(number)] for pairs in swaps(levels))
     core_swap = [(2 * i + a, 2 * i + 1 - a) for i in range(number // 2) for a in range(2)]
+    for pairs in (even_swap, odd_swap):
+        alone = set(range(levels)) - {i % levels for i, _ in pairs}
+        pairs.extend((a * levels + i, b * levels + i) for i in sorted(alone) for a, b in core_swap)
     even_chips, odd_chips = swaps(number, 2)
-    passing = swaps(number, 4)[0]
+    odd_chips += [pair for k in range(2) for pair in ((k, number - 2 + k), (number - 2 + k, k))]
     plane = (COLS, 8, LANES)
     planes = (tracers, *plane)
     pack = (tracers + 1, *plane)
@@ -527,14 +533,11 @@
     def around(edge, other):
         shown = jnp.concatenate([edge, other[:TILE_ROWS]])
         even = lax.ppermute(shown, "tiles", even_chips)
-        if number == 8:
-            odd = lax.ppermute(even, "tiles", passing)
-        else:
-            odd = lax.ppermute(shown, "tiles", odd_chips)
-        return jnp.concatenate([even, shown, odd, other[TILE_ROWS:]])
+        odd = lax.ppermute(shown, "tiles", odd_chips)
+        return jnp.concatenate([odd, even, shown, other[TILE_ROWS:]])
 
     def across(first, second):
-        return lax.ppermute(first, "slab", even_swap), lax.ppermute(second, "slab", odd_swap)
+        return lax.ppermute(first, ("tiles", "slab"), even_swap), lax.ppermute(second, ("tiles", "slab"), odd_swap)
 
     edge, give, lam, wet, mixing, spread, table = call(
         open_kernel,
@@ -548,12 +551,12 @@
     pack_a, pack_b, stay, keep = call(inner_first_kernel, [VMEM] * 6, [pack, pack, plane, planes], [])(
         spread, lam, wet, mixing, vertical, rate
     )
-    pack_a, pack_b, other = lax.optimization_barrier((pack_a, pack_b, other))
     from_a, from_b = across(pack_a, pack_b)
     near = around(edge, other)
     fixed_a, fixed_b, places = call(
         fixed_kernel, [SMEM] + [VMEM] * 3, [edges] * 2 + [jax.ShapeDtypeStruct(edges, I32)], []
     )(table, keep, pack_a, pack_b)
+
     halo = call(halo_kernel, [VMEM] * 5, [edges] * 2, [edges])
     change_a, change_b = halo(places, near, edge, fixed_a, fixed_b)
     got_a, got_b = across(change_a, change_b)

time: 49.4 us -> 44.4 us (0.90); the launches traced: 48.5 us -> 44.2 us
  starting transfers between devices: 17.8 us -> 15.2 us
  blocking collectives: 8.32 us -> 7.41 us
  waiting for transfers between devices: 14.6 us -> 13.9 us
    ppermute x10, waiting for transfers between devices: 12.7 us -> 9.02 us  [the longest x4 6.01 us: across(): lax.ppermute(first, ('tiles', 'slab'), even_swap)]
    ppermute x2, starting transfers between devices: 3.37 us -> 1.07 us  [around(): even = lax.ppermute(shown, 'tiles', even_chips)]
    ppermute x2, waiting for transfers between devices: 1.05 us -> 2.98 us  [around(): even = lax.ppermute(shown, 'tiles', even_chips)]
    ppermute x2, waiting for transfers between devices: 0.86 us -> 1.86 us  [shards(): other = lax.ppermute(give, 'tiles', core_swap)]
    all_to_all x1, blocking collectives: 8.32 us -> 7.41 us  [shards(): part = lax.all_to_all(part, 'tiles', 0, 0, tiled=True)]
    ppermute x2, starting transfers between devices: 0.59 us -> 0.07 us  [shards(): other = lax.ppermute(give, 'tiles', core_swap)]
  transfers between devices with their start and end apart: 14 -> 14, of which waited for: 9 -> 10; matrix products, arithmetic and copies ran while one was open for 0% -> 0% of each run, Pallas kernels for 5% -> 4%
where the time goes in v6:
time: 44.4 us; the launch traced here: 44.2 us
  starting transfers between devices  15.2 us (34%)
  waiting for transfers between devices  13.9 us (31%)
  blocking collectives  7.41 us (17%)
  Pallas kernels  6.34 us (14%)
  between operations  0.77 us (2%)
  local copies, waits for them, and re-layouts  0.6 us (1%)
    ppermute x4, starting transfers between devices, across(): lax.ppermute(first, ('tiles', 'slab'), even_swap)  8.5 us
    all_to_all x1, blocking collectives, shards(): part = lax.all_to_all(part, 'tiles', 0, 0, tiled=True)  7.41 us
    ppermute x4, waiting for transfers between devices, across(): lax.ppermute(first, ('tiles', 'slab'), even_swap)  6.01 us
    ppermute x2, starting transfers between devices, around(): odd = lax.ppermute(shown, 'tiles', odd_chips)  4.96 us
    ppermute x2, waiting for transfers between devices, around(): odd = lax.ppermute(shown, 'tiles', odd_chips)  3 us
    ppermute x2, waiting for transfers between devices, around(): even = lax.ppermute(shown, 'tiles', even_chips)  2.98 us
    ppermute x2, waiting for transfers between devices, shards(): other = lax.ppermute(give, 'tiles', core_swap)  1.86 us
    pallas_call x1, Pallas kernels, shards(): call(open_kernel, [HBM] * 5, [edges, given, planes, plane, plane, (tracer...  1.61 us
  transfers between devices with their start and end apart: 14, of which 10 were waited for; matrix products, arithmetic and copies ran while one was open for 0% of the time, Pallas kernels for 4%

profile of v6, /device:TPU:0, one launch (start us, length us, event | category | flops | bytes accessed | tf_op | source)
XLA Modules:
  0.0 44.2 jit_solution(10929097707297382379)
XLA Ops:
  0.6 0.0 copy-start.2
  0.6 0.0 copy-start
  0.7 1.6 %open_kernel.1 = (f32[64,128]{1,0:T(8,128)S(1)}, f32[32,128]{1,0:T(8,128)S(1)}, f32[3,32,8,128]{3,2,1,0:T(8,128)S(1)}, f32[32,8,128]{2,1,0:T(8,128)S(1)}, f32[32...) custom-call(f32[1,3,4,8100]{3,2,1,0:T(4,128)} %adjoint_hbm.1, f32[1,4,8100]{2,1,0:T(4,128)} %weights_hbm.1, ...), custom_call_target="tpu_custom_call" | custom-call | tf_op jit(solution)/shard_map/open_kernel/pallas_call | solution.py:542
  2.3 0.0 copy-done.2
  2.3 0.0 copy-done
  2.3 0.7 %inner_first_kernel.1 = (f32[4,32,8,128]{3,2,1,0:T(8,128)S(1)}, f32[4,32,8,128]{3,2,1,0:T(8,128)S(1)}, f32[32,8,128]{2,1,0:T(8,128)S(1)}, f32[3,32,8,128]{3,2,1,0:T(8,128)S(1)}) custom-call(f32[4,34,8,128]{3,2,1,0:T(8,128)S(1)} %get-tuple-element.34.spread, f32[3,32,8,128]{3,2,1,0:T(8,128)S(1)} %get-tuple-element.35.lam_ref, ...), custom_call_target="tpu_custom_call" | custom-call | tf_op jit(solution)/shard_map/inner_first_kernel/pallas_call | solution.py:551
  2.9 0.5 %collective-permute-start.5 = (f32[4,32,8,128]{3,2,1,0:T(8,128)S(1)}, f32[4,32,8,128]{3,2,1,0:T(8,128)S(1)}, u32[]{:S(2)}, u32[]{:S(2)}) collective-permute-start(f32[4,32,8,128]{3,2,1,0:T(8,128)S(1)} %get-tuple-element.40.pack_b), channel_id=1, source_target_pairs={{1,2},{5,6},{9,10},{13,14},{17,18},{21,22},{25,26},{29,30},{2,1},{... | collective-permute-start | bytes 1572872 | tf_op jit(solution)/shard_map/ppermute | solution.py:540
  3.5 4.1 %collective-permute-start.6 = (f32[4,32,8,128]{3,2,1,0:T(8,128)S(1)}, f32[4,32,8,128]{3,2,1,0:T(8,128)S(1)}, u32[]{:S(2)}, u32[]{:S(2)}) collective-permute-start(f32[4,32,8,128]{3,2,1,0:T(8,128)S(1)} %get-tuple-element.39.pack_a), channel_id=1, source_target_pairs={{0,1},{4,5},{8,9},{12,13},{16,17},{20,21},{24,25},{28,29},{1,0},{5... | collective-permute-start | bytes 1572872 | tf_op jit(solution)/shard_map/ppermute | solution.py:540
  7.6 0.0 collective-permute-start
  7.6 1.2 %collective-permute-done = f32[32,128]{1,0:T(8,128)S(1)} collective-permute-done((f32[32,128]{1,0:T(8,128)S(1)}, f32[32,128]{1,0:T(8,128)S(1)}, u32[]{:S(2)}, u32[]{:S(2)}) %collective-permute-start) | collective-permute-done | bytes 16416 | tf_op jit(solution)/shard_map/ppermute | solution.py:550
  8.8 2.4 %collective-permute-start.1 = (f32[80,128]{1,0:T(8,128)S(1)}, f32[80,128]{1,0:T(8,128)S(1)}, u32[]{:S(2)}, u32[]{:S(2)}) collective-permute-start(f32[80,128]{1,0:T(8,128)S(1)} %pad_maximum_fusion.2), channel_id=1, source_target_pairs={{8,16},{16,8},{12,20},{20,12},{0,24},{24,0},{4,28},{28,4},{9,17},{... | collective-permute-start | bytes 122888 | tf_op jit(solution)/shard_map/ppermute | solution.py:536
  11.2 0.5 %collective-permute-start.2 = (f32[80,128]{1,0:T(8,128)S(1)}, f32[80,128]{1,0:T(8,128)S(1)}, u32[]{:S(2)}, u32[]{:S(2)}) collective-permute-start(f32[80,128]{1,0:T(8,128)S(1)} %pad_maximum_fusion.2), channel_id=1, source_target_pairs={{0,8},{8,0},{4,12},{12,4},{16,24},{24,16},{20,28},{28,20},{1,9},{9... | collective-permute-start | bytes 122888 | tf_op jit(solution)/shard_map/ppermute | solution.py:535
  11.8 0.9 %fixed_kernel.1 = (f32[64,128]{1,0:T(8,128)S(1)}, f32[64,128]{1,0:T(8,128)S(1)}, s32[64,128]{1,0:T(8,128)S(1)}) custom-call(s32[4,4]{1,0:T(4,128)S(1)} %get-tuple-element.33.table_ref, f32[3,32,8,128]{3,2,1,0:T(8,128)S(1)} %get-tuple-element.38.keep_ref, f32[4,32,8,128]{3,2,1,0:T(8,128)S(1)} %get-tuple-element.39.pack_a, ...), custom_call_target="tpu_custom_call" | custom-call | tf_op jit(solution)/shard_map/fixed_kernel/pallas_call | solution.py:556
  12.7 1.1 %collective-permute-done.1 = f32[80,128]{1,0:T(8,128)S(1)} collective-permute-done((f32[80,128]{1,0:T(8,128)S(1)}, f32[80,128]{1,0:T(8,128)S(1)}, u32[]{:S(2)}, u32[]{:S(2)}) %collective-permute-start.1) | collective-permute-done | bytes 40992 | tf_op jit(solution)/shard_map/ppermute | solution.py:536
  13.8 1.4 %collective-permute-done.2 = f32[80,128]{1,0:T(8,128)S(1)} collective-permute-done((f32[80,128]{1,0:T(8,128)S(1)}, f32[80,128]{1,0:T(8,128)S(1)}, u32[]{:S(2)}, u32[]{:S(2)}) %collective-permute-start.2) | collective-permute-done | bytes 40992 | tf_op jit(solution)/shard_map/ppermute | solution.py:535
  15.3 0.1 halo_kernel.2
  15.4 0.1 collective-permute-start.3
  15.5 0.1 collective-permute-start.4
  15.5 0.0 collective-permute-done.5.from_b
  15.6 4.0 %collective-permute-done.6.from_a = f32[4,32,8,128]{3,2,1,0:T(8,128)S(1)} collective-permute-done((f32[4,32,8,128]{3,2,1,0:T(8,128)S(1)}, f32[4,32,8,128]{3,2,1,0:T(8,128)S(1)}, u32[]{:S(2)}, u32[]{:S(2)}) %collective-permute-start.6) | collective-permute-done | bytes 524320 | tf_op jit(solution)/shard_map/ppermute | solution.py:540
  19.6 0.1 mix_first_kernel.1
  19.7 0.3 collective-permute-done.3.got_a
  20.0 0.0 collective-permute-done.4.got_b
  20.0 0.6 %middle_kernel.1 = (f32[64,128]{1,0:T(8,128)S(1)}, f32[32,128]{1,0:T(8,128)S(1)}, f32[3,32,8,128]{3,2,1,0:T(8,128)S(1)}, f32[3,34,8,128]{3,2,1,0:T(8,128)S(1)}) custom-call(f32[64,128]{1,0:T(8,128)S(1)} %get-tuple-element.46.change_a, f32[64,128]{1,0:T(8,128)S(1)} %get-tuple-element.47.change_b, f32[64,128]{1,0:T(8,128)S(1)} %collective-permute-done.3.got_a, ...), custom_call_target="tpu_custom_call" | custom-call | tf_op jit(solution)/shard_map/middle_kernel/pallas_call | solution.py:566
  20.5 0.1 collective-permute-start.7
  20.6 0.5 %inner_kernel.1.taken_ref = f32[3,32,8,128]{3,2,1,0:T(8,128)S(1)} custom-call(f32[3,34,8,128]{3,2,1,0:T(8,128)S(1)} %get-tuple-element.50.spread, f32[3,32,8,128]{3,2,1,0:T(8,128)S(1)} %get-tuple-element.51.lam_ref, f32[32,8,128]{2,1,0:T(8,128)S(1)} %get-tuple-element.36.wet_ref, f32[32,8,128]{2,1,0:T(8,128)S(1)} %get-tuple-element.52.stay_ref, ...), custom_call_target="tpu_custom_call" | custom-call | tf_op jit(solution)/shard_map/inner_kernel/pallas_call | solution.py:570
  21.1 0.0 copy-start.1
  21.1 0.7 %collective-permute-done.7 = f32[32,128]{1,0:T(8,128)S(1)} collective-permute-done((f32[32,128]{1,0:T(8,128)S(1)}, f32[32,128]{1,0:T(8,128)S(1)}, u32[]{:S(2)}, u32[]{:S(2)}) %collective-permute-start.7) | collective-permute-done | bytes 16416 | tf_op jit(solution)/shard_map/ppermute | solution.py:569
  21.8 1.7 %collective-permute-start.12 = (f32[3,32,8,128]{3,2,1,0:T(8,128)S(1)}, f32[3,32,8,128]{3,2,1,0:T(8,128)S(1)}, u32[]{:S(2)}, u32[]{:S(2)}) collective-permute-start(f32[3,32,8,128]{3,2,1,0:T(8,128)S(1)} %inner_kernel.1.taken_ref), channel_id=1, source_target_pairs={{0,1},{4,5},{8,9},{12,13},{16,17},{20,21},{24,25},{28,29},{1,0},{5... | collective-permute-start | bytes 1179656 | tf_op jit(solution)/shard_map/ppermute | solution.py:540
  23.5 0.0 collective-permute-start.13
  23.5 2.5 %collective-permute-start.8 = (f32[80,128]{1,0:T(8,128)S(1)}, f32[80,128]{1,0:T(8,128)S(1)}, u32[]{:S(2)}, u32[]{:S(2)}) collective-permute-start(f32[80,128]{1,0:T(8,128)S(1)} %pad_maximum_fusion.3), channel_id=1, source_target_pairs={{8,16},{16,8},{12,20},{20,12},{0,24},{24,0},{4,28},{28,4},{9,17},{... | collective-permute-start | bytes 122888 | tf_op jit(solution)/shard_map/ppermute | solution.py:536
  26.0 0.5 %collective-permute-start.9 = (f32[80,128]{1,0:T(8,128)S(1)}, f32[80,128]{1,0:T(8,128)S(1)}, u32[]{:S(2)}, u32[]{:S(2)}) collective-permute-start(f32[80,128]{1,0:T(8,128)S(1)} %pad_maximum_fusion.3), channel_id=1, source_target_pairs={{0,8},{8,0},{4,12},{12,4},{16,24},{24,16},{20,28},{28,20},{1,9},{9... | collective-permute-start | bytes 122888 | tf_op jit(solution)/shard_map/ppermute | solution.py:535
  26.6 1.9 %collective-permute-done.8 = f32[80,128]{1,0:T(8,128)S(1)} collective-permute-done((f32[80,128]{1,0:T(8,128)S(1)}, f32[80,128]{1,0:T(8,128)S(1)}, u32[]{:S(2)}, u32[]{:S(2)}) %collective-permute-start.8) | collective-permute-done | bytes 40992 | tf_op jit(solution)/shard_map/ppermute | solution.py:536
  28.5 1.5 %collective-permute-done.9 = f32[80,128]{1,0:T(8,128)S(1)} collective-permute-done((f32[80,128]{1,0:T(8,128)S(1)}, f32[80,128]{1,0:T(8,128)S(1)}, u32[]{:S(2)}, u32[]{:S(2)}) %collective-permute-start.9) | collective-permute-done | bytes 40992 | tf_op jit(solution)/shard_map/ppermute | solution.py:535
  30.1 0.1 halo_kernel.3
  30.2 2.5 %collective-permute-start.10 = (f32[64,128]{1,0:T(8,128)S(1)}, f32[64,128]{1,0:T(8,128)S(1)}, u32[]{:S(2)}, u32[]{:S(2)}) collective-permute-start(f32[64,128]{1,0:T(8,128)S(1)} %get-tuple-element.55.change_a), channel_id=1, source_target_pairs={{0,1},{4,5},{8,9},{12,13},{16,17},{20,21},{24,25},{28,29},{1,0},{5... | collective-permute-start | bytes 98312 | tf_op jit(solution)/shard_map/ppermute | solution.py:540
  32.7 0.0 collective-permute-start.11
  32.7 0.6 %collective-permute-done.12.from_a = f32[3,32,8,128]{3,2,1,0:T(8,128)S(1)} collective-permute-done((f32[3,32,8,128]{3,2,1,0:T(8,128)S(1)}, f32[3,32,8,128]{3,2,1,0:T(8,128)S(1)}, u32[]{:S(2)}, u32[]{:S(2)}) %collective-permute-start.12) | collective-permute-done | bytes 393248 | tf_op jit(solution)/shard_map/ppermute | solution.py:540
  33.3 0.0 collective-permute-done.13.from_b
  33.3 0.0 copy-done.1
  33.3 0.2 mix_kernel.1
  33.5 1.1 %collective-permute-done.10.got_a = f32[64,128]{1,0:T(8,128)S(1)} collective-permute-done((f32[64,128]{1,0:T(8,128)S(1)}, f32[64,128]{1,0:T(8,128)S(1)}, u32[]{:S(2)}, u32[]{:S(2)}) %collective-permute-start.10) | collective-permute-done | bytes 32800 | tf_op jit(solution)/shard_map/ppermute | solution.py:540
  34.6 0.0 collective-permute-done.11.got_b
  34.6 1.6 %close_kernel.1 = (f32[1,3,4,8100]{3,2,1,0:T(4,128)}, f32[8,8,128]{2,1,0:T(8,128)S(1)}) custom-call(s32[32]{0:T(128)} %owner_hbm.1, f32[64,128]{1,0:T(8,128)S(1)} %get-tuple-element.55.change_a, f32[64,128]{1,0:T(8,128)S(1)} %get-tuple-element.56.change_b, f32[64,128]{1,0:T(8,128)S(1)} %collective-permute-done.10.got_a, ...), custom_call_target="tpu_custom_call" | custom-call | tf_op jit(solution)/shard_map/close_kernel/pallas_call | solution.py:580
  36.2 7.4 %all_to_all.5 = f32[8,8,128]{2,1,0:T(8,128)S(1)} all-to-all(f32[8,8,128]{2,1,0:T(8,128)S(1)} %get-tuple-element.63), channel_id=1, replica_groups=mesh['tiles'=8,'slab'=4] {'tiles'}, dimensions={0} | all-to-all | bytes 65536 | tf_op jit(solution)/shard_map/all_to_all | solution.py:588
  43.6 0.6 %slice.17 = f32[1,1,675]{2,1,0:T(1,128)} slice(f32[1,1,1024]{2,1,0:T(1,128)S(1)} %bitcast.1), slice={[0:1], [0:1], [0:675]} | slice | bytes 5400 | tf_op jit(solution)/shard_map/slice | solution.py:589
  (7 shorter events, 0.0 us)
Async XLA Ops:
  0.6 1.6 %copy-start.2 = (f32[1,4,8100]{2,1,0:T(4,128)S(1)}, f32[1,4,8100]{2,1,0:T(4,128)}, u32[]{:S(2)}) copy-start(f32[1,4,8100]{2,1,0:T(4,128)} %vertical_ref.1) | copy-start | bytes 388804
  0.6 1.6 %copy-start = (f32[3,4,8100]{2,1,0:T(4,128)S(1)}, f32[3,4,8100]{2,1,0:T(4,128)}, u32[]{:S(2)}) copy-start(f32[3,4,8100]{2,1,0:T(4,128)} %rate_ref.1) | copy-start | bytes 1166404
  2.9 12.6 %collective-permute-start.5 = (f32[4,32,8,128]{3,2,1,0:T(8,128)S(1)}, f32[4,32,8,128]{3,2,1,0:T(8,128)S(1)}, u32[]{:S(2)}, u32[]{:S(2)}) collective-permute-start(f32[4,32,8,128]{3,2,1,0:T(8,128)S(1)} %get-tuple-element.40.pack_b), channel_id=1, source_target_pairs={{1,2},{5,6},{9,10},{13,14},{17,18},{21,22},{25,26},{29,30},{2,1},{... | collective-permute-start | bytes 1572872 | tf_op jit(solution)/shard_map/ppermute | solution.py:540
  3.5 16.1 %collective-permute-start.6 = (f32[4,32,8,128]{3,2,1,0:T(8,128)S(1)}, f32[4,32,8,128]{3,2,1,0:T(8,128)S(1)}, u32[]{:S(2)}, u32[]{:S(2)}) collective-permute-start(f32[4,32,8,128]{3,2,1,0:T(8,128)S(1)} %get-tuple-element.39.pack_a), channel_id=1, source_target_pairs={{0,1},{4,5},{8,9},{12,13},{16,17},{20,21},{24,25},{28,29},{1,0},{5... | collective-permute-start | bytes 1572872 | tf_op jit(solution)/shard_map/ppermute | solution.py:540
  7.6 1.2 %collective-permute-start = (f32[32,128]{1,0:T(8,128)S(1)}, f32[32,128]{1,0:T(8,128)S(1)}, u32[]{:S(2)}, u32[]{:S(2)}) collective-permute-start(f32[32,128]{1,0:T(8,128)S(1)} %get-tuple-element.43), channel_id=1, source_target_pairs={{0,4},{4,0},{8,12},{12,8},{16,20},{20,16},{24,28},{28,24},{1,5},{5... | collective-permute-start | bytes 49160 | tf_op jit(solution)/shard_map/ppermute | solution.py:550
  8.8 5.0 %collective-permute-start.1 = (f32[80,128]{1,0:T(8,128)S(1)}, f32[80,128]{1,0:T(8,128)S(1)}, u32[]{:S(2)}, u32[]{:S(2)}) collective-permute-start(f32[80,128]{1,0:T(8,128)S(1)} %pad_maximum_fusion.2), channel_id=1, source_target_pairs={{8,16},{16,8},{12,20},{20,12},{0,24},{24,0},{4,28},{28,4},{9,17},{... | collective-permute-start | bytes 122888 | tf_op jit(solution)/shard_map/ppermute | solution.py:536
  11.2 4.0 %collective-permute-start.2 = (f32[80,128]{1,0:T(8,128)S(1)}, f32[80,128]{1,0:T(8,128)S(1)}, u32[]{:S(2)}, u32[]{:S(2)}) collective-permute-start(f32[80,128]{1,0:T(8,128)S(1)} %pad_maximum_fusion.2), channel_id=1, source_target_pairs={{0,8},{8,0},{4,12},{12,4},{16,24},{24,16},{20,28},{28,20},{1,9},{9... | collective-permute-start | bytes 122888 | tf_op jit(solution)/shard_map/ppermute | solution.py:535
  15.4 4.6 %collective-permute-start.3 = (f32[64,128]{1,0:T(8,128)S(1)}, f32[64,128]{1,0:T(8,128)S(1)}, u32[]{:S(2)}, u32[]{:S(2)}) collective-permute-start(f32[64,128]{1,0:T(8,128)S(1)} %get-tuple-element.46.change_a), channel_id=1, source_target_pairs={{0,1},{4,5},{8,9},{12,13},{16,17},{20,21},{24,25},{28,29},{1,0},{5... | collective-permute-start | bytes 98312 | tf_op jit(solution)/shard_map/ppermute | solution.py:540
  15.5 4.5 %collective-permute-start.4 = (f32[64,128]{1,0:T(8,128)S(1)}, f32[64,128]{1,0:T(8,128)S(1)}, u32[]{:S(2)}, u32[]{:S(2)}) collective-permute-start(f32[64,128]{1,0:T(8,128)S(1)} %get-tuple-element.47.change_b), channel_id=1, source_target_pairs={{1,2},{5,6},{9,10},{13,14},{17,18},{21,22},{25,26},{29,30},{2,1},{... | collective-permute-start | bytes 98312 | tf_op jit(solution)/shard_map/ppermute | solution.py:540
  20.5 1.2 %collective-permute-start.7 = (f32[32,128]{1,0:T(8,128)S(1)}, f32[32,128]{1,0:T(8,128)S(1)}, u32[]{:S(2)}, u32[]{:S(2)}) collective-permute-start(f32[32,128]{1,0:T(8,128)S(1)} %get-tuple-element.53), channel_id=1, source_target_pairs={{0,4},{4,0},{8,12},{12,8},{16,20},{20,16},{24,28},{28,24},{1,5},{5... | collective-permute-start | bytes 49160 | tf_op jit(solution)/shard_map/ppermute | solution.py:569
  21.1 12.2 %copy-start.1 = (f32[1,3,4,8100]{3,2,1,0:T(4,128)S(1)}, f32[1,3,4,8100]{3,2,1,0:T(4,128)}, u32[]{:S(2)}) copy-start(f32[1,3,4,8100]{3,2,1,0:T(4,128)} %state_ref.1) | copy-start | bytes 1166404
  21.8 11.5 %collective-permute-start.12 = (f32[3,32,8,128]{3,2,1,0:T(8,128)S(1)}, f32[3,32,8,128]{3,2,1,0:T(8,128)S(1)}, u32[]{:S(2)}, u32[]{:S(2)}) collective-permute-start(f32[3,32,8,128]{3,2,1,0:T(8,128)S(1)} %inner_kernel.1.taken_ref), channel_id=1, source_target_pairs={{0,1},{4,5},{8,9},{12,13},{16,17},{20,21},{24,25},{28,29},{1,0},{5... | collective-permute-start | bytes 1179656 | tf_op jit(solution)/shard_map/ppermute | solution.py:540
  23.5 9.8 %collective-permute-start.13 = (f32[3,32,8,128]{3,2,1,0:T(8,128)S(1)}, f32[3,32,8,128]{3,2,1,0:T(8,128)S(1)}, u32[]{:S(2)}, u32[]{:S(2)}) collective-permute-start(f32[3,32,8,128]{3,2,1,0:T(8,128)S(1)} %inner_kernel.1.taken_ref), channel_id=1, source_target_pairs={{1,2},{5,6},{9,10},{13,14},{17,18},{21,22},{25,26},{29,30},{2,1},{... | collective-permute-start | bytes 1179656 | tf_op jit(solution)/shard_map/ppermute | solution.py:540
  23.5 5.0 %collective-permute-start.8 = (f32[80,128]{1,0:T(8,128)S(1)}, f32[80,128]{1,0:T(8,128)S(1)}, u32[]{:S(2)}, u32[]{:S(2)}) collective-permute-start(f32[80,128]{1,0:T(8,128)S(1)} %pad_maximum_fusion.3), channel_id=1, source_target_pairs={{8,16},{16,8},{12,20},{20,12},{0,24},{24,0},{4,28},{28,4},{9,17},{... | collective-permute-start | bytes 122888 | tf_op jit(solution)/shard_map/ppermute | solution.py:536
  26.0 4.0 %collective-permute-start.9 = (f32[80,128]{1,0:T(8,128)S(1)}, f32[80,128]{1,0:T(8,128)S(1)}, u32[]{:S(2)}, u32[]{:S(2)}) collective-permute-start(f32[80,128]{1,0:T(8,128)S(1)} %pad_maximum_fusion.3), channel_id=1, source_target_pairs={{0,8},{8,0},{4,12},{12,4},{16,24},{24,16},{20,28},{28,20},{1,9},{9... | collective-permute-start | bytes 122888 | tf_op jit(solution)/shard_map/ppermute | solution.py:535
  30.2 4.4 %collective-permute-start.10 = (f32[64,128]{1,0:T(8,128)S(1)}, f32[64,128]{1,0:T(8,128)S(1)}, u32[]{:S(2)}, u32[]{:S(2)}) collective-permute-start(f32[64,128]{1,0:T(8,128)S(1)} %get-tuple-element.55.change_a), channel_id=1, source_target_pairs={{0,1},{4,5},{8,9},{12,13},{16,17},{20,21},{24,25},{28,29},{1,0},{5... | collective-permute-start | bytes 98312 | tf_op jit(solution)/shard_map/ppermute | solution.py:540
  32.7 1.9 %collective-permute-start.11 = (f32[64,128]{1,0:T(8,128)S(1)}, f32[64,128]{1,0:T(8,128)S(1)}, u32[]{:S(2)}, u32[]{:S(2)}) collective-permute-start(f32[64,128]{1,0:T(8,128)S(1)} %get-tuple-element.56.change_b), channel_id=1, source_target_pairs={{1,2},{5,6},{9,10},{13,14},{17,18},{21,22},{25,26},{29,30},{2,1},{... | collective-permute-start | bytes 98312 | tf_op jit(solution)/shard_map/ppermute | solution.py:540
